TPU v7x, 32 devices: a whole 2x2x4 slice. The times are simulated.
32 devices in a mesh: dp: 8 (over z, x), mp: 4 (over y, core).
Axes of the slice: x: 2, y: 2, z: 4, core: 2. Of those that a mesh axis runs over, the one named last changes fastest.
Arguments:
- activations: bfloat16 [8192, 8192], P('dp', 'mp'), may hold values from -6 to 6
- out_grads: bfloat16 [8192, 14336], P('dp', 'mp'), may hold values from -0.29882812 to 0.29882812
- basis: bfloat16 [8192, 512], P('dp'), may hold values from -0.25 to 0.25
- first_moment: float32 [512, 14336], P('dp', 'mp'), may hold values from -3 to 3
- second_moment: float32 [512, 14336], P('dp', 'mp'), may hold values from 0.01 to 1
Outputs:
- update: bfloat16 [8192, 14336], P('dp', 'mp')
- moment_one: float32 [512, 14336], P('dp', 'mp')
- moment_two: float32 [512, 14336], P('dp', 'mp')
All inputs are finite; a program needn't handle non-finite values.
Results may differ from a plain program's by a relative error of at most 0.0063.
Values may be sent and summed in bfloat16 or wider, within the bound.
No kernel may reach another device: no remote copies, remote signals or barrier semaphores. Data moves between devices by JAX's collectives and lax.ppermute only.
A program may use at most 128 MiB of HBM per device.

v0:
```python
import jax
import jax.numpy as jnp
from jax import lax
from jax.sharding import PartitionSpec as P

STEP = 10


BETA_ONE = 0.9
BETA_TWO = 0.999
ADAM_EPS = 1e-08


def local(activations, out_grads, basis, first_moment, second_moment):
    feature_rows = activations.shape[1]
    whole_basis = lax.all_gather(basis, "dp", axis=0, tiled=True)
    own_rows = lax.dynamic_slice_in_dim(
        whole_basis, lax.axis_index("mp") * feature_rows, feature_rows, 0
    )
    partial_value = jnp.dot(activations, own_rows, preferred_element_type=jnp.float32)
    projected = lax.psum(partial_value, "mp").astype(jnp.bfloat16)
    gradient = lax.psum_scatter(
        lax.dot_general(
            projected, out_grads, (((0,), (0,)), ((), ())), preferred_element_type=jnp.float32
        ),
        "dp",
        scatter_dimension=0,
        tiled=True,
    )
    moment_one = BETA_ONE * first_moment + (1.0 - BETA_ONE) * gradient
    moment_two = BETA_TWO * second_moment + (1.0 - BETA_TWO) * gradient * gradient
    unbiased_one = moment_one / (1.0 - BETA_ONE**STEP)
    unbiased_two = moment_two / (1.0 - BETA_TWO**STEP)
    direction = (unbiased_one / (jnp.sqrt(unbiased_two) + ADAM_EPS)).astype(jnp.bfloat16)
    whole_direction = lax.all_gather(direction, "dp", axis=0, tiled=True)
    update = jnp.dot(basis, whole_direction, preferred_element_type=jnp.float32).astype(
        jnp.bfloat16
    )
    return (update, moment_one, moment_two)


def solution(mesh):
    return jax.shard_map(
        local,
        mesh=mesh,
        in_specs=(P("dp", "mp"), P("dp", "mp"), P("dp", None), P("dp", "mp"), P("dp", "mp")),
        out_specs=(P("dp", "mp"), P("dp", "mp"), P("dp", "mp")),
        check_vma=False,
    )
```

profile of v0, /device:TPU:0, one launch (start us, length us, event | category | flops | bytes accessed | tf_op | source)
XLA Modules:
  0.0 417.4 jit_solution(5070847099676152691)
XLA Ops:
  7.2 0.0 all-gather.3.cloned.1.call-start
  7.2 0.7 all-gather.3.cloned.1.call-update
  7.9 0.0 reduce-scatter.2.cloned.1.call-start
  7.9 129.8 %all-gather.3.cloned.1.call-done = bf16[8192,512]{1,0:T(8,128)(2,1)} async-done(((bf16[1024,512]{1,0:T(8,128)(2,1)}), bf16[8192,512]{1,0:T(8,128)(2,1)}) %all-gather.3.cloned.1.call-update) | async-done | bytes 8388624 | tf_op jit(solution)/shard_map/all_gather | solution.py:16
  137.8 5.2 %fusion.3 = f32[1024,512]{0,1:T(8,128)S(1)} fusion(bf16[1024,2048]{1,0:T(8,128)(2,1)} %param.5, bf16[8192,512]{1,0:T(8,128)(2,1)} %all-gather.3.cloned.1.call-done, s32[]{:T(128)S(6)} %select_n.3), kind=kOutput, calls=%fused_computation.4 | convolution fusion | flops 2147483648 | bytes 8388612 | tf_op jit(solution)/shard_map/dot_general | solution.py:20
  143.0 40.6 %all-reduce.1 = bf16[1024,512]{0,1:T(8,128)(2,1)S(1)} all-reduce(f32[1024,512]{0,1:T(8,128)S(1)} %fusion.3), channel_id=1, replica_groups=mesh['dp'=8,'mp'=4] {'mp'}, use_global_device_ids=true, to_apply=%region_0.0 | all-reduce | flops 524288 | bytes 3145728 | tf_op jit(solution)/shard_map/psum | solution.py:21
  183.6 9.1 %fusion.11 = f32[512,3584]{1,0:T(8,128)} fusion(bf16[1024,512]{0,1:T(8,128)(2,1)S(1)} %all-reduce.1, bf16[1024,3584]{1,0:T(8,128)(2,1)} %param.6), kind=kOutput, calls=%fused_computation.12 | convolution fusion | flops 3758096384 | bytes 15728640 | tf_op jit(solution)/shard_map/dot_general | solution.py:23
  192.7 0.0 copy-start.1
  192.7 0.0 copy-start.2
  192.7 0.0 copy-start
  192.7 0.0 reduce-scatter.2.cloned.1.call-update
  192.7 0.0 all-gather.5.cloned.1.call-start
  192.8 131.0 %reduce-scatter.2.cloned.1.call-done = f32[64,3584]{1,0:T(8,128)} async-done(((f32[512,3584]{1,0:T(8,128)}), f32[64,3584]{1,0:T(8,128)}) %reduce-scatter.2.cloned.1.call-update) | async-done | bytes 917520 | tf_op jit(solution)/shard_map/reduce_scatter | solution.py:22
  323.8 0.0 copy-done.1
  323.8 0.0 copy-done.2
  323.8 2.9 divide_convert_fusion
  326.7 0.0 all-gather.5.cloned.1.call-update
  326.7 66.0 %all-gather.5.cloned.1.call-done = bf16[512,3584]{1,0:T(8,128)(2,1)} async-done(((bf16[64,3584]{1,0:T(8,128)(2,1)}), bf16[512,3584]{1,0:T(8,128)(2,1)}) %all-gather.5.cloned.1.call-update) | async-done | bytes 3670032 | tf_op jit(solution)/shard_map/all_gather | solution.py:35
  392.7 0.0 copy-done
  392.7 8.2 %fusion = bf16[1024,3584]{0,1:T(8,128)(2,1)} fusion(bf16[512,3584]{1,0:T(8,128)(2,1)} %all-gather.5.cloned.1.call-done, bf16[1024,512]{1,0:T(8,128)(2,1)S(1)} %copy-done), kind=kOutput, calls=%fused_computation.1 | convolution fusion | flops 3761766400 | bytes 12058624 | tf_op jit(solution)/shard_map/dot_general | solution.py:36
  401.0 9.9 %copy.8 = bf16[1024,3584]{1,0:T(8,128)(2,1)} copy(bf16[1024,3584]{0,1:T(8,128)(2,1)} %fusion) | data formatting | bytes 14680064
Async XLA Ops:
  7.2 130.6 %all-gather.3.cloned.1.call-start = ((), (), s32[]{:S(2)}) async-start(), calls=%async_computation.1 | async-start | bytes 9437184 | tf_op jit(solution)/shard_map/all_gather | solution.py:16
  7.9 315.9 %reduce-scatter.2.cloned.1.call-start = ((), (), s32[]{:S(2)}) async-start(), calls=%async_computation.2 | async-start | bytes 8257536 | tf_op jit(solution)/shard_map/reduce_scatter | solution.py:22
  192.7 131.1 %copy-start.1 = (f32[64,3584]{1,0:T(8,128)S(1)}, f32[64,3584]{1,0:T(8,128)}, u32[]{:S(2)}) copy-start(f32[64,3584]{1,0:T(8,128)} %param.8) | copy-start | bytes 2752516
  192.7 131.1 %copy-start.2 = (f32[64,3584]{1,0:T(8,128)S(1)}, f32[64,3584]{1,0:T(8,128)}, u32[]{:S(2)}) copy-start(f32[64,3584]{1,0:T(8,128)} %param.9) | copy-start | bytes 2752516
  192.7 200.1 %copy-start = (bf16[1024,512]{1,0:T(8,128)(2,1)S(1)}, bf16[1024,512]{1,0:T(8,128)(2,1)}, u32[]{:S(2)}) copy-start(bf16[1024,512]{1,0:T(8,128)(2,1)} %param.7) | copy-start | bytes 3145732
  192.7 200.0 %all-gather.5.cloned.1.call-start = ((), (), s32[]{:S(2)}) async-start(), calls=%async_computation.3 | async-start | bytes 4128768 | tf_op jit(solution)/shard_map/all_gather | solution.py:35
Sparse Core Ops, SparseCore 0:
  10.1 127.6 all-gather.2
  192.8 130.9 reduce-scatter.1
  326.8 65.8 all-gather.4
where the time goes:
time: 418 us; the launch traced here: 417 us
  waiting for transfers between devices  328 us (78%)
  blocking collectives  40.6 us (10%)
  matrix products  22.5 us (5%)
  between operations  13.8 us (3%)
  local copies, waits for them, and re-layouts  9.94 us (2%)
    reduce_scatter x1, waiting for transfers between devices, local(): lax.psum_scatter(lax.dot_general(projected, out_grads, (((0,), (0,)), (()...  131 us
    all_gather x1, waiting for transfers between devices, local(): whole_basis = lax.all_gather(basis, 'dp', axis=0, tiled=True)  130 us
    all_gather x1, waiting for transfers between devices, local(): whole_direction = lax.all_gather(direction, 'dp', axis=0, tiled=True)  66 us
    psum x1, blocking collectives, local(): projected = lax.psum(partial_value, 'mp').astype(jnp.bfloat16)  40.6 us
    unnamed x7, local copies, waits for them, and re-layouts  9.94 us
    dot_general x1, matrix products, local(): lax.dot_general(projected, out_grads, (((0,), (0,)), ((), ())), preferred...  9.08 us
  transfers between devices with their start and end apart: 3, of which 3 were waited for; matrix products, arithmetic and copies ran while one was open for 0% of the time, Pallas kernels for 0%

commit v1 on v0

v1 whole, which is shorter than its diff:
```python
import functools

import jax
import jax.numpy as jnp
from jax import lax
from jax.experimental import pallas as pl
from jax.experimental.pallas import tpu as pltpu
from jax.sharding import PartitionSpec as P

STEP = 10

BETA_ONE = 0.9
BETA_TWO = 0.999
ADAM_EPS = 1e-08

BF16 = jnp.bfloat16
F32 = jnp.float32
VMEM_LIMIT = 48 * 1024 * 1024
AXES = ("dp", "mp")


def tile_of(columns):
    for tile in (512, 256, 128):
        if columns % tile == 0:
            return tile
    return columns


def slot(line, r, n):
    rest = jnp.where(2 * line < n, 2 * line + r - n + 1, r)
    return jnp.where(line >= r, line - r, jnp.where(line + r < n, line + r, rest))


class Ring:
    def __init__(self, dp, mp):
        self.dp, self.mp, self.n = dp, mp, dp // 2

    def pairs(self, move):
        out = []
        for line in range(self.n):
            for pair in range(2):
                to = move(line, pair)
                if to is not None:
                    for m in range(self.mp):
                        out.append(((line * 2 + pair) * self.mp + m, (to[0] * 2 + to[1]) * self.mp + m))
        return out

    def swap(self, value):
        return lax.ppermute(value, AXES, self.pairs(lambda z, x: (z, 1 - x)))

    def up(self, value, valid):
        return lax.ppermute(value, AXES, self.pairs(lambda z, x: (z + 1, x) if z + 1 < self.n and valid(z) else None))

    def down(self, value, valid):
        return lax.ppermute(value, AXES, self.pairs(lambda z, x: (z - 1, x) if z > 0 and valid(z) else None))

    def gather(self, own):
        n = self.n
        line = lax.axis_index("dp") // 2
        ups, downs, others = [own], [own], [self.swap(own)]
        for r in range(1, n):
            ups.append(self.up(ups[-1], lambda z: z >= r - 1))
            downs.append(self.down(downs[-1], lambda z: z + r - 1 < n))
            value = jnp.where(line >= r, ups[r], downs[r])
            for k in range(1, r):
                users = [z for z in range(n) if z < r and z + r >= n and (2 * z + r - n + 1 if 2 * z < n else r) - z == k]
                for z in users:
                    value = jnp.where(line == z, downs[k], value)
            others.append(self.swap(value))
        return [own] + ups[1:] + downs[1:] + others

    def assemble(self, index_ref, blocks, out_ref):
        n = self.n
        rows = out_ref.shape[0] // self.dp
        line, pair = index_ref[0], index_ref[1]

        def put(ref, place, side):
            start = pl.multiple_of((place * 2 + side) * rows, rows)
            out_ref[pl.ds(start, rows), :] = ref[...]

        put(blocks[0], line, pair)
        for r in range(1, n):

            @pl.when(line >= r)
            def _(r=r):
                put(blocks[r], line - r, pair)

            @pl.when(line + r < n)
            def _(r=r):
                put(blocks[n - 1 + r], line + r, pair)

        for r in range(n):
            put(blocks[2 * n - 1 + r], slot(line, r, n), 1 - pair)

    def scatter_sum(self, send, keep):
        n = self.n
        line = lax.axis_index("dp") // 2
        got = [None] * n
        for r in reversed(range(n)):
            got[r] = self.swap(send[r])
        term = [keep[r].astype(F32) + got[r].astype(F32) for r in range(n)]
        from_above = from_below = None
        for k in reversed(range(1, n)):
            down = term[k]
            source = {}
            for z in range(n - k):
                r = k if z < k else (n - 1 - z + k if 2 * z < n else z + k)
                source.setdefault(r, []).append(z)
            up = None
            for r, places in source.items():
                if up is None:
                    up = term[r]
                else:
                    here = functools.reduce(jnp.logical_or, [line == z for z in places])
                    up = jnp.where(here, term[r], up)
            if from_above is not None:
                down = down + from_above.astype(F32)
                up = up + from_below.astype(F32)
            from_above = self.down(down.astype(BF16), lambda z: z >= k)
            from_below = self.up(up.astype(BF16), lambda z: z + k < n)
        return term[0] + from_above.astype(F32) + from_below.astype(F32)


def scatter_basis(basis, features, dp, mp):
    rows = basis.shape[0]
    piece = features // dp
    pairs = []
    for d in range(dp):
        for m in range(mp):
            start = m * features + d * piece
            pairs.append(((start // rows) * mp + (start % rows) // piece, d * mp + m))
    own = lax.dynamic_slice_in_dim(basis, lax.axis_index("mp") * piece, piece, 0)
    return lax.ppermute(own, AXES, pairs)


def project(ring, index, blocks, activations):
    tokens, features = activations.shape
    ranks = blocks[0].shape[1]
    mp = ring.mp
    half, step = mp // 2, tokens // mp

    def block_of(i, index):
        core, other = index[2], index[3]
        return jnp.where(i < half, 1 - core, core) * half + lax.rem(other + 1 + lax.rem(i, half), half)

    def kernel(index_ref, *refs):
        pieces, (act_ref, send_ref, keep_ref, held) = refs[: len(blocks)], refs[len(blocks) :]
        i = pl.program_id(0)

        @pl.when(i == 0)
        def _():
            ring.assemble(index_ref, pieces, held)

        value = jnp.dot(act_ref[...], held[...], preferred_element_type=F32)

        @pl.when(i < half)
        def _():
            send_ref[...] = value

        @pl.when(i >= half)
        def _():
            keep_ref[...] = value

    shape = jax.ShapeDtypeStruct((tokens // 2, ranks), F32)
    return pl.pallas_call(
        kernel,
        grid_spec=pltpu.PrefetchScalarGridSpec(
            num_scalar_prefetch=1,
            grid=(mp,),
            in_specs=[pl.BlockSpec(b.shape, lambda i, index: (0, 0)) for b in blocks]
            + [pl.BlockSpec((step, features), lambda i, index: (block_of(i, index), 0))],
            out_specs=[
                pl.BlockSpec((step, ranks), lambda i, index: (jnp.minimum(i, half - 1), 0)),
                pl.BlockSpec((step, ranks), lambda i, index: (jnp.maximum(i - half, 0), 0)),
            ],
            scratch_shapes=[pltpu.VMEM((features, ranks), BF16)],
        ),
        out_shape=[shape, shape],
        compiler_params=pltpu.CompilerParams(vmem_limit_bytes=VMEM_LIMIT),
        cost_estimate=pl.CostEstimate(
            flops=2 * tokens * features * ranks, bytes_accessed=2 * tokens * features, transcendentals=0
        ),
    )(index, *blocks, activations)


def sum_columns(ring, send, keep):
    mp, half = ring.mp, ring.mp // 2
    step = keep.shape[0] // half

    def move(value, core_step, other_step):
        pairs = []
        for d in range(ring.dp):
            for m in range(mp):
                other, core = divmod(m, 2)
                to = ((other + other_step) % half) * 2 + (core + core_step) % 2
                pairs.append((d * mp + m, d * mp + to))
        return lax.ppermute(value, AXES, pairs)

    from_core = move(send, 1, 0)
    total = None
    own = keep[(half - 1) * step :] + from_core[(half - 1) * step :]
    for j in range(half - 1):
        rows = slice(j * step, (j + 1) * step)
        own = own + move(keep[rows] + from_core[rows], 0, j + 1)
    own = own.astype(BF16)
    same = [own] + [move(own, 0, j) for j in range(1, half)]
    crossed = [move(value, 1, 0) for value in same]
    return same + crossed


def grad_rows(ring, index, pieces, out_grads, swapped):
    tokens, columns = out_grads.shape
    ranks = pieces[0].shape[1]
    mp, n = ring.mp, ring.n
    half, step = mp // 2, tokens // mp
    rows = ranks // ring.dp
    tile = tile_of(columns)

    def kernel(index_ref, *refs):
        pieces, (grads_ref, *outs), (held, turned, picked) = refs[:mp], refs[mp:-3], refs[-3:]
        line, pair, core, other = (index_ref[j] for j in range(4))

        @pl.when(pl.program_id(0) == 0)
        def _():
            for side in range(2):
                for j in range(half):
                    place = (core if side == 0 else 1 - core) * half + lax.rem(other - j + half, half)
                    held[pl.ds(pl.multiple_of(place * step, step), step), :] = pieces[side * half + j][...]
            turned[...] = held[...].T
            for r in range(n):
                start = (slot(line, r, n) * 2 + (1 - pair if swapped else pair)) * rows
                picked[r * rows : (r + 1) * rows, :] = turned[pl.ds(pl.multiple_of(start, rows), rows), :]

        value = jnp.dot(picked[...], grads_ref[...], preferred_element_type=F32).astype(BF16)
        for r in range(n):
            outs[r][...] = value[r * rows : (r + 1) * rows, :]

    return pl.pallas_call(
        kernel,
        grid_spec=pltpu.PrefetchScalarGridSpec(
            num_scalar_prefetch=1,
            grid=(columns // tile,),
            in_specs=[pl.BlockSpec((step, ranks), lambda i, index: (0, 0))] * mp
            + [pl.BlockSpec((tokens, tile), lambda i, index: (0, i))],
            out_specs=[pl.BlockSpec((rows, tile), lambda i, index: (0, i))] * n,
            scratch_shapes=[
                pltpu.VMEM((tokens, ranks), BF16),
                pltpu.VMEM((ranks, tokens), BF16),
                pltpu.VMEM((n * rows, tokens), BF16),
            ],
        ),
        out_shape=[jax.ShapeDtypeStruct((rows, columns), BF16)] * n,
        compiler_params=pltpu.CompilerParams(vmem_limit_bytes=VMEM_LIMIT),
        cost_estimate=pl.CostEstimate(
            flops=tokens * columns * ranks, bytes_accessed=2 * tokens * columns, transcendentals=0
        ),
    )(index, *pieces, out_grads)


def make_update(ring, index, blocks, basis):
    rows, ranks = basis.shape
    columns = blocks[0].shape[1]
    tile = tile_of(columns)

    def kernel(index_ref, *refs):
        pieces, (basis_ref, out_ref, held) = refs[: len(blocks)], refs[len(blocks) :]
        ring.assemble(index_ref, pieces, held)
        out_ref[...] = jnp.dot(basis_ref[...], held[...], preferred_element_type=F32).astype(BF16)

    return pl.pallas_call(
        kernel,
        grid_spec=pltpu.PrefetchScalarGridSpec(
            num_scalar_prefetch=1,
            grid=(columns // tile,),
            in_specs=[pl.BlockSpec((b.shape[0], tile), lambda i, index: (0, i)) for b in blocks]
            + [pl.BlockSpec((rows, ranks), lambda i, index: (0, 0))],
            out_specs=pl.BlockSpec((rows, tile), lambda i, index: (0, i)),
            scratch_shapes=[pltpu.VMEM((ranks, tile), BF16)],
        ),
        out_shape=jax.ShapeDtypeStruct((rows, columns), BF16),
        compiler_params=pltpu.CompilerParams(vmem_limit_bytes=VMEM_LIMIT),
        cost_estimate=pl.CostEstimate(
            flops=2 * rows * columns * ranks, bytes_accessed=2 * rows * columns, transcendentals=0
        ),
    )(index, *blocks, basis)


def solution(mesh):
    ring = Ring(mesh.shape["dp"], mesh.shape["mp"])

    def local(activations, out_grads, basis, first_moment, second_moment):
        d, m = lax.axis_index("dp"), lax.axis_index("mp")
        index = jnp.stack([d // 2, d % 2, m % 2, m // 2]).astype(jnp.int32)
        piece = scatter_basis(basis, activations.shape[1], ring.dp, ring.mp)
        send, keep = project(ring, index, ring.gather(piece), activations)
        projected = sum_columns(ring, send, keep)
        to_swap = grad_rows(ring, index, projected, out_grads, True)
        to_keep = grad_rows(ring, index, projected, out_grads, False)
        gradient = ring.scatter_sum(to_swap, to_keep)
        moment_one = BETA_ONE * first_moment + (1.0 - BETA_ONE) * gradient
        moment_two = BETA_TWO * second_moment + (1.0 - BETA_TWO) * gradient * gradient
        unbiased_one = moment_one / (1.0 - BETA_ONE**STEP)
        unbiased_two = moment_two / (1.0 - BETA_TWO**STEP)
        direction = (unbiased_one / (jnp.sqrt(unbiased_two) + ADAM_EPS)).astype(BF16)
        update = make_update(ring, index, ring.gather(direction), basis)
        return (update, moment_one, moment_two)

    return jax.shard_map(
        local,
        mesh=mesh,
        in_specs=(P("dp", "mp"), P("dp", "mp"), P("dp", None), P("dp", "mp"), P("dp", "mp")),
        out_specs=(P("dp", "mp"), P("dp", "mp"), P("dp", "mp")),
        check_vma=False,
    )
```

time: 418 us -> 235 us (0.56)
  waiting for transfers between devices: 328 us -> 121 us
  starting transfers between devices: 0.12 us -> 71.3 us
  blocking collectives: 40.6 us -> 0 us
  Pallas kernels: 0 us -> 29.3 us
  matrix products: 22.5 us -> 0 us
  between operations: 13.8 us -> 0.94 us
  local copies, waits for them, and re-layouts: 9.94 us -> 0.98 us
  other arithmetic: 2.88 us -> 7.79 us
    all_gather x2 -> x0, waiting for transfers between devices: 196 us -> none  [the longest x1 130 us: local(): whole_basis = lax.all_gather(basis, 'dp', axis=0, tiled=True)]
    reduce_scatter x1 -> x0, waiting for transfers between devices: 131 us -> none  [local(): lax.psum_scatter(lax.dot_general(projected, out_grads, (((0,), (0,)), (()...]
    ppermute x0 -> x36, waiting for transfers between devices: none -> 121 us  [the longest x9 44.1 us: down(): lax.ppermute(value, AXES, self.pairs(lambda z, x: (z - 1, x) if z > 0 and...]
    ppermute x0 -> x36, starting transfers between devices: none -> 71.3 us  [the longest x9 47.1 us: up(): lax.ppermute(value, AXES, self.pairs(lambda z, x: (z + 1, x) if z + 1 < s...]
    psum x1 -> x0, blocking collectives: 40.6 us -> none  [local(): projected = lax.psum(partial_value, 'mp').astype(jnp.bfloat16)]
    pallas_call x0 -> x4, Pallas kernels: none -> 29.3 us  [the longest x2 15.7 us: grad_rows(): pl.pallas_call(kernel, grid_spec=pltpu.PrefetchScalarGridSpec(num_scalar_...]
    dot_general x3 -> x0, matrix products: 22.5 us -> none  [the longest x1 9.08 us: local(): lax.dot_general(projected, out_grads, (((0,), (0,)), ((), ())), preferred...]
    unnamed x7 -> x4, local copies, waits for them, and re-layouts: 9.94 us -> 0.01 us
  transfers between devices with their start and end apart: 3 -> 36, of which waited for: 3 -> 24; matrix products, arithmetic and copies ran while one was open for 0% -> 2% of each run, Pallas kernels for 0% -> 3%
where the time goes in v1:
time: 235 us; the launch traced here: 231 us
  waiting for transfers between devices  121 us (51%)
  starting transfers between devices  71.3 us (30%)
  Pallas kernels  29.3 us (12%)
  other arithmetic  7.79 us (3%)
    ppermute x9, starting transfers between devices, up(): lax.ppermute(value, AXES, self.pairs(lambda z, x: (z + 1, x) if z + 1 < s...  47.1 us
    ppermute x9, waiting for transfers between devices, down(): lax.ppermute(value, AXES, self.pairs(lambda z, x: (z - 1, x) if z > 0 and...  44.1 us
    ppermute x12, waiting for transfers between devices, swap(): return lax.ppermute(value, AXES, self.pairs(lambda z, x: (z, 1 - x)))  39.7 us
    ppermute x5, waiting for transfers between devices, move(): return lax.ppermute(value, AXES, pairs)  25.4 us
    pallas_call x2, Pallas kernels, grad_rows(): pl.pallas_call(kernel, grid_spec=pltpu.PrefetchScalarGridSpec(num_scalar_...  15.7 us
    ppermute x12, starting transfers between devices, swap(): return lax.ppermute(value, AXES, self.pairs(lambda z, x: (z, 1 - x)))  11.8 us
    ppermute x9, waiting for transfers between devices, up(): lax.ppermute(value, AXES, self.pairs(lambda z, x: (z + 1, x) if z + 1 < s...  11.6 us
    ppermute x9, starting transfers between devices, down(): lax.ppermute(value, AXES, self.pairs(lambda z, x: (z - 1, x) if z > 0 and...  11.2 us
  transfers between devices with their start and end apart: 36, of which 24 were waited for; matrix products, arithmetic and copies ran while one was open for 2% of the time, Pallas kernels for 3%

profile of v1, /device:TPU:0, one launch (start us, length us, event | category | flops | bytes accessed | tf_op | source)
XLA Modules:
  0.0 231.2 jit_solution(2376551398731518090)
XLA Ops:
  3.6 24.5 %collective-permute-start.1 = (bf16[256,512]{1,0:T(8,128)(2,1)S(1)}, bf16[256,512]{1,0:T(8,128)(2,1)S(1)}, u32[]{:S(2)}, u32[]{:S(2)}) collective-permute-start(bf16[256,512]{1,0:T(8,128)(2,1)S(1)} %collective-permute-done.refs_0_), channel_id=1, source_target_pairs={{0,8},{1,9},{2,10},{3,11},{4,12},{5,13},{6,14},{7,15},{8,16},{9,17... | collective-permute-start | bytes 786440 | tf_op jit(solution)/shard_map/ppermute | solution.py:52
  28.1 3.8 %collective-permute-done.4.refs_4_ = bf16[256,512]{1,0:T(8,128)(2,1)S(1)} collective-permute-done((bf16[256,512]{1,0:T(8,128)(2,1)S(1)}, bf16[256,512]{1,0:T(8,128)(2,1)S(1)}, u32[]{:S(2)}, u32[]{:S(2)}) %collective-permute-start.4) | collective-permute-done | bytes 262176 | tf_op jit(solution)/shard_map/ppermute | solution.py:55
  34.4 8.8 %collective-permute-done.5.refs_5_ = bf16[256,512]{1,0:T(8,128)(2,1)S(1)} collective-permute-done((bf16[256,512]{1,0:T(8,128)(2,1)S(1)}, bf16[256,512]{1,0:T(8,128)(2,1)S(1)}, u32[]{:S(2)}, u32[]{:S(2)}) %collective-permute-start.5) | collective-permute-done | bytes 262176 | tf_op jit(solution)/shard_map/ppermute | solution.py:55
  45.3 2.1 collective-permute-start.9
  47.4 5.6 %collective-permute-done.6.refs_6_ = bf16[256,512]{1,0:T(8,128)(2,1)S(1)} collective-permute-done((bf16[256,512]{1,0:T(8,128)(2,1)S(1)}, bf16[256,512]{1,0:T(8,128)(2,1)S(1)}, u32[]{:S(2)}, u32[]{:S(2)}) %collective-permute-start.6) | collective-permute-done | bytes 262176 | tf_op jit(solution)/shard_map/ppermute | solution.py:55
  53.7 2.0 collective-permute-start.8
  55.8 4.3 %collective-permute-done.9.refs_9_ = bf16[256,512]{1,0:T(8,128)(2,1)S(1)} collective-permute-done((bf16[256,512]{1,0:T(8,128)(2,1)S(1)}, bf16[256,512]{1,0:T(8,128)(2,1)S(1)}, u32[]{:S(2)}, u32[]{:S(2)}) %collective-permute-start.9) | collective-permute-done | bytes 262176 | tf_op jit(solution)/shard_map/ppermute | solution.py:49
  60.1 5.6 %collective-permute-done.10.refs_10_ = bf16[256,512]{1,0:T(8,128)(2,1)S(1)} collective-permute-done((bf16[256,512]{1,0:T(8,128)(2,1)}, bf16[256,512]{1,0:T(8,128)(2,1)S(1)}, u32[]{:S(2)}, u32[]{:S(2)}) %collective-permute-start.10) | collective-permute-done | bytes 262176 | tf_op jit(solution)/shard_map/ppermute | solution.py:49
  65.7 4.3 %collective-permute-done.8.refs_8_ = bf16[256,512]{1,0:T(8,128)(2,1)S(1)} collective-permute-done((bf16[256,512]{1,0:T(8,128)(2,1)S(1)}, bf16[256,512]{1,0:T(8,128)(2,1)S(1)}, u32[]{:S(2)}, u32[]{:S(2)}) %collective-permute-start.8) | collective-permute-done | bytes 262176 | tf_op jit(solution)/shard_map/ppermute | solution.py:49
  70.0 5.6 %shard_map.76 = (f32[512,512]{1,0:T(8,128)S(1)}, f32[512,512]{1,0:T(8,128)S(1)}) custom-call(s32[4]{0:T(128)S(1)} %pad_add_fusion.index_ref, bf16[256,512]{1,0:T(8,128)(2,1)S(1)} %collective-permute-done.refs_0_, bf16[256,512]{1,0:T(8,128)(2,1)S(1)} %collective-permute-done.1.refs_1_, bf16[256,512]{1,0:T(8,128)(2,1)S(1)} %collective-permute-done.2.refs_2_, ...), custom_call_target="tpu_custom_call" | custom-call | flops 2147483648 | bytes 4194304 | tf_op jit(solution)/shard_map/pallas_call | solution.py:165
  75.7 2.6 %collective-permute-done.11 = f32[512,512]{1,0:T(8,128)S(1)} collective-permute-done((f32[512,512]{1,0:T(8,128)S(1)}, f32[512,512]{1,0:T(8,128)S(1)}, u32[]{:S(2)}, u32[]{:S(2)}) %collective-permute-start.11) | collective-permute-done | bytes 1048608 | tf_op jit(solution)/shard_map/ppermute | solution.py:197
  78.5 14.0 %collective-permute-done.12 = f32[256,512]{1,0:T(8,128)S(1)} collective-permute-done((f32[256,512]{1,0:T(8,128)S(1)}, f32[256,512]{1,0:T(8,128)S(1)}, u32[]{:S(2)}, u32[]{:S(2)}) %collective-permute-start.12) | collective-permute-done | bytes 524320 | tf_op jit(solution)/shard_map/ppermute | solution.py:197
  92.9 7.2 %collective-permute-done.13.refs_1_ = bf16[256,512]{1,0:T(8,128)(2,1)S(1)} collective-permute-done((bf16[256,512]{1,0:T(8,128)(2,1)S(1)}, bf16[256,512]{1,0:T(8,128)(2,1)S(1)}, u32[]{:S(2)}, u32[]{:S(2)}) %collective-permute-start.13) | collective-permute-done | bytes 262176 | tf_op jit(solution)/shard_map/ppermute | solution.py:197
  101.7 7.9 %shard_map.78 = (bf16[64,3584]{1,0:T(8,128)(2,1)S(1)}, bf16[64,3584]{1,0:T(8,128)(2,1)S(1)}, bf16[64,3584]{1,0:T(8,128)(2,1)S(1)}, bf16[64,3584]{1,0:T(8,128)(2,1)S(1)}) custom-call(s32[4]{0:T(128)S(1)} %pad_add_fusion.index_ref, bf16[256,512]{1,0:T(8,128)(2,1)S(1)} %fusion.3.refs_0_, bf16[256,512]{1,0:T(8,128)(2,1)S(1)} %collective-permute-done.13.refs_1_, ...), custom_call_target="tpu_custom_call" | custom-call | flops 1879048192 | bytes 7340032 | tf_op jit(solution)/shard_map/pallas_call | solution.py:238
  111.7 7.9 %shard_map.77 = (bf16[64,3584]{1,0:T(8,128)(2,1)S(1)}, bf16[64,3584]{1,0:T(8,128)(2,1)S(1)}, bf16[64,3584]{1,0:T(8,128)(2,1)S(1)}, bf16[64,3584]{1,0:T(8,128)(2,1)S(1)}) custom-call(s32[4]{0:T(128)S(1)} %pad_add_fusion.index_ref, bf16[256,512]{1,0:T(8,128)(2,1)S(1)} %fusion.3.refs_0_, bf16[256,512]{1,0:T(8,128)(2,1)S(1)} %collective-permute-done.13.refs_1_, ...), custom_call_target="tpu_custom_call" | custom-call | flops 1879048192 | bytes 7340032 | tf_op jit(solution)/shard_map/pallas_call | solution.py:238
  119.5 3.5 %collective-permute-done.19 = bf16[64,3584]{1,0:T(8,128)(2,1)S(1)} collective-permute-done((bf16[64,3584]{1,0:T(8,128)(2,1)S(1)}, bf16[64,3584]{1,0:T(8,128)(2,1)S(1)}, u32[]{:S(2)}, u32[]{:S(2)}) %collective-permute-start.19) | collective-permute-done | bytes 458784 | tf_op jit(solution)/shard_map/ppermute | solution.py:49
  123.1 4.3 %collective-permute-start.23 = (bf16[64,3584]{1,0:T(8,128)(2,1)S(1)}, bf16[64,3584]{1,0:T(8,128)(2,1)S(1)}, u32[]{:S(2)}, u32[]{:S(2)}) collective-permute-start(bf16[64,3584]{1,0:T(8,128)(2,1)S(1)} %fusion.1), channel_id=1, source_target_pairs={{0,8},{1,9},{2,10},{3,11},{4,12},{5,13},{6,14},{7,15}} | collective-permute-start | bytes 1376264 | tf_op jit(solution)/shard_map/ppermute | solution.py:52
  128.5 4.3 %collective-permute-done.18 = bf16[64,3584]{1,0:T(8,128)(2,1)S(1)} collective-permute-done((bf16[64,3584]{1,0:T(8,128)(2,1)S(1)}, bf16[64,3584]{1,0:T(8,128)(2,1)S(1)}, u32[]{:S(2)}, u32[]{:S(2)}) %collective-permute-start.18) | collective-permute-done | bytes 458784 | tf_op jit(solution)/shard_map/ppermute | solution.py:49
  132.8 3.0 %collective-permute-done.23 = bf16[64,3584]{1,0:T(8,128)(2,1)S(1)} collective-permute-done((bf16[64,3584]{1,0:T(8,128)(2,1)S(1)}, bf16[64,3584]{1,0:T(8,128)(2,1)S(1)}, u32[]{:S(2)}, u32[]{:S(2)}) %collective-permute-start.23) | collective-permute-done | bytes 458784 | tf_op jit(solution)/shard_map/ppermute | solution.py:52
  138.5 5.0 %collective-permute-start.24 = (bf16[64,3584]{1,0:T(8,128)(2,1)}, bf16[64,3584]{1,0:T(8,128)(2,1)}, u32[]{:S(2)}, u32[]{:S(2)}) collective-permute-start(bf16[64,3584]{1,0:T(8,128)(2,1)} %get-tuple-element.29), channel_id=1, source_target_pairs={{0,8},{1,9},{2,10},{3,11},{4,12},{5,13},{6,14},{7,15},{8,16},{9,17... | collective-permute-start | bytes 1376264 | tf_op jit(solution)/shard_map/ppermute | solution.py:52
  143.9 6.9 %collective-permute-done.24 = bf16[64,3584]{1,0:T(8,128)(2,1)} collective-permute-done((bf16[64,3584]{1,0:T(8,128)(2,1)}, bf16[64,3584]{1,0:T(8,128)(2,1)}, u32[]{:S(2)}, u32[]{:S(2)}) %collective-permute-start.24) | collective-permute-done | bytes 458784 | tf_op jit(solution)/shard_map/ppermute | solution.py:52
  153.8 5.5 %collective-permute-start.25 = (bf16[64,3584]{1,0:T(8,128)(2,1)S(1)}, bf16[64,3584]{1,0:T(8,128)(2,1)S(1)}, u32[]{:S(2)}, u32[]{:S(2)}) collective-permute-start(bf16[64,3584]{1,0:T(8,128)(2,1)S(1)} %get-tuple-element.27), channel_id=1, source_target_pairs={{0,8},{1,9},{2,10},{3,11},{4,12},{5,13},{6,14},{7,15},{8,16},{9,17... | collective-permute-start | bytes 1376264 | tf_op jit(solution)/shard_map/ppermute | solution.py:52
  159.4 5.5 %collective-permute-done.22 = bf16[64,3584]{1,0:T(8,128)(2,1)S(1)} collective-permute-done((bf16[64,3584]{1,0:T(8,128)(2,1)S(1)}, bf16[64,3584]{1,0:T(8,128)(2,1)S(1)}, u32[]{:S(2)}, u32[]{:S(2)}) %collective-permute-start.22) | collective-permute-done | bytes 458784 | tf_op jit(solution)/shard_map/ppermute | solution.py:55
  166.0 3.5 %divide_convert_fusion = (bf16[64,3584]{1,0:T(8,128)(2,1)S(1)}, f32[64,3584]{1,0:T(8,128)}, f32[64,3584]{1,0:T(8,128)}) fusion(bf16[64,3584]{1,0:T(8,128)(2,1)S(1)} %collective-permute-done.25, bf16[64,3584]{1,0:T(8,128)(2,1)S(1)} %collective-permute-done.22, bf16[64,3584]{1,0:T(8,128)(2,1)S(1)} %collective-permute-done.16, ...), kind=kLoop, calls=%fused_computation.2 | loop fusion | flops 4358144 | bytes 5963776 | tf_op jit(solution)/shard_map/convert_element_type | solution.py:304
  170.8 5.0 %collective-permute-start.26 = (bf16[64,3584]{1,0:T(8,128)(2,1)S(1)}, bf16[64,3584]{1,0:T(8,128)(2,1)S(1)}, u32[]{:S(2)}, u32[]{:S(2)}) collective-permute-start(bf16[64,3584]{1,0:T(8,128)(2,1)S(1)} %get-tuple-element.23.refs_0_), channel_id=1, source_target_pairs={{0,8},{1,9},{2,10},{3,11},{4,12},{5,13},{6,14},{7,15},{8,16},{9,17... | collective-permute-start | bytes 1376264 | tf_op jit(solution)/shard_map/ppermute | solution.py:52
  175.8 4.6 %collective-permute-done.29.refs_4_ = bf16[64,3584]{1,0:T(8,128)(2,1)S(1)} collective-permute-done((bf16[64,3584]{1,0:T(8,128)(2,1)S(1)}, bf16[64,3584]{1,0:T(8,128)(2,1)S(1)}, u32[]{:S(2)}, u32[]{:S(2)}) %collective-permute-start.29) | collective-permute-done | bytes 458784 | tf_op jit(solution)/shard_map/ppermute | solution.py:55
  183.9 9.0 %collective-permute-done.30.refs_5_ = bf16[64,3584]{1,0:T(8,128)(2,1)S(1)} collective-permute-done((bf16[64,3584]{1,0:T(8,128)(2,1)S(1)}, bf16[64,3584]{1,0:T(8,128)(2,1)S(1)}, u32[]{:S(2)}, u32[]{:S(2)}) %collective-permute-start.30) | collective-permute-done | bytes 458784 | tf_op jit(solution)/shard_map/ppermute | solution.py:55
  196.3 6.9 %collective-permute-done.31.refs_6_ = bf16[64,3584]{1,0:T(8,128)(2,1)S(1)} collective-permute-done((bf16[64,3584]{1,0:T(8,128)(2,1)S(1)}, bf16[64,3584]{1,0:T(8,128)(2,1)S(1)}, u32[]{:S(2)}, u32[]{:S(2)}) %collective-permute-start.31) | collective-permute-done | bytes 458784 | tf_op jit(solution)/shard_map/ppermute | solution.py:55
  205.4 2.6 %collective-permute-done.34.refs_9_ = bf16[64,3584]{1,0:T(8,128)(2,1)S(1)} collective-permute-done((bf16[64,3584]{1,0:T(8,128)(2,1)S(1)}, bf16[64,3584]{1,0:T(8,128)(2,1)S(1)}, u32[]{:S(2)}, u32[]{:S(2)}) %collective-permute-start.34) | collective-permute-done | bytes 458784 | tf_op jit(solution)/shard_map/ppermute | solution.py:49
  208.0 9.8 %collective-permute-done.35.refs_10_ = bf16[64,3584]{1,0:T(8,128)(2,1)S(1)} collective-permute-done((bf16[64,3584]{1,0:T(8,128)(2,1)S(1)}, bf16[64,3584]{1,0:T(8,128)(2,1)S(1)}, u32[]{:S(2)}, u32[]{:S(2)}) %collective-permute-start.35) | collective-permute-done | bytes 458784 | tf_op jit(solution)/shard_map/ppermute | solution.py:49
  217.8 5.3 %collective-permute-done.33.refs_8_ = bf16[64,3584]{1,0:T(8,128)(2,1)S(1)} collective-permute-done((bf16[64,3584]{1,0:T(8,128)(2,1)S(1)}, bf16[64,3584]{1,0:T(8,128)(2,1)S(1)}, u32[]{:S(2)}, u32[]{:S(2)}) %collective-permute-start.33) | collective-permute-done | bytes 458784 | tf_op jit(solution)/shard_map/ppermute | solution.py:49
  223.1 8.1 %shard_map.79 = bf16[1024,3584]{1,0:T(8,128)(2,1)} custom-call(s32[4]{0:T(128)S(1)} %pad_add_fusion.index_ref, bf16[64,3584]{1,0:T(8,128)(2,1)S(1)} %get-tuple-element.23.refs_0_, bf16[64,3584]{1,0:T(8,128)(2,1)S(1)} %collective-permute-done.26.refs_1_, bf16[64,3584]{1,0:T(8,128)(2,1)S(1)} %collective-permute-done.27.refs_2_, ...), custom_call_target="tpu_custom_call" | custom-call | flops 3758096384 | bytes 7340032 | tf_op jit(solution)/shard_map/pallas_call | solution.py:270
  (60 shorter events, 31.5 us)
Async XLA Ops:
  2.3 29.6 %collective-permute-start.4 = (bf16[256,512]{1,0:T(8,128)(2,1)S(1)}, bf16[256,512]{1,0:T(8,128)(2,1)S(1)}, u32[]{:S(2)}, u32[]{:S(2)}) collective-permute-start(bf16[256,512]{1,0:T(8,128)(2,1)S(1)} %collective-permute-done.refs_0_), channel_id=1, source_target_pairs={{8,0},{9,1},{10,2},{11,3},{12,4},{13,5},{14,6},{15,7},{16,8},{17,9... | collective-permute-start | bytes 786440 | tf_op jit(solution)/shard_map/ppermute | solution.py:55
  3.6 30.1 %collective-permute-start.1 = (bf16[256,512]{1,0:T(8,128)(2,1)S(1)}, bf16[256,512]{1,0:T(8,128)(2,1)S(1)}, u32[]{:S(2)}, u32[]{:S(2)}) collective-permute-start(bf16[256,512]{1,0:T(8,128)(2,1)S(1)} %collective-permute-done.refs_0_), channel_id=1, source_target_pairs={{0,8},{1,9},{2,10},{3,11},{4,12},{5,13},{6,14},{7,15},{8,16},{9,17... | collective-permute-start | bytes 786440 | tf_op jit(solution)/shard_map/ppermute | solution.py:52
  31.9 11.3 %collective-permute-start.5 = (bf16[256,512]{1,0:T(8,128)(2,1)S(1)}, bf16[256,512]{1,0:T(8,128)(2,1)S(1)}, u32[]{:S(2)}, u32[]{:S(2)}) collective-permute-start(bf16[256,512]{1,0:T(8,128)(2,1)S(1)} %collective-permute-done.4.refs_4_), channel_id=1, source_target_pairs={{8,0},{9,1},{10,2},{11,3},{12,4},{13,5},{14,6},{15,7},{16,8},{17,9... | collective-permute-start | bytes 786440 | tf_op jit(solution)/shard_map/ppermute | solution.py:55
  33.7 10.8 %collective-permute-start.2 = (bf16[256,512]{1,0:T(8,128)(2,1)S(1)}, bf16[256,512]{1,0:T(8,128)(2,1)S(1)}, u32[]{:S(2)}, u32[]{:S(2)}) collective-permute-start(bf16[256,512]{1,0:T(8,128)(2,1)S(1)} %collective-permute-done.1.refs_1_), channel_id=1, source_target_pairs={{8,16},{9,17},{10,18},{11,19},{12,20},{13,21},{14,22},{15,23},{16,... | collective-permute-start | bytes 786440 | tf_op jit(solution)/shard_map/ppermute | solution.py:52
  43.2 9.8 %collective-permute-start.6 = (bf16[256,512]{1,0:T(8,128)(2,1)S(1)}, bf16[256,512]{1,0:T(8,128)(2,1)S(1)}, u32[]{:S(2)}, u32[]{:S(2)}) collective-permute-start(bf16[256,512]{1,0:T(8,128)(2,1)S(1)} %collective-permute-done.5.refs_5_), channel_id=1, source_target_pairs={{8,0},{9,1},{10,2},{11,3},{12,4},{13,5},{14,6},{15,7}} | collective-permute-start | bytes 786440 | tf_op jit(solution)/shard_map/ppermute | solution.py:55
  44.5 8.5 %collective-permute-start.3 = (bf16[256,512]{1,0:T(8,128)(2,1)S(1)}, bf16[256,512]{1,0:T(8,128)(2,1)S(1)}, u32[]{:S(2)}, u32[]{:S(2)}) collective-permute-start(bf16[256,512]{1,0:T(8,128)(2,1)S(1)} %collective-permute-done.2.refs_2_), channel_id=1, source_target_pairs={{16,24},{17,25},{18,26},{19,27},{20,28},{21,29},{22,30},{23,31}} | collective-permute-start | bytes 786440 | tf_op jit(solution)/shard_map/ppermute | solution.py:52
  45.2 10.6 %collective-permute-start.7 = (bf16[256,512]{1,0:T(8,128)(2,1)S(1)}, bf16[256,512]{1,0:T(8,128)(2,1)S(1)}, u32[]{:S(2)}, u32[]{:S(2)}) collective-permute-start(bf16[256,512]{1,0:T(8,128)(2,1)S(1)} %collective-permute-done.refs_0_), channel_id=1, source_target_pairs={{0,4},{1,5},{2,6},{3,7},{4,0},{5,1},{6,2},{7,3},{8,12},{9,13},{10,... | collective-permute-start | bytes 786440 | tf_op jit(solution)/shard_map/ppermute | solution.py:49
  45.3 14.8 %collective-permute-start.9 = (bf16[256,512]{1,0:T(8,128)(2,1)S(1)}, bf16[256,512]{1,0:T(8,128)(2,1)S(1)}, u32[]{:S(2)}, u32[]{:S(2)}) collective-permute-start(bf16[256,512]{1,0:T(8,128)(2,1)S(1)} %broadcast_select_fusion.2), channel_id=1, source_target_pairs={{0,4},{1,5},{2,6},{3,7},{4,0},{5,1},{6,2},{7,3},{8,12},{9,13},{10,... | collective-permute-start | bytes 786440 | tf_op jit(solution)/shard_map/ppermute | solution.py:49
  53.7 12.0 %collective-permute-start.10 = (bf16[256,512]{1,0:T(8,128)(2,1)}, bf16[256,512]{1,0:T(8,128)(2,1)S(1)}, u32[]{:S(2)}, u32[]{:S(2)}) collective-permute-start(bf16[256,512]{1,0:T(8,128)(2,1)} %get-tuple-element.32), channel_id=1, source_target_pairs={{0,4},{1,5},{2,6},{3,7},{4,0},{5,1},{6,2},{7,3},{8,12},{9,13},{10,... | collective-permute-start | bytes 786440 | tf_op jit(solution)/shard_map/ppermute | solution.py:49
  53.7 16.3 %collective-permute-start.8 = (bf16[256,512]{1,0:T(8,128)(2,1)S(1)}, bf16[256,512]{1,0:T(8,128)(2,1)S(1)}, u32[]{:S(2)}, u32[]{:S(2)}) collective-permute-start(bf16[256,512]{1,0:T(8,128)(2,1)S(1)} %get-tuple-element.33), channel_id=1, source_target_pairs={{0,4},{1,5},{2,6},{3,7},{4,0},{5,1},{6,2},{7,3},{8,12},{9,13},{10,... | collective-permute-start | bytes 786440 | tf_op jit(solution)/shard_map/ppermute | solution.py:49
  78.4 14.0 %collective-permute-start.12 = (f32[256,512]{1,0:T(8,128)S(1)}, f32[256,512]{1,0:T(8,128)S(1)}, u32[]{:S(2)}, u32[]{:S(2)}) collective-permute-start(f32[256,512]{1,0:T(8,128)S(1)} %slice_add_fusion), channel_id=1, source_target_pairs={{0,2},{1,3},{2,0},{3,1},{4,6},{5,7},{6,4},{7,5},{8,10},{9,11},{10,... | collective-permute-start | bytes 1572872 | tf_op jit(solution)/shard_map/ppermute | solution.py:197
  92.6 7.6 %collective-permute-start.13 = (bf16[256,512]{1,0:T(8,128)(2,1)S(1)}, bf16[256,512]{1,0:T(8,128)(2,1)S(1)}, u32[]{:S(2)}, u32[]{:S(2)}) collective-permute-start(bf16[256,512]{1,0:T(8,128)(2,1)S(1)} %fusion.3.refs_0_), channel_id=1, source_target_pairs={{0,2},{1,3},{2,0},{3,1},{4,6},{5,7},{6,4},{7,5},{8,10},{9,11},{10,... | collective-permute-start | bytes 786440 | tf_op jit(solution)/shard_map/ppermute | solution.py:197
  92.9 7.2 %collective-permute-start.14 = (bf16[256,512]{1,0:T(8,128)(2,1)S(1)}, bf16[256,512]{1,0:T(8,128)(2,1)S(1)}, u32[]{:S(2)}, u32[]{:S(2)}) collective-permute-start(bf16[256,512]{1,0:T(8,128)(2,1)S(1)} %fusion.3.refs_0_), channel_id=1, source_target_pairs={{0,1},{1,0},{2,3},{3,2},{4,5},{5,4},{6,7},{7,6},{8,9},{9,8},{10,11... | collective-permute-start | bytes 786440 | tf_op jit(solution)/shard_map/ppermute | solution.py:197
  109.6 13.4 %collective-permute-start.19 = (bf16[64,3584]{1,0:T(8,128)(2,1)S(1)}, bf16[64,3584]{1,0:T(8,128)(2,1)S(1)}, u32[]{:S(2)}, u32[]{:S(2)}) collective-permute-start(bf16[64,3584]{1,0:T(8,128)(2,1)S(1)} %get-tuple-element.22), channel_id=1, source_target_pairs={{0,4},{1,5},{2,6},{3,7},{4,0},{5,1},{6,2},{7,3},{8,12},{9,13},{10,... | collective-permute-start | bytes 1376264 | tf_op jit(solution)/shard_map/ppermute | solution.py:49
  109.9 22.9 %collective-permute-start.18 = (bf16[64,3584]{1,0:T(8,128)(2,1)S(1)}, bf16[64,3584]{1,0:T(8,128)(2,1)S(1)}, u32[]{:S(2)}, u32[]{:S(2)}) collective-permute-start(bf16[64,3584]{1,0:T(8,128)(2,1)S(1)} %get-tuple-element.20), channel_id=1, source_target_pairs={{0,4},{1,5},{2,6},{3,7},{4,0},{5,1},{6,2},{7,3},{8,12},{9,13},{10,... | collective-permute-start | bytes 1376264 | tf_op jit(solution)/shard_map/ppermute | solution.py:49
  123.1 12.7 %collective-permute-start.23 = (bf16[64,3584]{1,0:T(8,128)(2,1)S(1)}, bf16[64,3584]{1,0:T(8,128)(2,1)S(1)}, u32[]{:S(2)}, u32[]{:S(2)}) collective-permute-start(bf16[64,3584]{1,0:T(8,128)(2,1)S(1)} %fusion.1), channel_id=1, source_target_pairs={{0,8},{1,9},{2,10},{3,11},{4,12},{5,13},{6,14},{7,15}} | collective-permute-start | bytes 1376264 | tf_op jit(solution)/shard_map/ppermute | solution.py:52
  127.4 8.4 %collective-permute-start.20 = (bf16[64,3584]{1,0:T(8,128)(2,1)S(1)}, bf16[64,3584]{1,0:T(8,128)(2,1)S(1)}, u32[]{:S(2)}, u32[]{:S(2)}) collective-permute-start(bf16[64,3584]{1,0:T(8,128)(2,1)S(1)} %fusion.1), channel_id=1, source_target_pairs={{24,16},{25,17},{26,18},{27,19},{28,20},{29,21},{30,22},{31,23}} | collective-permute-start | bytes 1376264 | tf_op jit(solution)/shard_map/ppermute | solution.py:55
  128.1 15.7 %collective-permute-start.17 = (bf16[64,3584]{1,0:T(8,128)(2,1)S(1)}, bf16[64,3584]{1,0:T(8,128)(2,1)}, u32[]{:S(2)}, u32[]{:S(2)}) collective-permute-start(bf16[64,3584]{1,0:T(8,128)(2,1)S(1)} %get-tuple-element.18), channel_id=1, source_target_pairs={{0,4},{1,5},{2,6},{3,7},{4,0},{5,1},{6,2},{7,3},{8,12},{9,13},{10,... | collective-permute-start | bytes 1376264 | tf_op jit(solution)/shard_map/ppermute | solution.py:49
  138.5 12.2 %collective-permute-start.24 = (bf16[64,3584]{1,0:T(8,128)(2,1)}, bf16[64,3584]{1,0:T(8,128)(2,1)}, u32[]{:S(2)}, u32[]{:S(2)}) collective-permute-start(bf16[64,3584]{1,0:T(8,128)(2,1)} %get-tuple-element.29), channel_id=1, source_target_pairs={{0,8},{1,9},{2,10},{3,11},{4,12},{5,13},{6,14},{7,15},{8,16},{9,17... | collective-permute-start | bytes 1376264 | tf_op jit(solution)/shard_map/ppermute | solution.py:52
  143.6 15.8 %collective-permute-start.16 = (bf16[64,3584]{1,0:T(8,128)(2,1)S(1)}, bf16[64,3584]{1,0:T(8,128)(2,1)S(1)}, u32[]{:S(2)}, u32[]{:S(2)}) collective-permute-start(bf16[64,3584]{1,0:T(8,128)(2,1)S(1)} %get-tuple-element.16), channel_id=1, source_target_pairs={{0,4},{1,5},{2,6},{3,7},{4,0},{5,1},{6,2},{7,3},{8,12},{9,13},{10,... | collective-permute-start | bytes 1376264 | tf_op jit(solution)/shard_map/ppermute | solution.py:49
  152.5 12.3 %collective-permute-start.22 = (bf16[64,3584]{1,0:T(8,128)(2,1)S(1)}, bf16[64,3584]{1,0:T(8,128)(2,1)S(1)}, u32[]{:S(2)}, u32[]{:S(2)}) collective-permute-start(bf16[64,3584]{1,0:T(8,128)(2,1)S(1)} %get-tuple-element.26), channel_id=1, source_target_pairs={{8,0},{9,1},{10,2},{11,3},{12,4},{13,5},{14,6},{15,7},{16,8},{17,9... | collective-permute-start | bytes 1376264 | tf_op jit(solution)/shard_map/ppermute | solution.py:55
  153.8 12.2 %collective-permute-start.25 = (bf16[64,3584]{1,0:T(8,128)(2,1)S(1)}, bf16[64,3584]{1,0:T(8,128)(2,1)S(1)}, u32[]{:S(2)}, u32[]{:S(2)}) collective-permute-start(bf16[64,3584]{1,0:T(8,128)(2,1)S(1)} %get-tuple-element.27), channel_id=1, source_target_pairs={{0,8},{1,9},{2,10},{3,11},{4,12},{5,13},{6,14},{7,15},{8,16},{9,17... | collective-permute-start | bytes 1376264 | tf_op jit(solution)/shard_map/ppermute | solution.py:52
  169.5 10.9 %collective-permute-start.29 = (bf16[64,3584]{1,0:T(8,128)(2,1)S(1)}, bf16[64,3584]{1,0:T(8,128)(2,1)S(1)}, u32[]{:S(2)}, u32[]{:S(2)}) collective-permute-start(bf16[64,3584]{1,0:T(8,128)(2,1)S(1)} %get-tuple-element.23.refs_0_), channel_id=1, source_target_pairs={{8,0},{9,1},{10,2},{11,3},{12,4},{13,5},{14,6},{15,7},{16,8},{17,9... | collective-permute-start | bytes 1376264 | tf_op jit(solution)/shard_map/ppermute | solution.py:55
  170.8 11.0 %collective-permute-start.26 = (bf16[64,3584]{1,0:T(8,128)(2,1)S(1)}, bf16[64,3584]{1,0:T(8,128)(2,1)S(1)}, u32[]{:S(2)}, u32[]{:S(2)}) collective-permute-start(bf16[64,3584]{1,0:T(8,128)(2,1)S(1)} %get-tuple-element.23.refs_0_), channel_id=1, source_target_pairs={{0,8},{1,9},{2,10},{3,11},{4,12},{5,13},{6,14},{7,15},{8,16},{9,17... | collective-permute-start | bytes 1376264 | tf_op jit(solution)/shard_map/ppermute | solution.py:52
  180.4 12.5 %collective-permute-start.30 = (bf16[64,3584]{1,0:T(8,128)(2,1)S(1)}, bf16[64,3584]{1,0:T(8,128)(2,1)S(1)}, u32[]{:S(2)}, u32[]{:S(2)}) collective-permute-start(bf16[64,3584]{1,0:T(8,128)(2,1)S(1)} %collective-permute-done.29.refs_4_), channel_id=1, source_target_pairs={{8,0},{9,1},{10,2},{11,3},{12,4},{13,5},{14,6},{15,7},{16,8},{17,9... | collective-permute-start | bytes 1376264 | tf_op jit(solution)/shard_map/ppermute | solution.py:55
  181.8 12.4 %collective-permute-start.27 = (bf16[64,3584]{1,0:T(8,128)(2,1)S(1)}, bf16[64,3584]{1,0:T(8,128)(2,1)S(1)}, u32[]{:S(2)}, u32[]{:S(2)}) collective-permute-start(bf16[64,3584]{1,0:T(8,128)(2,1)S(1)} %collective-permute-done.26.refs_1_), channel_id=1, source_target_pairs={{8,16},{9,17},{10,18},{11,19},{12,20},{13,21},{14,22},{15,23},{16,... | collective-permute-start | bytes 1376264 | tf_op jit(solution)/shard_map/ppermute | solution.py:52
  182.5 22.9 %collective-permute-start.32 = (bf16[64,3584]{1,0:T(8,128)(2,1)S(1)}, bf16[64,3584]{1,0:T(8,128)(2,1)S(1)}, u32[]{:S(2)}, u32[]{:S(2)}) collective-permute-start(bf16[64,3584]{1,0:T(8,128)(2,1)S(1)} %get-tuple-element.23.refs_0_), channel_id=1, source_target_pairs={{0,4},{1,5},{2,6},{3,7},{4,0},{5,1},{6,2},{7,3},{8,12},{9,13},{10,... | collective-permute-start | bytes 1376264 | tf_op jit(solution)/shard_map/ppermute | solution.py:49
  192.9 10.4 %collective-permute-start.31 = (bf16[64,3584]{1,0:T(8,128)(2,1)S(1)}, bf16[64,3584]{1,0:T(8,128)(2,1)S(1)}, u32[]{:S(2)}, u32[]{:S(2)}) collective-permute-start(bf16[64,3584]{1,0:T(8,128)(2,1)S(1)} %collective-permute-done.30.refs_5_), channel_id=1, source_target_pairs={{8,0},{9,1},{10,2},{11,3},{12,4},{13,5},{14,6},{15,7}} | collective-permute-start | bytes 1376264 | tf_op jit(solution)/shard_map/ppermute | solution.py:55
  194.2 9.1 %collective-permute-start.28 = (bf16[64,3584]{1,0:T(8,128)(2,1)S(1)}, bf16[64,3584]{1,0:T(8,128)(2,1)S(1)}, u32[]{:S(2)}, u32[]{:S(2)}) collective-permute-start(bf16[64,3584]{1,0:T(8,128)(2,1)S(1)} %collective-permute-done.27.refs_2_), channel_id=1, source_target_pairs={{16,24},{17,25},{18,26},{19,27},{20,28},{21,29},{22,30},{23,31}} | collective-permute-start | bytes 1376264 | tf_op jit(solution)/shard_map/ppermute | solution.py:52
  194.9 13.1 %collective-permute-start.34 = (bf16[64,3584]{1,0:T(8,128)(2,1)S(1)}, bf16[64,3584]{1,0:T(8,128)(2,1)S(1)}, u32[]{:S(2)}, u32[]{:S(2)}) collective-permute-start(bf16[64,3584]{1,0:T(8,128)(2,1)S(1)} %broadcast_select_fusion), channel_id=1, source_target_pairs={{0,4},{1,5},{2,6},{3,7},{4,0},{5,1},{6,2},{7,3},{8,12},{9,13},{10,... | collective-permute-start | bytes 1376264 | tf_op jit(solution)/shard_map/ppermute | solution.py:49
  203.3 14.5 %collective-permute-start.35 = (bf16[64,3584]{1,0:T(8,128)(2,1)S(1)}, bf16[64,3584]{1,0:T(8,128)(2,1)S(1)}, u32[]{:S(2)}, u32[]{:S(2)}) collective-permute-start(bf16[64,3584]{1,0:T(8,128)(2,1)S(1)} %get-tuple-element.30), channel_id=1, source_target_pairs={{0,4},{1,5},{2,6},{3,7},{4,0},{5,1},{6,2},{7,3},{8,12},{9,13},{10,... | collective-permute-start | bytes 1376264 | tf_op jit(solution)/shard_map/ppermute | solution.py:49
  204.8 18.4 %collective-permute-start.33 = (bf16[64,3584]{1,0:T(8,128)(2,1)S(1)}, bf16[64,3584]{1,0:T(8,128)(2,1)S(1)}, u32[]{:S(2)}, u32[]{:S(2)}) collective-permute-start(bf16[64,3584]{1,0:T(8,128)(2,1)S(1)} %get-tuple-element.31), channel_id=1, source_target_pairs={{0,4},{1,5},{2,6},{3,7},{4,0},{5,1},{6,2},{7,3},{8,12},{9,13},{10,... | collective-permute-start | bytes 1376264 | tf_op jit(solution)/shard_map/ppermute | solution.py:49
  (6 other events, 111.9 us)

commit v2 on v0

v2 whole, which is shorter than its diff:
```python
import functools

import jax
import jax.numpy as jnp
from jax import lax
from jax.experimental import pallas as pl
from jax.experimental.pallas import tpu as pltpu
from jax.sharding import PartitionSpec as P

STEP = 10

BETA_ONE = 0.9
BETA_TWO = 0.999
ADAM_EPS = 1e-08

BF16 = jnp.bfloat16
F32 = jnp.float32
VMEM_LIMIT = 48 * 1024 * 1024
AXES = ("dp", "mp")
PARTS = 2
HALVES = 2
ANYWHERE = pl.BlockSpec(memory_space=pltpu.MemorySpace.HBM)


def tile_of(columns):
    for tile in (896, 512, 256, 128):
        if columns % tile == 0:
            return tile
    return columns


class Cube:
    def __init__(self, dp, mp):
        self.dp, self.mp = dp, mp
        self.order = [1 << j for j in range(dp.bit_length() - 1)]

    def swap(self, value, bit):
        pairs = [(d * self.mp + m, (d ^ bit) * self.mp + m) for d in range(self.dp) for m in range(self.mp)]
        return lax.ppermute(value, AXES, pairs)

    def sum_order(self):
        k = len(self.order)
        return [
            sum(bit for j, bit in enumerate(self.order) if not (p >> (k - 1 - j)) & 1) for p in range(self.dp)
        ]

    def gather_order(self):
        later = self.order[:1:-1]
        base = [sum(bit for j, bit in enumerate(later) if (i >> j) & 1) for i in range(1 << len(later))]
        first, second = self.order[:2]
        return [[r | extra for r in base] for extra in (0, second, first, first | second)]

    def sum_up(self, quarters):
        sent_first, sent_last, next_out, kept = quarters
        first, second = self.order[:2]
        got_first, got_last = self.swap(sent_first, first), self.swap(sent_last, first)
        out = (next_out.astype(F32) + got_first.astype(F32)).astype(BF16)
        terms = [(kept, 0), (got_last, 0), (self.swap(out, second), 0)]
        rows = kept.shape[0]
        for bit in self.order[2:]:
            rows //= 2
            out = sum(t[at : at + rows].astype(F32) for t, at in terms).astype(BF16)
            terms = [(t, at + rows) for t, at in terms] + [(self.swap(out, bit), 0)]
        return terms

    def gather(self, own):
        first, second = self.order[:2]
        for bit in self.order[:1:-1]:
            own = jnp.concatenate([own, self.swap(own, bit)])
        across = self.swap(own, second)
        return [own, across, self.swap(own, first), self.swap(across, first)]


def split_ranks(basis, dp, part, parts, wait_for):
    if parts == 1:
        return basis
    rows, ranks = basis.shape
    share = ranks // dp
    sub = share // parts

    def kernel(basis_ref, *refs):
        source = lax.broadcasted_iota(jnp.int32, (ranks, ranks // parts), 0)
        target = lax.broadcasted_iota(jnp.int32, (ranks, ranks // parts), 1)
        wanted = (target // sub) * share + part * sub + target % sub
        pick = jnp.where(source == wanted, 1.0, 0.0).astype(BF16)
        refs[-1][...] = jnp.dot(basis_ref[...], pick, preferred_element_type=F32).astype(BF16)

    return pl.pallas_call(
        kernel,
        in_specs=[pl.BlockSpec(basis.shape)] + [ANYWHERE] * len(wait_for),
        out_shape=jax.ShapeDtypeStruct((rows, ranks // parts), BF16),
        compiler_params=pltpu.CompilerParams(vmem_limit_bytes=VMEM_LIMIT),
    )(basis, *wait_for)


def fetch_basis(cube, basis):
    dp, mp = cube.dp, cube.mp
    shards = max(dp // mp // 2, 1)
    here = []
    for j in range(shards):
        pairs = []
        for line in range(dp // 2):
            q = line // shards
            for pair in range(2):
                for m in range(mp):
                    holder = ((q + m) % (mp // 2)) * 2 + q // (mp // 2)
                    source = (m * shards + (line + j) % shards) * 2 + pair
                    pairs.append((source * mp + holder, (line * 2 + pair) * mp + m))
        here.append(lax.ppermute(basis, AXES, pairs))
    return here


def project(cube, index, blocks, activations, wait_for):
    tokens, features = activations.shape
    rows, ranks = blocks[0].shape
    shards = len(blocks) // 2
    half = cube.mp // 2
    step = tokens // (2 * half)

    def block_of(i, index):
        return jnp.where(i < half, 1 - index[1], index[1]) * half + lax.rem(i, half)

    def kernel(index_ref, *refs):
        pieces, act_ref, (send_ref, keep_ref, held) = refs[: 2 * shards], refs[2 * shards], refs[-3:]
        i = pl.program_id(0)

        @pl.when(i == 0)
        def _():
            line, pair = index_ref[0] // 2, lax.rem(index_ref[0], 2)
            for j in range(2 * shards):
                side = pair if j < shards else 1 - pair
                start = (lax.rem(line + j, shards) * 2 + side) * rows
                held[pl.ds(pl.multiple_of(start, rows), rows), :] = pieces[j][...]

        value = jnp.dot(act_ref[...], held[...], preferred_element_type=F32)

        @pl.when(i < half)
        def _():
            send_ref[...] = value

        @pl.when(i >= half)
        def _():
            keep_ref[...] = value

    shape = jax.ShapeDtypeStruct((tokens // 2, ranks), F32)
    return pl.pallas_call(
        kernel,
        grid_spec=pltpu.PrefetchScalarGridSpec(
            num_scalar_prefetch=1,
            grid=(2 * half,),
            in_specs=[pl.BlockSpec(b.shape, lambda i, index: (0, 0)) for b in blocks]
            + [pl.BlockSpec((step, features), lambda i, index: (block_of(i, index), 0))]
            + [ANYWHERE] * len(wait_for),
            out_specs=[
                pl.BlockSpec((step, ranks), lambda i, index: (jnp.minimum(i, half - 1), 0)),
                pl.BlockSpec((step, ranks), lambda i, index: (jnp.maximum(i - half, 0), 0)),
            ],
            scratch_shapes=[pltpu.VMEM((features, ranks), BF16)],
        ),
        out_shape=[shape, shape],
        compiler_params=pltpu.CompilerParams(vmem_limit_bytes=VMEM_LIMIT),
        cost_estimate=pl.CostEstimate(
            flops=2 * tokens * features * ranks, bytes_accessed=2 * tokens * features, transcendentals=0
        ),
    )(index, *blocks, activations, *wait_for)


def sum_columns(cube, send, keep):
    mp, half = cube.mp, cube.mp // 2

    def move(value, core_step, other_step):
        pairs = []
        for d in range(cube.dp):
            for m in range(mp):
                other, core = divmod(m, 2)
                to = ((other + other_step) % half) * 2 + (core + core_step) % 2
                pairs.append((d * mp + m, d * mp + to))
        return lax.ppermute(value, AXES, pairs)

    chip = keep + move(send, 1, 0)
    total = chip
    for j in range(1, half):
        total = total + move(chip, 0, j)
    own = total.astype(BF16)
    return own, move(own, 1, 0)


def grad_rows(cube, index, pieces, out_grads, first_column, columns, wait_for):
    tokens = out_grads.shape[0]
    ranks = pieces[0].shape[1]
    rows = ranks // cube.dp
    quarter = ranks // 4
    tile = tile_of(columns)
    order = cube.sum_order()

    def kernel(index_ref, own_ref, other_ref, grads_ref, *refs):
        outs, (held, turned, picked) = refs[-7:-3], refs[-3:]
        here, core = index_ref[0], index_ref[1]

        @pl.when(pl.program_id(0) == 0)
        def _():
            half = tokens // 2
            held[pl.ds(pl.multiple_of(core * half, half), half), :] = own_ref[...]
            held[pl.ds(pl.multiple_of((1 - core) * half, half), half), :] = other_ref[...]
            turned[...] = held[...].T
            for p, relative in enumerate(order):
                start = pl.multiple_of((here ^ relative) * rows, rows)
                picked[p * rows : (p + 1) * rows, :] = turned[pl.ds(start, rows), :]

        value = jnp.dot(picked[...], grads_ref[...], preferred_element_type=F32).astype(BF16)
        for j in range(4):
            outs[j][...] = value[j * quarter : (j + 1) * quarter, :]

    return pl.pallas_call(
        kernel,
        grid_spec=pltpu.PrefetchScalarGridSpec(
            num_scalar_prefetch=1,
            grid=(columns // tile,),
            in_specs=[pl.BlockSpec((tokens // 2, ranks), lambda i, index: (0, 0))] * 2
            + [pl.BlockSpec((tokens, tile), lambda i, index: (0, first_column // tile + i))]
            + [ANYWHERE] * len(wait_for),
            out_specs=[pl.BlockSpec((quarter, tile), lambda i, index: (0, i))] * 4,
            scratch_shapes=[
                pltpu.VMEM((tokens, ranks), BF16),
                pltpu.VMEM((ranks, tokens), BF16),
                pltpu.VMEM((ranks, tokens), BF16),
            ],
        ),
        out_shape=[jax.ShapeDtypeStruct((quarter, columns), BF16)] * 4,
        compiler_params=pltpu.CompilerParams(vmem_limit_bytes=VMEM_LIMIT),
        cost_estimate=pl.CostEstimate(
            flops=2 * tokens * columns * ranks, bytes_accessed=2 * tokens * columns, transcendentals=0
        ),
    )(index, *pieces, out_grads, *wait_for)


def adam(cube, terms, first_moment, second_moment, part, first_column, before, wait_for):
    columns = terms[0][0].shape[1]
    share, width = first_moment.shape
    rows = terms[-1][0].shape[0]
    count = len(terms)

    def kernel(*refs):
        gradient = refs[0][...].astype(F32)
        for ref in refs[1:count]:
            gradient = gradient + ref[...].astype(F32)
        first_ref, second_ref = refs[count : count + 2]
        direction_ref, one_ref, two_ref = refs[-3:]
        moment_one = BETA_ONE * first_ref[...] + (1.0 - BETA_ONE) * gradient
        moment_two = BETA_TWO * second_ref[...] + (1.0 - BETA_TWO) * gradient * gradient
        unbiased_one = moment_one / (1.0 - BETA_ONE**STEP)
        unbiased_two = moment_two / (1.0 - BETA_TWO**STEP)
        direction_ref[...] = (unbiased_one / (jnp.sqrt(unbiased_two) + ADAM_EPS)).astype(BF16)
        one_ref[...] = moment_one
        two_ref[...] = moment_two

    term_specs = [pl.BlockSpec((rows, columns), lambda i, at=at // rows: (at, 0)) for _, at in terms]
    moment_spec = pl.BlockSpec((rows, columns), lambda i: (part, first_column // columns))
    moment = jax.ShapeDtypeStruct((share, width), F32)
    return pl.pallas_call(
        kernel,
        grid=(1,),
        in_specs=term_specs + [moment_spec] * 2 + [ANYWHERE] * len(before + wait_for),
        out_specs=[pl.BlockSpec((rows, columns), lambda i: (0, 0)), moment_spec, moment_spec],
        out_shape=[jax.ShapeDtypeStruct((rows, columns), BF16), moment, moment],
        input_output_aliases={count + 2: 1, count + 3: 2} if before else {},
        compiler_params=pltpu.CompilerParams(vmem_limit_bytes=VMEM_LIMIT),
        cost_estimate=pl.CostEstimate(
            flops=16 * rows * columns, bytes_accessed=26 * rows * columns, transcendentals=rows * columns
        ),
    )(*(t for t, _ in terms), first_moment, second_moment, *before, *wait_for)


def make_update(cube, index, groups, basis, first_column, width, before):
    rows, ranks = basis.shape
    parts = len(groups)
    columns = groups[0][0].shape[1]
    share = ranks // cube.dp
    sub = share // parts
    tile = tile_of(columns)
    blocks = [b for group in groups for b in group]
    order = cube.gather_order()

    def kernel(index_ref, *refs):
        pieces, basis_ref, (out_ref, held) = refs[: len(blocks)], refs[len(blocks)], refs[-2:]
        here = index_ref[0]
        for part in range(parts):
            for j, relatives in enumerate(order):
                for i, relative in enumerate(relatives):
                    start = pl.multiple_of((here ^ relative) * share + part * sub, sub)
                    held[pl.ds(start, sub), :] = pieces[part * 4 + j][i * sub : (i + 1) * sub, :]
        out_ref[...] = jnp.dot(basis_ref[...], held[...], preferred_element_type=F32).astype(BF16)

    return pl.pallas_call(
        kernel,
        grid_spec=pltpu.PrefetchScalarGridSpec(
            num_scalar_prefetch=1,
            grid=(columns // tile,),
            in_specs=[pl.BlockSpec((b.shape[0], tile), lambda i, index: (0, i)) for b in blocks]
            + [pl.BlockSpec((rows, ranks), lambda i, index: (0, 0))]
            + [ANYWHERE] * len(before),
            out_specs=pl.BlockSpec((rows, tile), lambda i, index: (0, first_column // tile + i)),
            scratch_shapes=[pltpu.VMEM((ranks, tile), BF16)],
        ),
        out_shape=jax.ShapeDtypeStruct((rows, width), BF16),
        input_output_aliases={len(blocks) + 2: 0} if before else {},
        compiler_params=pltpu.CompilerParams(vmem_limit_bytes=VMEM_LIMIT),
        cost_estimate=pl.CostEstimate(
            flops=2 * rows * columns * ranks, bytes_accessed=2 * rows * columns, transcendentals=0
        ),
    )(index, *blocks, basis, *before)


def solution(mesh):
    cube = Cube(mesh.shape["dp"], mesh.shape["mp"])

    def local(activations, out_grads, basis, first_moment, second_moment):
        d, m = lax.axis_index("dp"), lax.axis_index("mp")
        index = jnp.stack([d, m % 2]).astype(jnp.int32)
        share, width = first_moment.shape
        parts = PARTS if share % (16 * PARTS) == 0 else 1
        columns = width // HALVES
        here = []
        for h in range(parts):
            part = split_ranks(basis, cube.dp, h, parts, here[-1][:1] if here else [])
            here.append(fetch_basis(cube, part))
        partial = []
        for h in range(parts):
            blocks = here[h] + [cube.swap(value, 1) for value in here[h]]
            partial.append(project(cube, index, blocks, activations, []))
        groups, moments, update = [[None] * parts for _ in range(HALVES)], [], []
        terms = []
        for h in range(parts):
            projected = sum_columns(cube, *partial[h])
            for f in range(HALVES):
                wait_for = [partial[h + 1][0]] if h + 1 < parts else []
                quarters = grad_rows(cube, index, projected, out_grads, f * columns, columns, wait_for)
                terms.append((h, f, cube.sum_up(quarters)))
        for h, f, sums in terms:
            wait_for = groups[f][h - 1][1:] if h else []
            direction, *moments = adam(cube, sums, first_moment, second_moment, h, f * columns, moments, wait_for)
            groups[f][h] = cube.gather(direction)
        for f in range(HALVES):
            update = [make_update(cube, index, groups[f], basis, f * columns, width, update)]
        return (*update, *moments)

    return jax.shard_map(
        local,
        mesh=mesh,
        in_specs=(P("dp", "mp"), P("dp", "mp"), P("dp", None), P("dp", "mp"), P("dp", "mp")),
        out_specs=(P("dp", "mp"), P("dp", "mp"), P("dp", "mp")),
        check_vma=False,
    )
```

time: 418 us -> 185 us (0.44)
  waiting for transfers between devices: 328 us -> 67.1 us
  starting transfers between devices: 0.12 us -> 75.2 us
  blocking collectives: 40.6 us -> 0 us
  Pallas kernels: 0 us -> 38.3 us
  matrix products: 22.5 us -> 0 us
  between operations: 13.8 us -> 0.97 us
  local copies, waits for them, and re-layouts: 9.94 us -> 2.53 us
    all_gather x2 -> x0, waiting for transfers between devices: 196 us -> none  [the longest x1 130 us: local(): whole_basis = lax.all_gather(basis, 'dp', axis=0, tiled=True)]
    reduce_scatter x1 -> x0, waiting for transfers between devices: 131 us -> none  [local(): lax.psum_scatter(lax.dot_general(projected, out_grads, (((0,), (0,)), (()...]
    ppermute x0 -> x42, starting transfers between devices: none -> 75.2 us  [the longest x34 38.5 us: swap(): return lax.ppermute(value, AXES, pairs)]
    ppermute x0 -> x42, waiting for transfers between devices: none -> 67.1 us  [the longest x34 63.1 us: swap(): return lax.ppermute(value, AXES, pairs)]
    psum x1 -> x0, blocking collectives: 40.6 us -> none  [local(): projected = lax.psum(partial_value, 'mp').astype(jnp.bfloat16)]
    pallas_call x0 -> x14, Pallas kernels: none -> 38.3 us  [the longest x4 15.4 us: grad_rows(): pl.pallas_call(kernel, grid_spec=pltpu.PrefetchScalarGridSpec(num_scalar_...]
    dot_general x3 -> x0, matrix products: 22.5 us -> none  [the longest x1 9.08 us: local(): lax.dot_general(projected, out_grads, (((0,), (0,)), ((), ())), preferred...]
    unnamed x7 -> x14, local copies, waits for them, and re-layouts: 9.94 us -> 2.49 us
  transfers between devices with their start and end apart: 3 -> 42, of which waited for: 3 -> 19; matrix products, arithmetic and copies ran while one was open for 0% -> 0% of each run, Pallas kernels for 0% -> 18%
where the time goes in v2:
time: 185 us
  starting transfers between devices  75.2 us (41%)
  waiting for transfers between devices  67.1 us (36%)
  Pallas kernels  38.3 us (21%)
  local copies, waits for them, and re-layouts  2.53 us (1%)
    ppermute x34, waiting for transfers between devices, swap(): return lax.ppermute(value, AXES, pairs)  63.1 us
    ppermute x34, starting transfers between devices, swap(): return lax.ppermute(value, AXES, pairs)  38.5 us
    ppermute x6, starting transfers between devices, move(): return lax.ppermute(value, AXES, pairs)  35.3 us
    pallas_call x4, Pallas kernels, grad_rows(): pl.pallas_call(kernel, grid_spec=pltpu.PrefetchScalarGridSpec(num_scalar_...  15.4 us
    pallas_call x2, Pallas kernels, make_update(): pl.pallas_call(kernel, grid_spec=pltpu.PrefetchScalarGridSpec(num_scalar_...  9.34 us
    pallas_call x2, Pallas kernels, project(): pl.pallas_call(kernel, grid_spec=pltpu.PrefetchScalarGridSpec(num_scalar_...  9.14 us
    ppermute x6, waiting for transfers between devices, move(): return lax.ppermute(value, AXES, pairs)  3.92 us
  transfers between devices with their start and end apart: 42, of which 19 were waited for; matrix products, arithmetic and copies ran while one was open for 0% of the time, Pallas kernels for 18%

profile of v2, /device:TPU:0, one launch (start us, length us, event | category | flops | bytes accessed | tf_op | source)
XLA Modules:
  0.0 184.8 jit_solution(3604163594529496398)
XLA Ops:
  3.0 3.0 %collective-permute-start.1 = (bf16[1024,256]{1,0:T(8,128)(2,1)S(1)}, bf16[1024,256]{1,0:T(8,128)(2,1)S(1)}, u32[]{:S(2)}, u32[]{:S(2)}) collective-permute-start(bf16[1024,256]{1,0:T(8,128)(2,1)S(1)} %collective-permute-done.refs_0_), channel_id=1, source_target_pairs={{0,4},{1,5},{2,6},{3,7},{4,0},{5,1},{6,2},{7,3},{8,12},{9,13},{10,... | collective-permute-start | bytes 1572872 | tf_op jit(solution)/shard_map/ppermute | solution.py:39
  8.5 4.7 %collective-permute-done.1.refs_1_ = bf16[1024,256]{1,0:T(8,128)(2,1)S(1)} collective-permute-done((bf16[1024,256]{1,0:T(8,128)(2,1)S(1)}, bf16[1024,256]{1,0:T(8,128)(2,1)S(1)}, u32[]{:S(2)}, u32[]{:S(2)}) %collective-permute-start.1) | collective-permute-done | bytes 524320 | tf_op jit(solution)/shard_map/ppermute | solution.py:39
  13.2 4.6 %shard_map.77 = (f32[512,256]{1,0:T(8,128)S(1)}, f32[512,256]{1,0:T(8,128)S(1)}) custom-call(s32[2]{0:T(128)S(1)} %pad_add_fusion.index_ref, bf16[1024,256]{1,0:T(8,128)(2,1)S(1)} %collective-permute-done.refs_0_, bf16[1024,256]{1,0:T(8,128)(2,1)S(1)} %collective-permute-done.1.refs_1_, bf16[1024,2048]{1,0:T(8,128)(2,1)} %refs_2_.3), custom_call_target="tpu_custom_call" | custom-call | flops 1073741824 | bytes 4194304 | tf_op jit(solution)/shard_map/pallas_call | solution.py:146
  17.8 14.0 %collective-permute-start.2 = (f32[512,256]{1,0:T(8,128)S(1)}, f32[512,256]{1,0:T(8,128)S(1)}, u32[]{:S(2)}, u32[]{:S(2)}) collective-permute-start(f32[512,256]{1,0:T(8,128)S(1)} %get-tuple-element.36), channel_id=1, source_target_pairs={{0,1},{1,0},{2,3},{3,2},{4,5},{5,4},{6,7},{7,6},{8,9},{9,8},{10,11... | collective-permute-start | bytes 1572872 | tf_op jit(solution)/shard_map/ppermute | solution.py:178
  33.4 11.4 %collective-permute-start.3 = (f32[512,256]{1,0:T(8,128)S(1)}, f32[512,256]{1,0:T(8,128)S(1)}, u32[]{:S(2)}, u32[]{:S(2)}) collective-permute-start(f32[512,256]{1,0:T(8,128)S(1)} %add.53), channel_id=1, source_target_pairs={{0,2},{1,3},{2,0},{3,1},{4,6},{5,7},{6,4},{7,5},{8,10},{9,11},{10,... | collective-permute-start | bytes 1572872 | tf_op jit(solution)/shard_map/ppermute | solution.py:178
  44.8 4.6 %shard_map.79 = (f32[512,256]{1,0:T(8,128)S(1)}, f32[512,256]{1,0:T(8,128)S(1)}) custom-call(s32[2]{0:T(128)S(1)} %pad_add_fusion.index_ref, bf16[1024,256]{1,0:T(8,128)(2,1)S(1)} %collective-permute-done.5.refs_0_, bf16[1024,256]{1,0:T(8,128)(2,1)S(1)} %collective-permute-done.6.refs_1_, bf16[1024,2048]{1,0:T(8,128)(2,1)} %refs_2_.3), custom_call_target="tpu_custom_call" | custom-call | flops 1073741824 | bytes 4194304 | tf_op jit(solution)/shard_map/pallas_call | solution.py:146
  49.4 4.3 %collective-permute-start.19 = (f32[512,256]{1,0:T(8,128)S(1)}, f32[512,256]{1,0:T(8,128)S(1)}, u32[]{:S(2)}, u32[]{:S(2)}) collective-permute-start(f32[512,256]{1,0:T(8,128)S(1)} %get-tuple-element.37.refs_0_), channel_id=1, source_target_pairs={{0,1},{1,0},{2,3},{3,2},{4,5},{5,4},{6,7},{7,6},{8,9},{9,8},{10,11... | collective-permute-start | bytes 1572872 | tf_op jit(solution)/shard_map/ppermute | solution.py:178
  53.7 2.0 %collective-permute-done.3 = f32[512,256]{1,0:T(8,128)S(1)} collective-permute-done((f32[512,256]{1,0:T(8,128)S(1)}, f32[512,256]{1,0:T(8,128)S(1)}, u32[]{:S(2)}, u32[]{:S(2)}) %collective-permute-start.3) | collective-permute-done | bytes 524320 | tf_op jit(solution)/shard_map/ppermute | solution.py:178
  57.4 3.8 %shard_map.81 = (bf16[64,1792]{1,0:T(8,128)(2,1)S(1)}, bf16[64,1792]{1,0:T(8,128)(2,1)S(1)}, bf16[64,1792]{1,0:T(8,128)(2,1)S(1)}, bf16[64,1792]{1,0:T(8,128)(2,1)S(1)}) custom-call(s32[2]{0:T(128)S(1)} %pad_add_fusion.index_ref, bf16[512,256]{1,0:T(8,128)(2,1)S(1)} %add_convert_fusion.1.own_ref, bf16[512,256]{1,0:T(8,128)(2,1)S(1)} %collective-permute-done.4.other_ref, ...), custom_call_target="tpu_custom_call" | custom-call | flops 939524096 | bytes 3670016 | tf_op jit(solution)/shard_map/pallas_call | solution.py:214
  61.2 1.6 collective-permute-start.12
  62.9 5.4 %collective-permute-start.20 = (f32[512,256]{1,0:T(8,128)S(1)}, f32[512,256]{1,0:T(8,128)S(1)}, u32[]{:S(2)}, u32[]{:S(2)}) collective-permute-start(f32[512,256]{1,0:T(8,128)S(1)} %add.61), channel_id=1, source_target_pairs={{0,2},{1,3},{2,0},{3,1},{4,6},{5,7},{6,4},{7,5},{8,10},{9,11},{10,... | collective-permute-start | bytes 1572872 | tf_op jit(solution)/shard_map/ppermute | solution.py:178
  68.8 3.9 %shard_map.80 = (bf16[64,1792]{1,0:T(8,128)(2,1)S(1)}, bf16[64,1792]{1,0:T(8,128)(2,1)S(1)}, bf16[64,1792]{1,0:T(8,128)(2,1)S(1)}, bf16[64,1792]{1,0:T(8,128)(2,1)S(1)}) custom-call(s32[2]{0:T(128)S(1)} %pad_add_fusion.index_ref, bf16[512,256]{1,0:T(8,128)(2,1)S(1)} %add_convert_fusion.1.own_ref, bf16[512,256]{1,0:T(8,128)(2,1)S(1)} %collective-permute-done.4.other_ref, ...), custom_call_target="tpu_custom_call" | custom-call | flops 939524096 | bytes 3670016 | tf_op jit(solution)/shard_map/pallas_call | solution.py:214
  74.9 10.3 %collective-permute-done.8 = bf16[64,1792]{1,0:T(8,128)(2,1)S(1)} collective-permute-done((bf16[64,1792]{1,0:T(8,128)(2,1)S(1)}, bf16[64,1792]{1,0:T(8,128)(2,1)S(1)}, u32[]{:S(2)}, u32[]{:S(2)}) %collective-permute-start.8) | collective-permute-done | bytes 229408 | tf_op jit(solution)/shard_map/ppermute | solution.py:39
  85.2 2.2 %collective-permute-start.9 = (bf16[64,1792]{1,0:T(8,128)(2,1)S(1)}, bf16[64,1792]{1,0:T(8,128)(2,1)S(1)}, u32[]{:S(2)}, u32[]{:S(2)}) collective-permute-start(bf16[64,1792]{1,0:T(8,128)(2,1)S(1)} %add_convert_fusion.5), channel_id=1, source_target_pairs={{0,8},{1,9},{2,10},{3,11},{4,12},{5,13},{6,14},{7,15},{8,0},{9,1},... | collective-permute-start | bytes 688136 | tf_op jit(solution)/shard_map/ppermute | solution.py:39
  87.7 3.4 %collective-permute-start.14 = (bf16[32,1792]{1,0:T(8,128)(2,1)S(1)}, bf16[32,1792]{1,0:T(8,128)(2,1)S(1)}, u32[]{:S(2)}, u32[]{:S(2)}) collective-permute-start(bf16[32,1792]{1,0:T(8,128)(2,1)S(1)} %add_convert_fusion.8), channel_id=1, source_target_pairs={{0,16},{1,17},{2,18},{3,19},{4,20},{5,21},{6,22},{7,23},{8,24},{9,... | collective-permute-start | bytes 344072 | tf_op jit(solution)/shard_map/ppermute | solution.py:39
  92.6 4.7 %collective-permute-start.10 = (bf16[32,1792]{1,0:T(8,128)(2,1)S(1)}, bf16[32,1792]{1,0:T(8,128)(2,1)S(1)}, u32[]{:S(2)}, u32[]{:S(2)}) collective-permute-start(bf16[32,1792]{1,0:T(8,128)(2,1)S(1)} %add_convert_fusion.9), channel_id=1, source_target_pairs={{0,16},{1,17},{2,18},{3,19},{4,20},{5,21},{6,22},{7,23},{8,24},{9,... | collective-permute-start | bytes 344072 | tf_op jit(solution)/shard_map/ppermute | solution.py:39
  97.3 3.8 %shard_map.85 = (bf16[64,1792]{1,0:T(8,128)(2,1)S(1)}, bf16[64,1792]{1,0:T(8,128)(2,1)S(1)}, bf16[64,1792]{1,0:T(8,128)(2,1)S(1)}, bf16[64,1792]{1,0:T(8,128)(2,1)S(1)}) custom-call(s32[2]{0:T(128)S(1)} %pad_add_fusion.index_ref, bf16[512,256]{1,0:T(8,128)(2,1)S(1)} %add_convert_fusion.own_ref, bf16[512,256]{1,0:T(8,128)(2,1)S(1)} %collective-permute-done.21.other_ref, ...), custom_call_target="tpu_custom_call" | custom-call | flops 939524096 | bytes 3670016 | tf_op jit(solution)/shard_map/pallas_call | solution.py:214
  103.3 3.9 %shard_map.84 = (bf16[64,1792]{1,0:T(8,128)(2,1)S(1)}, bf16[64,1792]{1,0:T(8,128)(2,1)S(1)}, bf16[64,1792]{1,0:T(8,128)(2,1)S(1)}, bf16[64,1792]{1,0:T(8,128)(2,1)S(1)}) custom-call(s32[2]{0:T(128)S(1)} %pad_add_fusion.index_ref, bf16[512,256]{1,0:T(8,128)(2,1)S(1)} %add_convert_fusion.own_ref, bf16[512,256]{1,0:T(8,128)(2,1)S(1)} %collective-permute-done.21.other_ref, ...), custom_call_target="tpu_custom_call" | custom-call | flops 939524096 | bytes 3670016 | tf_op jit(solution)/shard_map/pallas_call | solution.py:214
  111.1 8.4 %collective-permute-done.30 = bf16[32,1792]{1,0:T(8,128)(2,1)S(1)} collective-permute-done((bf16[32,1792]{1,0:T(8,128)(2,1)S(1)}, bf16[32,1792]{1,0:T(8,128)(2,1)S(1)}, u32[]{:S(2)}, u32[]{:S(2)}) %collective-permute-start.30) | collective-permute-done | bytes 114720 | tf_op jit(solution)/shard_map/ppermute | solution.py:39
  119.6 6.4 %collective-permute-done.15 = bf16[32,1792]{1,0:T(8,128)(2,1)S(1)} collective-permute-done((bf16[32,1792]{1,0:T(8,128)(2,1)S(1)}, bf16[32,1792]{1,0:T(8,128)(2,1)S(1)}, u32[]{:S(2)}, u32[]{:S(2)}) %collective-permute-start.15) | collective-permute-done | bytes 114720 | tf_op jit(solution)/shard_map/ppermute | solution.py:39
  127.4 2.1 %collective-permute-start.28 = (bf16[64,1792]{1,0:T(8,128)(2,1)S(1)}, bf16[64,1792]{1,0:T(8,128)(2,1)S(1)}, u32[]{:S(2)}, u32[]{:S(2)}) collective-permute-start(bf16[64,1792]{1,0:T(8,128)(2,1)S(1)} %add_convert_fusion.2), channel_id=1, source_target_pairs={{0,8},{1,9},{2,10},{3,11},{4,12},{5,13},{6,14},{7,15},{8,0},{9,1},... | collective-permute-start | bytes 688136 | tf_op jit(solution)/shard_map/ppermute | solution.py:39
  129.6 9.7 %collective-permute-done.28.refs_2_ = bf16[64,1792]{1,0:T(8,128)(2,1)S(1)} collective-permute-done((bf16[64,1792]{1,0:T(8,128)(2,1)S(1)}, bf16[64,1792]{1,0:T(8,128)(2,1)S(1)}, u32[]{:S(2)}, u32[]{:S(2)}) %collective-permute-start.28) | collective-permute-done | bytes 229408 | tf_op jit(solution)/shard_map/ppermute | solution.py:39
  142.6 4.8 %collective-permute-done.24.refs_2_ = bf16[64,1792]{1,0:T(8,128)(2,1)S(1)} collective-permute-done((bf16[64,1792]{1,0:T(8,128)(2,1)S(1)}, bf16[64,1792]{1,0:T(8,128)(2,1)S(1)}, u32[]{:S(2)}, u32[]{:S(2)}) %collective-permute-start.24) | collective-permute-done | bytes 229408 | tf_op jit(solution)/shard_map/ppermute | solution.py:39
  147.5 3.0 %collective-permute-start.25 = (bf16[32,1792]{1,0:T(8,128)(2,1)S(1)}, bf16[32,1792]{1,0:T(8,128)(2,1)S(1)}, u32[]{:S(2)}, u32[]{:S(2)}) collective-permute-start(bf16[32,1792]{1,0:T(8,128)(2,1)S(1)} %add_convert_fusion.7), channel_id=1, source_target_pairs={{0,16},{1,17},{2,18},{3,19},{4,20},{5,21},{6,22},{7,23},{8,24},{9,... | collective-permute-start | bytes 344072 | tf_op jit(solution)/shard_map/ppermute | solution.py:39
  150.5 5.5 %collective-permute-done.29.refs_3_ = bf16[32,1792]{1,0:T(8,128)(2,1)S(1)} collective-permute-done((bf16[32,1792]{1,0:T(8,128)(2,1)S(1)}, bf16[32,1792]{1,0:T(8,128)(2,1)S(1)}, u32[]{:S(2)}, u32[]{:S(2)}) %collective-permute-start.29) | collective-permute-done | bytes 114720 | tf_op jit(solution)/shard_map/ppermute | solution.py:39
  158.3 2.4 %collective-permute-start.34 = (bf16[32,1792]{1,0:T(8,128)(2,1)S(1)}, bf16[32,1792]{1,0:T(8,128)(2,1)S(1)}, u32[]{:S(2)}, u32[]{:S(2)}) collective-permute-start(bf16[32,1792]{1,0:T(8,128)(2,1)S(1)} %get-tuple-element.63), channel_id=1, source_target_pairs={{0,16},{1,17},{2,18},{3,19},{4,20},{5,21},{6,22},{7,23},{8,24},{9,... | collective-permute-start | bytes 344072 | tf_op jit(solution)/shard_map/ppermute | solution.py:39
  160.7 2.4 %collective-permute-done.38 = bf16[32,1792]{1,0:T(8,128)(2,1)S(1)} collective-permute-done((bf16[32,1792]{1,0:T(8,128)(2,1)S(1)}, bf16[32,1792]{1,0:T(8,128)(2,1)S(1)}, u32[]{:S(2)}, u32[]{:S(2)}) %collective-permute-start.38) | collective-permute-done | bytes 114720 | tf_op jit(solution)/shard_map/ppermute | solution.py:39
  163.2 2.3 %collective-permute-done.34 = bf16[32,1792]{1,0:T(8,128)(2,1)S(1)} collective-permute-done((bf16[32,1792]{1,0:T(8,128)(2,1)S(1)}, bf16[32,1792]{1,0:T(8,128)(2,1)S(1)}, u32[]{:S(2)}, u32[]{:S(2)}) %collective-permute-start.34) | collective-permute-done | bytes 114720 | tf_op jit(solution)/shard_map/ppermute | solution.py:39
  166.4 2.8 %collective-permute-done.39.refs_5_ = bf16[64,1792]{1,0:T(8,128)(2,1)S(1)} collective-permute-done((bf16[64,1792]{1,0:T(8,128)(2,1)S(1)}, bf16[64,1792]{1,0:T(8,128)(2,1)S(1)}, u32[]{:S(2)}, u32[]{:S(2)}) %collective-permute-start.39) | collective-permute-done | bytes 229408 | tf_op jit(solution)/shard_map/ppermute | solution.py:39
  172.3 2.9 %collective-permute-done.41.refs_7_ = bf16[64,1792]{1,0:T(8,128)(2,1)S(1)} collective-permute-done((bf16[64,1792]{1,0:T(8,128)(2,1)S(1)}, bf16[64,1792]{1,0:T(8,128)(2,1)S(1)}, u32[]{:S(2)}, u32[]{:S(2)}) %collective-permute-start.41) | collective-permute-done | bytes 229408 | tf_op jit(solution)/shard_map/ppermute | solution.py:39
  175.2 4.7 %shard_map.88.refs_9_ = bf16[1024,3584]{1,0:T(8,128)(2,1)} custom-call(s32[2]{0:T(128)S(1)} %pad_add_fusion.index_ref, bf16[64,1792]{1,0:T(8,128)(2,1)S(1)} %constant_dynamic-update-slice_fusion.2.refs_0_, bf16[64,1792]{1,0:T(8,128)(2,1)S(1)} %collective-permute-done.31.refs_8_.refs_1_, bf16[64,1792]{1,0:T(8,128)(2,1)S(1)} %collective-permute-done.32.refs_9_.refs_2_, ...), custom_call_target="tpu_custom_call" | custom-call | flops 1879048192 | bytes 3670016 | tf_op jit(solution)/shard_map/pallas_call | solution.py:294
  180.1 4.7 %shard_map.89 = bf16[1024,3584]{1,0:T(8,128)(2,1)} custom-call(s32[2]{0:T(128)S(1)} %pad_add_fusion.index_ref, bf16[64,1792]{1,0:T(8,128)(2,1)S(1)} %constant_dynamic-update-slice_fusion.refs_0_, bf16[64,1792]{1,0:T(8,128)(2,1)S(1)} %collective-permute-done.16.refs_8_.refs_1_, ...), custom_call_target="tpu_custom_call", output_to_operand_aliasing={{}: (10, {})} | custom-call | flops 1879048192 | bytes 3670016 | tf_op jit(solution)/shard_map/pallas_call | solution.py:294
  (97 shorter events, 30.3 us)
Async XLA Ops:
  3.0 10.2 %collective-permute-start.1 = (bf16[1024,256]{1,0:T(8,128)(2,1)S(1)}, bf16[1024,256]{1,0:T(8,128)(2,1)S(1)}, u32[]{:S(2)}, u32[]{:S(2)}) collective-permute-start(bf16[1024,256]{1,0:T(8,128)(2,1)S(1)} %collective-permute-done.refs_0_), channel_id=1, source_target_pairs={{0,4},{1,5},{2,6},{3,7},{4,0},{5,1},{6,2},{7,3},{8,12},{9,13},{10,... | collective-permute-start | bytes 1572872 | tf_op jit(solution)/shard_map/ppermute | solution.py:39
  7.8 24.0 %collective-permute-start.5 = (bf16[1024,256]{1,0:T(8,128)(2,1)S(1)}, bf16[1024,256]{1,0:T(8,128)(2,1)S(1)}, u32[]{:S(2)}, u32[]{:S(2)}) collective-permute-start(bf16[1024,256]{1,0:T(8,128)(2,1)S(1)} %shard_map.78), channel_id=1, source_target_pairs={{0,0},{10,1},{16,2},{26,3},{4,4},{14,5},{20,6},{30,7},{2,8},{8,9},... | collective-permute-start | bytes 1572872 | tf_op jit(solution)/shard_map/ppermute | solution.py:109
  17.8 15.5 %collective-permute-start.2 = (f32[512,256]{1,0:T(8,128)S(1)}, f32[512,256]{1,0:T(8,128)S(1)}, u32[]{:S(2)}, u32[]{:S(2)}) collective-permute-start(f32[512,256]{1,0:T(8,128)S(1)} %get-tuple-element.36), channel_id=1, source_target_pairs={{0,1},{1,0},{2,3},{3,2},{4,5},{5,4},{6,7},{7,6},{8,9},{9,8},{10,11... | collective-permute-start | bytes 1572872 | tf_op jit(solution)/shard_map/ppermute | solution.py:178
  31.8 13.0 %collective-permute-start.6 = (bf16[1024,256]{1,0:T(8,128)(2,1)S(1)}, bf16[1024,256]{1,0:T(8,128)(2,1)S(1)}, u32[]{:S(2)}, u32[]{:S(2)}) collective-permute-start(bf16[1024,256]{1,0:T(8,128)(2,1)S(1)} %collective-permute-done.5.refs_0_), channel_id=1, source_target_pairs={{0,4},{1,5},{2,6},{3,7},{4,0},{5,1},{6,2},{7,3},{8,12},{9,13},{10,... | collective-permute-start | bytes 1572872 | tf_op jit(solution)/shard_map/ppermute | solution.py:39
  33.4 22.3 %collective-permute-start.3 = (f32[512,256]{1,0:T(8,128)S(1)}, f32[512,256]{1,0:T(8,128)S(1)}, u32[]{:S(2)}, u32[]{:S(2)}) collective-permute-start(f32[512,256]{1,0:T(8,128)S(1)} %add.53), channel_id=1, source_target_pairs={{0,2},{1,3},{2,0},{3,1},{4,6},{5,7},{6,4},{7,5},{8,10},{9,11},{10,... | collective-permute-start | bytes 1572872 | tf_op jit(solution)/shard_map/ppermute | solution.py:178
  49.4 13.4 %collective-permute-start.19 = (f32[512,256]{1,0:T(8,128)S(1)}, f32[512,256]{1,0:T(8,128)S(1)}, u32[]{:S(2)}, u32[]{:S(2)}) collective-permute-start(f32[512,256]{1,0:T(8,128)S(1)} %get-tuple-element.37.refs_0_), channel_id=1, source_target_pairs={{0,1},{1,0},{2,3},{3,2},{4,5},{5,4},{6,7},{7,6},{8,9},{9,8},{10,11... | collective-permute-start | bytes 1572872 | tf_op jit(solution)/shard_map/ppermute | solution.py:178
  61.2 13.5 %collective-permute-start.12 = (bf16[64,1792]{1,0:T(8,128)(2,1)S(1)}, bf16[64,1792]{1,0:T(8,128)(2,1)S(1)}, u32[]{:S(2)}, u32[]{:S(2)}) collective-permute-start(bf16[64,1792]{1,0:T(8,128)(2,1)S(1)} %get-tuple-element.45), channel_id=1, source_target_pairs={{0,4},{1,5},{2,6},{3,7},{4,0},{5,1},{6,2},{7,3},{8,12},{9,13},{10,... | collective-permute-start | bytes 688136 | tf_op jit(solution)/shard_map/ppermute | solution.py:39
  62.9 24.6 %collective-permute-start.20 = (f32[512,256]{1,0:T(8,128)S(1)}, f32[512,256]{1,0:T(8,128)S(1)}, u32[]{:S(2)}, u32[]{:S(2)}) collective-permute-start(f32[512,256]{1,0:T(8,128)S(1)} %add.61), channel_id=1, source_target_pairs={{0,2},{1,3},{2,0},{3,1},{4,6},{5,7},{6,4},{7,5},{8,10},{9,11},{10,... | collective-permute-start | bytes 1572872 | tf_op jit(solution)/shard_map/ppermute | solution.py:178
  68.3 19.4 %collective-permute-start.11 = (bf16[64,1792]{1,0:T(8,128)(2,1)S(1)}, bf16[64,1792]{1,0:T(8,128)(2,1)S(1)}, u32[]{:S(2)}, u32[]{:S(2)}) collective-permute-start(bf16[64,1792]{1,0:T(8,128)(2,1)S(1)} %get-tuple-element.43), channel_id=1, source_target_pairs={{0,4},{1,5},{2,6},{3,7},{4,0},{5,1},{6,2},{7,3},{8,12},{9,13},{10,... | collective-permute-start | bytes 688136 | tf_op jit(solution)/shard_map/ppermute | solution.py:39
  72.7 18.5 %collective-permute-start.7 = (bf16[64,1792]{1,0:T(8,128)(2,1)S(1)}, bf16[64,1792]{1,0:T(8,128)(2,1)S(1)}, u32[]{:S(2)}, u32[]{:S(2)}) collective-permute-start(bf16[64,1792]{1,0:T(8,128)(2,1)S(1)} %get-tuple-element.39), channel_id=1, source_target_pairs={{0,4},{1,5},{2,6},{3,7},{4,0},{5,1},{6,2},{7,3},{8,12},{9,13},{10,... | collective-permute-start | bytes 688136 | tf_op jit(solution)/shard_map/ppermute | solution.py:39
  74.2 11.0 %collective-permute-start.8 = (bf16[64,1792]{1,0:T(8,128)(2,1)S(1)}, bf16[64,1792]{1,0:T(8,128)(2,1)S(1)}, u32[]{:S(2)}, u32[]{:S(2)}) collective-permute-start(bf16[64,1792]{1,0:T(8,128)(2,1)S(1)} %get-tuple-element.41), channel_id=1, source_target_pairs={{0,4},{1,5},{2,6},{3,7},{4,0},{5,1},{6,2},{7,3},{8,12},{9,13},{10,... | collective-permute-start | bytes 688136 | tf_op jit(solution)/shard_map/ppermute | solution.py:39
  74.8 12.8 %collective-permute-start.13 = (bf16[64,1792]{1,0:T(8,128)(2,1)S(1)}, bf16[64,1792]{1,0:T(8,128)(2,1)S(1)}, u32[]{:S(2)}, u32[]{:S(2)}) collective-permute-start(bf16[64,1792]{1,0:T(8,128)(2,1)S(1)} %add_convert_fusion.4), channel_id=1, source_target_pairs={{0,8},{1,9},{2,10},{3,11},{4,12},{5,13},{6,14},{7,15},{8,0},{9,1},... | collective-permute-start | bytes 688136 | tf_op jit(solution)/shard_map/ppermute | solution.py:39
  87.6 9.7 %collective-permute-start.21 = (bf16[512,256]{1,0:T(8,128)(2,1)S(1)}, bf16[512,256]{1,0:T(8,128)(2,1)S(1)}, u32[]{:S(2)}, u32[]{:S(2)}) collective-permute-start(bf16[512,256]{1,0:T(8,128)(2,1)S(1)} %add_convert_fusion.own_ref), channel_id=1, source_target_pairs={{0,1},{1,0},{2,3},{3,2},{4,5},{5,4},{6,7},{7,6},{8,9},{9,8},{10,11... | collective-permute-start | bytes 786440 | tf_op jit(solution)/shard_map/ppermute | solution.py:178
  87.7 20.8 %collective-permute-start.14 = (bf16[32,1792]{1,0:T(8,128)(2,1)S(1)}, bf16[32,1792]{1,0:T(8,128)(2,1)S(1)}, u32[]{:S(2)}, u32[]{:S(2)}) collective-permute-start(bf16[32,1792]{1,0:T(8,128)(2,1)S(1)} %add_convert_fusion.8), channel_id=1, source_target_pairs={{0,16},{1,17},{2,18},{3,19},{4,20},{5,21},{6,22},{7,23},{8,24},{9,... | collective-permute-start | bytes 344072 | tf_op jit(solution)/shard_map/ppermute | solution.py:39
  92.6 17.5 %collective-permute-start.10 = (bf16[32,1792]{1,0:T(8,128)(2,1)S(1)}, bf16[32,1792]{1,0:T(8,128)(2,1)S(1)}, u32[]{:S(2)}, u32[]{:S(2)}) collective-permute-start(bf16[32,1792]{1,0:T(8,128)(2,1)S(1)} %add_convert_fusion.9), channel_id=1, source_target_pairs={{0,16},{1,17},{2,18},{3,19},{4,20},{5,21},{6,22},{7,23},{8,24},{9,... | collective-permute-start | bytes 344072 | tf_op jit(solution)/shard_map/ppermute | solution.py:39
  101.2 28.4 %collective-permute-start.26 = (bf16[64,1792]{1,0:T(8,128)(2,1)S(1)}, bf16[64,1792]{1,0:T(8,128)(2,1)S(1)}, u32[]{:S(2)}, u32[]{:S(2)}) collective-permute-start(bf16[64,1792]{1,0:T(8,128)(2,1)S(1)} %get-tuple-element.55), channel_id=1, source_target_pairs={{0,4},{1,5},{2,6},{3,7},{4,0},{5,1},{6,2},{7,3},{8,12},{9,13},{10,... | collective-permute-start | bytes 688136 | tf_op jit(solution)/shard_map/ppermute | solution.py:39
  102.5 24.7 %collective-permute-start.27 = (bf16[64,1792]{1,0:T(8,128)(2,1)S(1)}, bf16[64,1792]{1,0:T(8,128)(2,1)S(1)}, u32[]{:S(2)}, u32[]{:S(2)}) collective-permute-start(bf16[64,1792]{1,0:T(8,128)(2,1)S(1)} %get-tuple-element.57), channel_id=1, source_target_pairs={{0,4},{1,5},{2,6},{3,7},{4,0},{5,1},{6,2},{7,3},{8,12},{9,13},{10,... | collective-permute-start | bytes 688136 | tf_op jit(solution)/shard_map/ppermute | solution.py:39
  107.1 32.3 %collective-permute-start.22 = (bf16[64,1792]{1,0:T(8,128)(2,1)S(1)}, bf16[64,1792]{1,0:T(8,128)(2,1)S(1)}, u32[]{:S(2)}, u32[]{:S(2)}) collective-permute-start(bf16[64,1792]{1,0:T(8,128)(2,1)S(1)} %get-tuple-element.51), channel_id=1, source_target_pairs={{0,4},{1,5},{2,6},{3,7},{4,0},{5,1},{6,2},{7,3},{8,12},{9,13},{10,... | collective-permute-start | bytes 688136 | tf_op jit(solution)/shard_map/ppermute | solution.py:39
  108.5 18.9 %collective-permute-start.23 = (bf16[64,1792]{1,0:T(8,128)(2,1)S(1)}, bf16[64,1792]{1,0:T(8,128)(2,1)S(1)}, u32[]{:S(2)}, u32[]{:S(2)}) collective-permute-start(bf16[64,1792]{1,0:T(8,128)(2,1)S(1)} %get-tuple-element.53), channel_id=1, source_target_pairs={{0,4},{1,5},{2,6},{3,7},{4,0},{5,1},{6,2},{7,3},{8,12},{9,13},{10,... | collective-permute-start | bytes 688136 | tf_op jit(solution)/shard_map/ppermute | solution.py:39
  110.1 9.4 %collective-permute-start.30 = (bf16[32,1792]{1,0:T(8,128)(2,1)S(1)}, bf16[32,1792]{1,0:T(8,128)(2,1)S(1)}, u32[]{:S(2)}, u32[]{:S(2)}) collective-permute-start(bf16[32,1792]{1,0:T(8,128)(2,1)S(1)} %get-tuple-element.60), channel_id=1, source_target_pairs={{0,16},{1,17},{2,18},{3,19},{4,20},{5,21},{6,22},{7,23},{8,24},{9,... | collective-permute-start | bytes 344072 | tf_op jit(solution)/shard_map/ppermute | solution.py:39
  125.9 21.5 %collective-permute-start.32 = (bf16[64,1792]{1,0:T(8,128)(2,1)S(1)}, bf16[64,1792]{1,0:T(8,128)(2,1)S(1)}, u32[]{:S(2)}, u32[]{:S(2)}) collective-permute-start(bf16[64,1792]{1,0:T(8,128)(2,1)S(1)} %constant_dynamic-update-slice_fusion.2.refs_0_), channel_id=1, source_target_pairs={{0,4},{1,5},{2,6},{3,7},{4,0},{5,1},{6,2},{7,3},{8,12},{9,13},{10,... | collective-permute-start | bytes 688136 | tf_op jit(solution)/shard_map/ppermute | solution.py:39
  127.2 13.3 %collective-permute-start.31 = (bf16[64,1792]{1,0:T(8,128)(2,1)S(1)}, bf16[64,1792]{1,0:T(8,128)(2,1)S(1)}, u32[]{:S(2)}, u32[]{:S(2)}) collective-permute-start(bf16[64,1792]{1,0:T(8,128)(2,1)S(1)} %constant_dynamic-update-slice_fusion.2.refs_0_), channel_id=1, source_target_pairs={{0,8},{1,9},{2,10},{3,11},{4,12},{5,13},{6,14},{7,15},{8,0},{9,1},... | collective-permute-start | bytes 688136 | tf_op jit(solution)/shard_map/ppermute | solution.py:39
  127.4 12.0 %collective-permute-start.28 = (bf16[64,1792]{1,0:T(8,128)(2,1)S(1)}, bf16[64,1792]{1,0:T(8,128)(2,1)S(1)}, u32[]{:S(2)}, u32[]{:S(2)}) collective-permute-start(bf16[64,1792]{1,0:T(8,128)(2,1)S(1)} %add_convert_fusion.2), channel_id=1, source_target_pairs={{0,8},{1,9},{2,10},{3,11},{4,12},{5,13},{6,14},{7,15},{8,0},{9,1},... | collective-permute-start | bytes 688136 | tf_op jit(solution)/shard_map/ppermute | solution.py:39
  129.5 12.3 %collective-permute-start.16 = (bf16[64,1792]{1,0:T(8,128)(2,1)S(1)}, bf16[64,1792]{1,0:T(8,128)(2,1)S(1)}, u32[]{:S(2)}, u32[]{:S(2)}) collective-permute-start(bf16[64,1792]{1,0:T(8,128)(2,1)S(1)} %constant_dynamic-update-slice_fusion.refs_0_), channel_id=1, source_target_pairs={{0,8},{1,9},{2,10},{3,11},{4,12},{5,13},{6,14},{7,15},{8,0},{9,1},... | collective-permute-start | bytes 688136 | tf_op jit(solution)/shard_map/ppermute | solution.py:39
  139.3 8.1 %collective-permute-start.24 = (bf16[64,1792]{1,0:T(8,128)(2,1)S(1)}, bf16[64,1792]{1,0:T(8,128)(2,1)S(1)}, u32[]{:S(2)}, u32[]{:S(2)}) collective-permute-start(bf16[64,1792]{1,0:T(8,128)(2,1)S(1)} %add_convert_fusion.3), channel_id=1, source_target_pairs={{0,8},{1,9},{2,10},{3,11},{4,12},{5,13},{6,14},{7,15},{8,0},{9,1},... | collective-permute-start | bytes 688136 | tf_op jit(solution)/shard_map/ppermute | solution.py:39
  139.4 17.4 %collective-permute-start.17 = (bf16[64,1792]{1,0:T(8,128)(2,1)S(1)}, bf16[64,1792]{1,0:T(8,128)(2,1)S(1)}, u32[]{:S(2)}, u32[]{:S(2)}) collective-permute-start(bf16[64,1792]{1,0:T(8,128)(2,1)S(1)} %constant_dynamic-update-slice_fusion.refs_0_), channel_id=1, source_target_pairs={{0,4},{1,5},{2,6},{3,7},{4,0},{5,1},{6,2},{7,3},{8,12},{9,13},{10,... | collective-permute-start | bytes 688136 | tf_op jit(solution)/shard_map/ppermute | solution.py:39
  140.5 15.4 %collective-permute-start.33 = (bf16[64,1792]{1,0:T(8,128)(2,1)S(1)}, bf16[64,1792]{1,0:T(8,128)(2,1)S(1)}, u32[]{:S(2)}, u32[]{:S(2)}) collective-permute-start(bf16[64,1792]{1,0:T(8,128)(2,1)S(1)} %collective-permute-done.31.refs_8_.refs_1_), channel_id=1, source_target_pairs={{0,4},{1,5},{2,6},{3,7},{4,0},{5,1},{6,2},{7,3},{8,12},{9,13},{10,... | collective-permute-start | bytes 688136 | tf_op jit(solution)/shard_map/ppermute | solution.py:39
  141.8 15.6 %collective-permute-start.18 = (bf16[64,1792]{1,0:T(8,128)(2,1)S(1)}, bf16[64,1792]{1,0:T(8,128)(2,1)S(1)}, u32[]{:S(2)}, u32[]{:S(2)}) collective-permute-start(bf16[64,1792]{1,0:T(8,128)(2,1)S(1)} %collective-permute-done.16.refs_8_.refs_1_), channel_id=1, source_target_pairs={{0,4},{1,5},{2,6},{3,7},{4,0},{5,1},{6,2},{7,3},{8,12},{9,13},{10,... | collective-permute-start | bytes 688136 | tf_op jit(solution)/shard_map/ppermute | solution.py:39
  147.4 8.5 %collective-permute-start.29 = (bf16[32,1792]{1,0:T(8,128)(2,1)S(1)}, bf16[32,1792]{1,0:T(8,128)(2,1)S(1)}, u32[]{:S(2)}, u32[]{:S(2)}) collective-permute-start(bf16[32,1792]{1,0:T(8,128)(2,1)S(1)} %add_convert_fusion.6), channel_id=1, source_target_pairs={{0,16},{1,17},{2,18},{3,19},{4,20},{5,21},{6,22},{7,23},{8,24},{9,... | collective-permute-start | bytes 344072 | tf_op jit(solution)/shard_map/ppermute | solution.py:39
  147.5 9.9 %collective-permute-start.25 = (bf16[32,1792]{1,0:T(8,128)(2,1)S(1)}, bf16[32,1792]{1,0:T(8,128)(2,1)S(1)}, u32[]{:S(2)}, u32[]{:S(2)}) collective-permute-start(bf16[32,1792]{1,0:T(8,128)(2,1)S(1)} %add_convert_fusion.7), channel_id=1, source_target_pairs={{0,16},{1,17},{2,18},{3,19},{4,20},{5,21},{6,22},{7,23},{8,24},{9,... | collective-permute-start | bytes 344072 | tf_op jit(solution)/shard_map/ppermute | solution.py:39
  169.9 10.0 %collective-permute-start.36 = (bf16[64,1792]{1,0:T(8,128)(2,1)S(1)}, bf16[64,1792]{1,0:T(8,128)(2,1)S(1)}, u32[]{:S(2)}, u32[]{:S(2)}) collective-permute-start(bf16[64,1792]{1,0:T(8,128)(2,1)S(1)} %constant_dynamic-update-slice_fusion.4.refs_4_), channel_id=1, source_target_pairs={{0,4},{1,5},{2,6},{3,7},{4,0},{5,1},{6,2},{7,3},{8,12},{9,13},{10,... | collective-permute-start | bytes 688136 | tf_op jit(solution)/shard_map/ppermute | solution.py:39
  171.6 8.5 %collective-permute-start.37 = (bf16[64,1792]{1,0:T(8,128)(2,1)S(1)}, bf16[64,1792]{1,0:T(8,128)(2,1)S(1)}, u32[]{:S(2)}, u32[]{:S(2)}) collective-permute-start(bf16[64,1792]{1,0:T(8,128)(2,1)S(1)} %collective-permute-done.35.refs_5_), channel_id=1, source_target_pairs={{0,4},{1,5},{2,6},{3,7},{4,0},{5,1},{6,2},{7,3},{8,12},{9,13},{10,... | collective-permute-start | bytes 688136 | tf_op jit(solution)/shard_map/ppermute | solution.py:39
  (15 other events, 154.1 us)

commit v3 on v2

--- a/solution.py
+++ b/solution.py
@@ -29,43 +29,59 @@
     return columns
 
 
+def add_after(one, other, wait_for):
+    def kernel(one_ref, other_ref, *refs):
+        refs[-1][...] = (one_ref[...].astype(F32) + other_ref[...].astype(F32)).astype(BF16)
+
+    return pl.pallas_call(
+        kernel,
+        in_specs=[pl.BlockSpec(one.shape)] * 2 + [ANYWHERE] * len(wait_for),
+        out_shape=jax.ShapeDtypeStruct(one.shape, BF16),
+        compiler_params=pltpu.CompilerParams(vmem_limit_bytes=VMEM_LIMIT),
+    )(one, other, *wait_for)
+
+
 class Cube:
     def __init__(self, dp, mp):
         self.dp, self.mp = dp, mp
-        self.order = [1 << j for j in range(dp.bit_length() - 1)]
+        bits = [1 << j for j in range(dp.bit_length() - 1)]
+        self.pair_first = bits
+        self.pair_last = bits[1:] + bits[:1]
+        self.pair_mid = bits[1:2] + bits[:1] + bits[2:]
 
     def swap(self, value, bit):
         pairs = [(d * self.mp + m, (d ^ bit) * self.mp + m) for d in range(self.dp) for m in range(self.mp)]
         return lax.ppermute(value, AXES, pairs)
 
-    def sum_order(self):
-        k = len(self.order)
-        return [
-            sum(bit for j, bit in enumerate(self.order) if not (p >> (k - 1 - j)) & 1) for p in range(self.dp)
-        ]
-
-    def gather_order(self):
-        later = self.order[:1:-1]
+    def sum_order(self, order):
+        k = len(order)
+        return [sum(bit for j, bit in enumerate(order) if not (p >> (k - 1 - j)) & 1) for p in range(self.dp)]
+
+    def gather_order(self, order):
+        later = order[:1:-1]
         base = [sum(bit for j, bit in enumerate(later) if (i >> j) & 1) for i in range(1 << len(later))]
-        first, second = self.order[:2]
+        first, second = order[:2]
         return [[r | extra for r in base] for extra in (0, second, first, first | second)]
 
-    def sum_up(self, quarters):
+    def sum_up(self, quarters, order, wait_for):
         sent_first, sent_last, next_out, kept = quarters
-        first, second = self.order[:2]
+        first, second = order[:2]
         got_first, got_last = self.swap(sent_first, first), self.swap(sent_last, first)
-        out = (next_out.astype(F32) + got_first.astype(F32)).astype(BF16)
+        if wait_for:
+            out = add_after(next_out, got_first, wait_for)
+        else:
+            out = (next_out.astype(F32) + got_first.astype(F32)).astype(BF16)
         terms = [(kept, 0), (got_last, 0), (self.swap(out, second), 0)]
         rows = kept.shape[0]
-        for bit in self.order[2:]:
+        for bit in order[2:]:
             rows //= 2
             out = sum(t[at : at + rows].astype(F32) for t, at in terms).astype(BF16)
             terms = [(t, at + rows) for t, at in terms] + [(self.swap(out, bit), 0)]
         return terms
 
-    def gather(self, own):
-        first, second = self.order[:2]
-        for bit in self.order[:1:-1]:
+    def gather(self, own, order):
+        first, second = order[:2]
+        for bit in order[:1:-1]:
             own = jnp.concatenate([own, self.swap(own, bit)])
         across = self.swap(own, second)
         return [own, across, self.swap(own, first), self.swap(across, first)]
@@ -185,13 +201,13 @@
     return own, move(own, 1, 0)
 
 
-def grad_rows(cube, index, pieces, out_grads, first_column, columns, wait_for):
+def grad_rows(cube, index, pieces, out_grads, order, first_column, columns, wait_for):
     tokens = out_grads.shape[0]
     ranks = pieces[0].shape[1]
     rows = ranks // cube.dp
     quarter = ranks // 4
     tile = tile_of(columns)
-    order = cube.sum_order()
+    relatives = cube.sum_order(order)
 
     def kernel(index_ref, own_ref, other_ref, grads_ref, *refs):
         outs, (held, turned, picked) = refs[-7:-3], refs[-3:]
@@ -203,7 +219,7 @@
             held[pl.ds(pl.multiple_of(core * half, half), half), :] = own_ref[...]
             held[pl.ds(pl.multiple_of((1 - core) * half, half), half), :] = other_ref[...]
             turned[...] = held[...].T
-            for p, relative in enumerate(order):
+            for p, relative in enumerate(relatives):
                 start = pl.multiple_of((here ^ relative) * rows, rows)
                 picked[p * rows : (p + 1) * rows, :] = turned[pl.ds(start, rows), :]
 
@@ -271,7 +287,7 @@
     )(*(t for t, _ in terms), first_moment, second_moment, *before, *wait_for)
 
 
-def make_update(cube, index, groups, basis, first_column, width, before):
+def make_update(cube, index, groups, orders, basis, first_column, width, before):
     rows, ranks = basis.shape
     parts = len(groups)
     columns = groups[0][0].shape[1]
@@ -279,13 +295,13 @@
     sub = share // parts
     tile = tile_of(columns)
     blocks = [b for group in groups for b in group]
-    order = cube.gather_order()
+    places = [cube.gather_order(order) for order in orders]
 
     def kernel(index_ref, *refs):
         pieces, basis_ref, (out_ref, held) = refs[: len(blocks)], refs[len(blocks)], refs[-2:]
         here = index_ref[0]
         for part in range(parts):
-            for j, relatives in enumerate(order):
+            for j, relatives in enumerate(places[part]):
                 for i, relative in enumerate(relatives):
                     start = pl.multiple_of((here ^ relative) * share + part * sub, sub)
                     held[pl.ds(start, sub), :] = pieces[part * 4 + j][i * sub : (i + 1) * sub, :]
@@ -328,20 +344,31 @@
         for h in range(parts):
             blocks = here[h] + [cube.swap(value, 1) for value in here[h]]
             partial.append(project(cube, index, blocks, activations, []))
-        groups, moments, update = [[None] * parts for _ in range(HALVES)], [], []
-        terms = []
-        for h in range(parts):
-            projected = sum_columns(cube, *partial[h])
+        sums, quarters, groups, moments, update = {}, {}, [[None] * parts for _ in range(HALVES)], [], []
+        projected = [sum_columns(cube, *value) for value in partial]
+        sum_orders = [cube.pair_mid, cube.pair_first] if parts > 1 else [cube.pair_first]
+        gather_orders = [cube.pair_first, cube.pair_first] if parts > 1 else [cube.pair_first]
+        for h in range(parts):
             for f in range(HALVES):
-                wait_for = [partial[h + 1][0]] if h + 1 < parts else []
-                quarters = grad_rows(cube, index, projected, out_grads, f * columns, columns, wait_for)
-                terms.append((h, f, cube.sum_up(quarters)))
-        for h, f, sums in terms:
-            wait_for = groups[f][h - 1][1:] if h else []
-            direction, *moments = adam(cube, sums, first_moment, second_moment, h, f * columns, moments, wait_for)
-            groups[f][h] = cube.gather(direction)
+                wait_for = []
+                if h + 1 < parts:
+                    wait_for = [partial[h + 1][0]]
+                quarters[h, f] = grad_rows(
+                    cube, index, projected[h], out_grads, sum_orders[h], f * columns, columns, wait_for
+                )
+        for h in range(parts):
+            for f in range(HALVES):
+                wait_for = [quarters[h + 1, g][0] for g in range(HALVES)] if h + 1 < parts and f else []
+                sums[h, f] = cube.sum_up(quarters[h, f], sum_orders[h], wait_for)
+        for h in range(parts):
+            for f in range(HALVES):
+                wait_for = groups[f][h - 1][1:] if h else []
+                direction, *moments = adam(
+                    cube, sums[h, f], first_moment, second_moment, h, f * columns, moments, wait_for
+                )
+                groups[f][h] = cube.gather(direction, gather_orders[h])
         for f in range(HALVES):
-            update = [make_update(cube, index, groups[f], basis, f * columns, width, update)]
+            update = [make_update(cube, index, groups[f], gather_orders, basis, f * columns, width, update)]
         return (*update, *moments)
 
     return jax.shard_map(

time: 185 us -> 175 us (0.946)
  waiting for transfers between devices: 67.1 us -> 52.3 us
  starting transfers between devices: 75.2 us -> 80.1 us
    ppermute x34, waiting for transfers between devices: 63.1 us -> 45.7 us  [swap(): return lax.ppermute(value, AXES, pairs)]
    ppermute x34, starting transfers between devices: 38.5 us -> 47.1 us  [swap(): return lax.ppermute(value, AXES, pairs)]
    ppermute x6, starting transfers between devices: 35.3 us -> 31.6 us  [move(): return lax.ppermute(value, AXES, pairs)]
    ppermute x6, waiting for transfers between devices: 3.92 us -> 6.55 us  [move(): return lax.ppermute(value, AXES, pairs)]
  transfers between devices with their start and end apart: 42 -> 42, of which waited for: 19 -> 18; matrix products, arithmetic and copies ran while one was open for 0% -> 0% of each run, Pallas kernels for 18% -> 19%
where the time goes in v3:
time: 175 us
  starting transfers between devices  80.1 us (46%)
  waiting for transfers between devices  52.3 us (30%)
  Pallas kernels  38.4 us (22%)
  local copies, waits for them, and re-layouts  2.53 us (1%)
    ppermute x34, starting transfers between devices, swap(): return lax.ppermute(value, AXES, pairs)  47.1 us
    ppermute x34, waiting for transfers between devices, swap(): return lax.ppermute(value, AXES, pairs)  45.7 us
    ppermute x6, starting transfers between devices, move(): return lax.ppermute(value, AXES, pairs)  31.6 us
    pallas_call x4, Pallas kernels, grad_rows(): pl.pallas_call(kernel, grid_spec=pltpu.PrefetchScalarGridSpec(num_scalar_...  15.4 us
    pallas_call x2, Pallas kernels, make_update(): pl.pallas_call(kernel, grid_spec=pltpu.PrefetchScalarGridSpec(num_scalar_...  9.33 us
    pallas_call x2, Pallas kernels, project(): pl.pallas_call(kernel, grid_spec=pltpu.PrefetchScalarGridSpec(num_scalar_...  9.14 us
    ppermute x6, waiting for transfers between devices, move(): return lax.ppermute(value, AXES, pairs)  6.55 us
    pallas_call x4, Pallas kernels, adam(): pl.pallas_call(kernel, grid=(1,), in_specs=term_specs + [moment_spec] * 2...  3.56 us
  transfers between devices with their start and end apart: 42, of which 18 were waited for; matrix products, arithmetic and copies ran while one was open for 0% of the time, Pallas kernels for 19%

profile of v3, /device:TPU:0, one launch (start us, length us, event | category | flops | bytes accessed | tf_op | source)
XLA Modules:
  0.0 175.0 jit_solution(10297762553996526386)
XLA Ops:
  3.0 3.0 %collective-permute-start.1 = (bf16[1024,256]{1,0:T(8,128)(2,1)S(1)}, bf16[1024,256]{1,0:T(8,128)(2,1)S(1)}, u32[]{:S(2)}, u32[]{:S(2)}) collective-permute-start(bf16[1024,256]{1,0:T(8,128)(2,1)S(1)} %collective-permute-done.refs_0_), channel_id=1, source_target_pairs={{0,4},{1,5},{2,6},{3,7},{4,0},{5,1},{6,2},{7,3},{8,12},{9,13},{10,... | collective-permute-start | bytes 1572872 | tf_op jit(solution)/shard_map/ppermute | solution.py:54
  8.5 4.7 %collective-permute-done.1.refs_1_ = bf16[1024,256]{1,0:T(8,128)(2,1)S(1)} collective-permute-done((bf16[1024,256]{1,0:T(8,128)(2,1)S(1)}, bf16[1024,256]{1,0:T(8,128)(2,1)S(1)}, u32[]{:S(2)}, u32[]{:S(2)}) %collective-permute-start.1) | collective-permute-done | bytes 524320 | tf_op jit(solution)/shard_map/ppermute | solution.py:54
  13.2 4.6 %shard_map.77 = (f32[512,256]{1,0:T(8,128)S(1)}, f32[512,256]{1,0:T(8,128)S(1)}) custom-call(s32[2]{0:T(128)S(1)} %pad_add_fusion.index_ref, bf16[1024,256]{1,0:T(8,128)(2,1)S(1)} %collective-permute-done.refs_0_, bf16[1024,256]{1,0:T(8,128)(2,1)S(1)} %collective-permute-done.1.refs_1_, bf16[1024,2048]{1,0:T(8,128)(2,1)} %refs_2_.3), custom_call_target="tpu_custom_call" | custom-call | flops 1073741824 | bytes 4194304 | tf_op jit(solution)/shard_map/pallas_call | solution.py:162
  17.8 14.0 %collective-permute-start.2 = (f32[512,256]{1,0:T(8,128)S(1)}, f32[512,256]{1,0:T(8,128)S(1)}, u32[]{:S(2)}, u32[]{:S(2)}) collective-permute-start(f32[512,256]{1,0:T(8,128)S(1)} %get-tuple-element.36), channel_id=1, source_target_pairs={{0,1},{1,0},{2,3},{3,2},{4,5},{5,4},{6,7},{7,6},{8,9},{9,8},{10,11... | collective-permute-start | bytes 1572872 | tf_op jit(solution)/shard_map/ppermute | solution.py:194
  33.4 11.4 %collective-permute-start.3 = (f32[512,256]{1,0:T(8,128)S(1)}, f32[512,256]{1,0:T(8,128)S(1)}, u32[]{:S(2)}, u32[]{:S(2)}) collective-permute-start(f32[512,256]{1,0:T(8,128)S(1)} %add.50), channel_id=1, source_target_pairs={{0,2},{1,3},{2,0},{3,1},{4,6},{5,7},{6,4},{7,5},{8,10},{9,11},{10,... | collective-permute-start | bytes 1572872 | tf_op jit(solution)/shard_map/ppermute | solution.py:194
  44.8 4.6 %shard_map.79 = (f32[512,256]{1,0:T(8,128)S(1)}, f32[512,256]{1,0:T(8,128)S(1)}) custom-call(s32[2]{0:T(128)S(1)} %pad_add_fusion.index_ref, bf16[1024,256]{1,0:T(8,128)(2,1)S(1)} %collective-permute-done.5.refs_0_, bf16[1024,256]{1,0:T(8,128)(2,1)S(1)} %collective-permute-done.6.refs_1_, bf16[1024,2048]{1,0:T(8,128)(2,1)} %refs_2_.3), custom_call_target="tpu_custom_call" | custom-call | flops 1073741824 | bytes 4194304 | tf_op jit(solution)/shard_map/pallas_call | solution.py:162
  49.4 4.3 %collective-permute-start.9 = (f32[512,256]{1,0:T(8,128)S(1)}, f32[512,256]{1,0:T(8,128)S(1)}, u32[]{:S(2)}, u32[]{:S(2)}) collective-permute-start(f32[512,256]{1,0:T(8,128)S(1)} %get-tuple-element.37.refs_0_), channel_id=1, source_target_pairs={{0,1},{1,0},{2,3},{3,2},{4,5},{5,4},{6,7},{7,6},{8,9},{9,8},{10,11... | collective-permute-start | bytes 1572872 | tf_op jit(solution)/shard_map/ppermute | solution.py:194
  53.7 2.0 %collective-permute-done.3 = f32[512,256]{1,0:T(8,128)S(1)} collective-permute-done((f32[512,256]{1,0:T(8,128)S(1)}, f32[512,256]{1,0:T(8,128)S(1)}, u32[]{:S(2)}, u32[]{:S(2)}) %collective-permute-start.3) | collective-permute-done | bytes 524320 | tf_op jit(solution)/shard_map/ppermute | solution.py:194
  57.4 3.8 %shard_map.84 = (bf16[64,1792]{1,0:T(8,128)(2,1)S(1)}, bf16[64,1792]{1,0:T(8,128)(2,1)S(1)}, bf16[64,1792]{1,0:T(8,128)(2,1)S(1)}, bf16[64,1792]{1,0:T(8,128)(2,1)S(1)}) custom-call(s32[2]{0:T(128)S(1)} %pad_add_fusion.index_ref, bf16[512,256]{1,0:T(8,128)(2,1)S(1)} %add_convert_fusion.1.own_ref, bf16[512,256]{1,0:T(8,128)(2,1)S(1)} %collective-permute-done.4.other_ref, ...), custom_call_target="tpu_custom_call" | custom-call | flops 939524096 | bytes 3670016 | tf_op jit(solution)/shard_map/pallas_call | solution.py:230
  61.2 3.7 %collective-permute-start.15 = (bf16[64,1792]{1,0:T(8,128)(2,1)S(1)}, bf16[64,1792]{1,0:T(8,128)(2,1)S(1)}, u32[]{:S(2)}, u32[]{:S(2)}) collective-permute-start(bf16[64,1792]{1,0:T(8,128)(2,1)S(1)} %get-tuple-element.48), channel_id=1, source_target_pairs={{0,8},{1,9},{2,10},{3,11},{4,12},{5,13},{6,14},{7,15},{8,0},{9,1},... | collective-permute-start | bytes 688136 | tf_op jit(solution)/shard_map/ppermute | solution.py:54
  66.8 2.0 %collective-permute-start.14 = (bf16[64,1792]{1,0:T(8,128)(2,1)S(1)}, bf16[64,1792]{1,0:T(8,128)(2,1)S(1)}, u32[]{:S(2)}, u32[]{:S(2)}) collective-permute-start(bf16[64,1792]{1,0:T(8,128)(2,1)S(1)} %get-tuple-element.46), channel_id=1, source_target_pairs={{0,8},{1,9},{2,10},{3,11},{4,12},{5,13},{6,14},{7,15},{8,0},{9,1},... | collective-permute-start | bytes 688136 | tf_op jit(solution)/shard_map/ppermute | solution.py:54
  68.8 3.9 %shard_map.80 = (bf16[64,1792]{1,0:T(8,128)(2,1)S(1)}, bf16[64,1792]{1,0:T(8,128)(2,1)S(1)}, bf16[64,1792]{1,0:T(8,128)(2,1)S(1)}, bf16[64,1792]{1,0:T(8,128)(2,1)S(1)}) custom-call(s32[2]{0:T(128)S(1)} %pad_add_fusion.index_ref, bf16[512,256]{1,0:T(8,128)(2,1)S(1)} %add_convert_fusion.1.own_ref, bf16[512,256]{1,0:T(8,128)(2,1)S(1)} %collective-permute-done.4.other_ref, ...), custom_call_target="tpu_custom_call" | custom-call | flops 939524096 | bytes 3670016 | tf_op jit(solution)/shard_map/pallas_call | solution.py:230
  72.8 2.0 %collective-permute-start.8 = (bf16[64,1792]{1,0:T(8,128)(2,1)S(1)}, bf16[64,1792]{1,0:T(8,128)(2,1)S(1)}, u32[]{:S(2)}, u32[]{:S(2)}) collective-permute-start(bf16[64,1792]{1,0:T(8,128)(2,1)S(1)} %get-tuple-element.41), channel_id=1, source_target_pairs={{0,8},{1,9},{2,10},{3,11},{4,12},{5,13},{6,14},{7,15},{8,0},{9,1},... | collective-permute-start | bytes 688136 | tf_op jit(solution)/shard_map/ppermute | solution.py:54
  76.4 2.6 %collective-permute-done.10 = f32[512,256]{1,0:T(8,128)S(1)} collective-permute-done((f32[512,256]{1,0:T(8,128)S(1)}, f32[512,256]{1,0:T(8,128)S(1)}, u32[]{:S(2)}, u32[]{:S(2)}) %collective-permute-start.10) | collective-permute-done | bytes 524320 | tf_op jit(solution)/shard_map/ppermute | solution.py:194
  79.2 1.9 %collective-permute-done.16.refs_2_ = bf16[64,1792]{1,0:T(8,128)(2,1)S(1)} collective-permute-done((bf16[64,1792]{1,0:T(8,128)(2,1)S(1)}, bf16[64,1792]{1,0:T(8,128)(2,1)S(1)}, u32[]{:S(2)}, u32[]{:S(2)}) %collective-permute-start.16) | collective-permute-done | bytes 229408 | tf_op jit(solution)/shard_map/ppermute | solution.py:54
  82.5 3.9 %shard_map.82 = (bf16[64,1792]{1,0:T(8,128)(2,1)S(1)}, bf16[64,1792]{1,0:T(8,128)(2,1)S(1)}, bf16[64,1792]{1,0:T(8,128)(2,1)S(1)}, bf16[64,1792]{1,0:T(8,128)(2,1)S(1)}) custom-call(s32[2]{0:T(128)S(1)} %pad_add_fusion.index_ref, bf16[512,256]{1,0:T(8,128)(2,1)S(1)} %add_convert_fusion.own_ref, bf16[512,256]{1,0:T(8,128)(2,1)S(1)} %collective-permute-done.11.other_ref, ...), custom_call_target="tpu_custom_call" | custom-call | flops 939524096 | bytes 3670016 | tf_op jit(solution)/shard_map/pallas_call | solution.py:230
  87.7 3.8 %shard_map.81 = (bf16[64,1792]{1,0:T(8,128)(2,1)S(1)}, bf16[64,1792]{1,0:T(8,128)(2,1)S(1)}, bf16[64,1792]{1,0:T(8,128)(2,1)S(1)}, bf16[64,1792]{1,0:T(8,128)(2,1)S(1)}) custom-call(s32[2]{0:T(128)S(1)} %pad_add_fusion.index_ref, bf16[512,256]{1,0:T(8,128)(2,1)S(1)} %add_convert_fusion.own_ref, bf16[512,256]{1,0:T(8,128)(2,1)S(1)} %collective-permute-done.11.other_ref, ...), custom_call_target="tpu_custom_call" | custom-call | flops 939524096 | bytes 3670016 | tf_op jit(solution)/shard_map/pallas_call | solution.py:230
  96.6 5.6 %collective-permute-done.30 = bf16[32,1792]{1,0:T(8,128)(2,1)S(1)} collective-permute-done((bf16[32,1792]{1,0:T(8,128)(2,1)S(1)}, bf16[32,1792]{1,0:T(8,128)(2,1)S(1)}, u32[]{:S(2)}, u32[]{:S(2)}) %collective-permute-start.30) | collective-permute-done | bytes 114720 | tf_op jit(solution)/shard_map/ppermute | solution.py:54
  109.2 5.2 %collective-permute-done.13.refs_3_ = bf16[32,1792]{1,0:T(8,128)(2,1)S(1)} collective-permute-done((bf16[32,1792]{1,0:T(8,128)(2,1)S(1)}, bf16[32,1792]{1,0:T(8,128)(2,1)S(1)}, u32[]{:S(2)}, u32[]{:S(2)}) %collective-permute-start.13) | collective-permute-done | bytes 114720 | tf_op jit(solution)/shard_map/ppermute | solution.py:54
  115.4 3.4 %collective-permute-start.18 = (bf16[32,1792]{1,0:T(8,128)(2,1)S(1)}, bf16[32,1792]{1,0:T(8,128)(2,1)S(1)}, u32[]{:S(2)}, u32[]{:S(2)}) collective-permute-start(bf16[32,1792]{1,0:T(8,128)(2,1)S(1)} %get-tuple-element.51), channel_id=1, source_target_pairs={{0,16},{1,17},{2,18},{3,19},{4,20},{5,21},{6,22},{7,23},{8,24},{9,... | collective-permute-start | bytes 344072 | tf_op jit(solution)/shard_map/ppermute | solution.py:54
  118.7 3.5 %collective-permute-done.18 = bf16[32,1792]{1,0:T(8,128)(2,1)S(1)} collective-permute-done((bf16[32,1792]{1,0:T(8,128)(2,1)S(1)}, bf16[32,1792]{1,0:T(8,128)(2,1)S(1)}, u32[]{:S(2)}, u32[]{:S(2)}) %collective-permute-start.18) | collective-permute-done | bytes 114720 | tf_op jit(solution)/shard_map/ppermute | solution.py:54
  122.9 3.4 %collective-permute-start.24 = (bf16[64,1792]{1,0:T(8,128)(2,1)S(1)}, bf16[64,1792]{1,0:T(8,128)(2,1)S(1)}, u32[]{:S(2)}, u32[]{:S(2)}) collective-permute-start(bf16[64,1792]{1,0:T(8,128)(2,1)S(1)} %add_convert_fusion.3), channel_id=1, source_target_pairs={{0,8},{1,9},{2,10},{3,11},{4,12},{5,13},{6,14},{7,15},{8,0},{9,1},... | collective-permute-start | bytes 688136 | tf_op jit(solution)/shard_map/ppermute | solution.py:54
  128.6 3.6 %collective-permute-done.24.refs_2_ = bf16[64,1792]{1,0:T(8,128)(2,1)S(1)} collective-permute-done((bf16[64,1792]{1,0:T(8,128)(2,1)S(1)}, bf16[64,1792]{1,0:T(8,128)(2,1)S(1)}, u32[]{:S(2)}, u32[]{:S(2)}) %collective-permute-start.24) | collective-permute-done | bytes 229408 | tf_op jit(solution)/shard_map/ppermute | solution.py:54
  132.2 2.0 %collective-permute-start.29 = (bf16[32,1792]{1,0:T(8,128)(2,1)S(1)}, bf16[32,1792]{1,0:T(8,128)(2,1)S(1)}, u32[]{:S(2)}, u32[]{:S(2)}) collective-permute-start(bf16[32,1792]{1,0:T(8,128)(2,1)S(1)} %add_convert_fusion.5), channel_id=1, source_target_pairs={{0,16},{1,17},{2,18},{3,19},{4,20},{5,21},{6,22},{7,23},{8,24},{9,... | collective-permute-start | bytes 344072 | tf_op jit(solution)/shard_map/ppermute | solution.py:54
  135.2 5.5 %collective-permute-done.29.refs_3_ = bf16[32,1792]{1,0:T(8,128)(2,1)S(1)} collective-permute-done((bf16[32,1792]{1,0:T(8,128)(2,1)S(1)}, bf16[32,1792]{1,0:T(8,128)(2,1)S(1)}, u32[]{:S(2)}, u32[]{:S(2)}) %collective-permute-start.29) | collective-permute-done | bytes 114720 | tf_op jit(solution)/shard_map/ppermute | solution.py:54
  141.7 5.6 %collective-permute-done.38 = bf16[32,1792]{1,0:T(8,128)(2,1)S(1)} collective-permute-done((bf16[32,1792]{1,0:T(8,128)(2,1)S(1)}, bf16[32,1792]{1,0:T(8,128)(2,1)S(1)}, u32[]{:S(2)}, u32[]{:S(2)}) %collective-permute-start.38) | collective-permute-done | bytes 114720 | tf_op jit(solution)/shard_map/ppermute | solution.py:54
  148.6 4.2 %collective-permute-start.34 = (bf16[32,1792]{1,0:T(8,128)(2,1)S(1)}, bf16[32,1792]{1,0:T(8,128)(2,1)S(1)}, u32[]{:S(2)}, u32[]{:S(2)}) collective-permute-start(bf16[32,1792]{1,0:T(8,128)(2,1)S(1)} %get-tuple-element.63), channel_id=1, source_target_pairs={{0,16},{1,17},{2,18},{3,19},{4,20},{5,21},{6,22},{7,23},{8,24},{9,... | collective-permute-start | bytes 344072 | tf_op jit(solution)/shard_map/ppermute | solution.py:54
  152.8 3.9 %collective-permute-done.34 = bf16[32,1792]{1,0:T(8,128)(2,1)S(1)} collective-permute-done((bf16[32,1792]{1,0:T(8,128)(2,1)S(1)}, bf16[32,1792]{1,0:T(8,128)(2,1)S(1)}, u32[]{:S(2)}, u32[]{:S(2)}) %collective-permute-start.34) | collective-permute-done | bytes 114720 | tf_op jit(solution)/shard_map/ppermute | solution.py:54
  159.9 3.0 %collective-permute-done.35.refs_5_ = bf16[64,1792]{1,0:T(8,128)(2,1)S(1)} collective-permute-done((bf16[64,1792]{1,0:T(8,128)(2,1)S(1)}, bf16[64,1792]{1,0:T(8,128)(2,1)S(1)}, u32[]{:S(2)}, u32[]{:S(2)}) %collective-permute-start.35) | collective-permute-done | bytes 229408 | tf_op jit(solution)/shard_map/ppermute | solution.py:54
  162.9 2.5 %collective-permute-done.41.refs_7_ = bf16[64,1792]{1,0:T(8,128)(2,1)S(1)} collective-permute-done((bf16[64,1792]{1,0:T(8,128)(2,1)S(1)}, bf16[64,1792]{1,0:T(8,128)(2,1)S(1)}, u32[]{:S(2)}, u32[]{:S(2)}) %collective-permute-start.41) | collective-permute-done | bytes 229408 | tf_op jit(solution)/shard_map/ppermute | solution.py:54
  165.4 4.7 %shard_map.89.refs_9_ = bf16[1024,3584]{1,0:T(8,128)(2,1)} custom-call(s32[2]{0:T(128)S(1)} %pad_add_fusion.index_ref, bf16[64,1792]{1,0:T(8,128)(2,1)S(1)} %constant_dynamic-update-slice_fusion.2.refs_0_, bf16[64,1792]{1,0:T(8,128)(2,1)S(1)} %collective-permute-done.31.refs_8_.refs_1_, bf16[64,1792]{1,0:T(8,128)(2,1)S(1)} %collective-permute-done.32.refs_9_.refs_2_, ...), custom_call_target="tpu_custom_call" | custom-call | flops 1879048192 | bytes 3670016 | tf_op jit(solution)/shard_map/pallas_call | solution.py:310
  170.3 4.7 %shard_map.90 = bf16[1024,3584]{1,0:T(8,128)(2,1)} custom-call(s32[2]{0:T(128)S(1)} %pad_add_fusion.index_ref, bf16[64,1792]{1,0:T(8,128)(2,1)S(1)} %constant_dynamic-update-slice_fusion.refs_0_, bf16[64,1792]{1,0:T(8,128)(2,1)S(1)} %collective-permute-done.19.refs_8_.refs_1_, ...), custom_call_target="tpu_custom_call", output_to_operand_aliasing={{}: (10, {})} | custom-call | flops 1879048192 | bytes 3670016 | tf_op jit(solution)/shard_map/pallas_call | solution.py:310
  (97 shorter events, 36.8 us)
Async XLA Ops:
  3.0 10.2 %collective-permute-start.1 = (bf16[1024,256]{1,0:T(8,128)(2,1)S(1)}, bf16[1024,256]{1,0:T(8,128)(2,1)S(1)}, u32[]{:S(2)}, u32[]{:S(2)}) collective-permute-start(bf16[1024,256]{1,0:T(8,128)(2,1)S(1)} %collective-permute-done.refs_0_), channel_id=1, source_target_pairs={{0,4},{1,5},{2,6},{3,7},{4,0},{5,1},{6,2},{7,3},{8,12},{9,13},{10,... | collective-permute-start | bytes 1572872 | tf_op jit(solution)/shard_map/ppermute | solution.py:54
  7.8 24.0 %collective-permute-start.5 = (bf16[1024,256]{1,0:T(8,128)(2,1)S(1)}, bf16[1024,256]{1,0:T(8,128)(2,1)S(1)}, u32[]{:S(2)}, u32[]{:S(2)}) collective-permute-start(bf16[1024,256]{1,0:T(8,128)(2,1)S(1)} %shard_map.78), channel_id=1, source_target_pairs={{0,0},{10,1},{16,2},{26,3},{4,4},{14,5},{20,6},{30,7},{2,8},{8,9},... | collective-permute-start | bytes 1572872 | tf_op jit(solution)/shard_map/ppermute | solution.py:125
  17.8 15.5 %collective-permute-start.2 = (f32[512,256]{1,0:T(8,128)S(1)}, f32[512,256]{1,0:T(8,128)S(1)}, u32[]{:S(2)}, u32[]{:S(2)}) collective-permute-start(f32[512,256]{1,0:T(8,128)S(1)} %get-tuple-element.36), channel_id=1, source_target_pairs={{0,1},{1,0},{2,3},{3,2},{4,5},{5,4},{6,7},{7,6},{8,9},{9,8},{10,11... | collective-permute-start | bytes 1572872 | tf_op jit(solution)/shard_map/ppermute | solution.py:194
  31.8 13.0 %collective-permute-start.6 = (bf16[1024,256]{1,0:T(8,128)(2,1)S(1)}, bf16[1024,256]{1,0:T(8,128)(2,1)S(1)}, u32[]{:S(2)}, u32[]{:S(2)}) collective-permute-start(bf16[1024,256]{1,0:T(8,128)(2,1)S(1)} %collective-permute-done.5.refs_0_), channel_id=1, source_target_pairs={{0,4},{1,5},{2,6},{3,7},{4,0},{5,1},{6,2},{7,3},{8,12},{9,13},{10,... | collective-permute-start | bytes 1572872 | tf_op jit(solution)/shard_map/ppermute | solution.py:54
  33.4 22.3 %collective-permute-start.3 = (f32[512,256]{1,0:T(8,128)S(1)}, f32[512,256]{1,0:T(8,128)S(1)}, u32[]{:S(2)}, u32[]{:S(2)}) collective-permute-start(f32[512,256]{1,0:T(8,128)S(1)} %add.50), channel_id=1, source_target_pairs={{0,2},{1,3},{2,0},{3,1},{4,6},{5,7},{6,4},{7,5},{8,10},{9,11},{10,... | collective-permute-start | bytes 1572872 | tf_op jit(solution)/shard_map/ppermute | solution.py:194
  49.4 15.6 %collective-permute-start.9 = (f32[512,256]{1,0:T(8,128)S(1)}, f32[512,256]{1,0:T(8,128)S(1)}, u32[]{:S(2)}, u32[]{:S(2)}) collective-permute-start(f32[512,256]{1,0:T(8,128)S(1)} %get-tuple-element.37.refs_0_), channel_id=1, source_target_pairs={{0,1},{1,0},{2,3},{3,2},{4,5},{5,4},{6,7},{7,6},{8,9},{9,8},{10,11... | collective-permute-start | bytes 1572872 | tf_op jit(solution)/shard_map/ppermute | solution.py:194
  61.2 13.5 %collective-permute-start.15 = (bf16[64,1792]{1,0:T(8,128)(2,1)S(1)}, bf16[64,1792]{1,0:T(8,128)(2,1)S(1)}, u32[]{:S(2)}, u32[]{:S(2)}) collective-permute-start(bf16[64,1792]{1,0:T(8,128)(2,1)S(1)} %get-tuple-element.48), channel_id=1, source_target_pairs={{0,8},{1,9},{2,10},{3,11},{4,12},{5,13},{6,14},{7,15},{8,0},{9,1},... | collective-permute-start | bytes 688136 | tf_op jit(solution)/shard_map/ppermute | solution.py:54
  65.0 14.0 %collective-permute-start.10 = (f32[512,256]{1,0:T(8,128)S(1)}, f32[512,256]{1,0:T(8,128)S(1)}, u32[]{:S(2)}, u32[]{:S(2)}) collective-permute-start(f32[512,256]{1,0:T(8,128)S(1)} %add.52), channel_id=1, source_target_pairs={{0,2},{1,3},{2,0},{3,1},{4,6},{5,7},{6,4},{7,5},{8,10},{9,11},{10,... | collective-permute-start | bytes 1572872 | tf_op jit(solution)/shard_map/ppermute | solution.py:194
  66.8 12.4 %collective-permute-start.14 = (bf16[64,1792]{1,0:T(8,128)(2,1)S(1)}, bf16[64,1792]{1,0:T(8,128)(2,1)S(1)}, u32[]{:S(2)}, u32[]{:S(2)}) collective-permute-start(bf16[64,1792]{1,0:T(8,128)(2,1)S(1)} %get-tuple-element.46), channel_id=1, source_target_pairs={{0,8},{1,9},{2,10},{3,11},{4,12},{5,13},{6,14},{7,15},{8,0},{9,1},... | collective-permute-start | bytes 688136 | tf_op jit(solution)/shard_map/ppermute | solution.py:54
  72.7 30.3 %collective-permute-start.7 = (bf16[64,1792]{1,0:T(8,128)(2,1)S(1)}, bf16[64,1792]{1,0:T(8,128)(2,1)S(1)}, u32[]{:S(2)}, u32[]{:S(2)}) collective-permute-start(bf16[64,1792]{1,0:T(8,128)(2,1)S(1)} %get-tuple-element.39), channel_id=1, source_target_pairs={{0,8},{1,9},{2,10},{3,11},{4,12},{5,13},{6,14},{7,15},{8,0},{9,1},... | collective-permute-start | bytes 688136 | tf_op jit(solution)/shard_map/ppermute | solution.py:54
  72.8 19.6 %collective-permute-start.8 = (bf16[64,1792]{1,0:T(8,128)(2,1)S(1)}, bf16[64,1792]{1,0:T(8,128)(2,1)S(1)}, u32[]{:S(2)}, u32[]{:S(2)}) collective-permute-start(bf16[64,1792]{1,0:T(8,128)(2,1)S(1)} %get-tuple-element.41), channel_id=1, source_target_pairs={{0,8},{1,9},{2,10},{3,11},{4,12},{5,13},{6,14},{7,15},{8,0},{9,1},... | collective-permute-start | bytes 688136 | tf_op jit(solution)/shard_map/ppermute | solution.py:54
  81.2 12.6 %collective-permute-start.17 = (bf16[32,1792]{1,0:T(8,128)(2,1)S(1)}, bf16[32,1792]{1,0:T(8,128)(2,1)S(1)}, u32[]{:S(2)}, u32[]{:S(2)}) collective-permute-start(bf16[32,1792]{1,0:T(8,128)(2,1)S(1)} %add_convert_fusion.7), channel_id=1, source_target_pairs={{0,16},{1,17},{2,18},{3,19},{4,20},{5,21},{6,22},{7,23},{8,24},{9,... | collective-permute-start | bytes 344072 | tf_op jit(solution)/shard_map/ppermute | solution.py:54
  86.4 21.0 %collective-permute-start.23 = (bf16[64,1792]{1,0:T(8,128)(2,1)S(1)}, bf16[64,1792]{1,0:T(8,128)(2,1)S(1)}, u32[]{:S(2)}, u32[]{:S(2)}) collective-permute-start(bf16[64,1792]{1,0:T(8,128)(2,1)S(1)} %get-tuple-element.44.refs_1_), channel_id=1, source_target_pairs={{0,4},{1,5},{2,6},{3,7},{4,0},{5,1},{6,2},{7,3},{8,12},{9,13},{10,... | collective-permute-start | bytes 688136 | tf_op jit(solution)/shard_map/ppermute | solution.py:54
  91.6 14.4 %collective-permute-start.27 = (bf16[64,1792]{1,0:T(8,128)(2,1)S(1)}, bf16[64,1792]{1,0:T(8,128)(2,1)S(1)}, u32[]{:S(2)}, u32[]{:S(2)}) collective-permute-start(bf16[64,1792]{1,0:T(8,128)(2,1)S(1)} %get-tuple-element.43.refs_0_), channel_id=1, source_target_pairs={{0,4},{1,5},{2,6},{3,7},{4,0},{5,1},{6,2},{7,3},{8,12},{9,13},{10,... | collective-permute-start | bytes 688136 | tf_op jit(solution)/shard_map/ppermute | solution.py:54
  92.4 11.9 %collective-permute-start.12 = (bf16[64,1792]{1,0:T(8,128)(2,1)S(1)}, bf16[64,1792]{1,0:T(8,128)(2,1)S(1)}, u32[]{:S(2)}, u32[]{:S(2)}) collective-permute-start(bf16[64,1792]{1,0:T(8,128)(2,1)S(1)} %shard_map.83), channel_id=1, source_target_pairs={{0,4},{1,5},{2,6},{3,7},{4,0},{5,1},{6,2},{7,3},{8,12},{9,13},{10,... | collective-permute-start | bytes 688136 | tf_op jit(solution)/shard_map/ppermute | solution.py:54
  94.7 7.5 %collective-permute-start.30 = (bf16[32,1792]{1,0:T(8,128)(2,1)S(1)}, bf16[32,1792]{1,0:T(8,128)(2,1)S(1)}, u32[]{:S(2)}, u32[]{:S(2)}) collective-permute-start(bf16[32,1792]{1,0:T(8,128)(2,1)S(1)} %get-tuple-element.60), channel_id=1, source_target_pairs={{0,16},{1,17},{2,18},{3,19},{4,20},{5,21},{6,22},{7,23},{8,24},{9,... | collective-permute-start | bytes 344072 | tf_op jit(solution)/shard_map/ppermute | solution.py:54
  102.2 26.2 %collective-permute-start.22 = (bf16[64,1792]{1,0:T(8,128)(2,1)S(1)}, bf16[64,1792]{1,0:T(8,128)(2,1)S(1)}, u32[]{:S(2)}, u32[]{:S(2)}) collective-permute-start(bf16[64,1792]{1,0:T(8,128)(2,1)S(1)} %get-tuple-element.53), channel_id=1, source_target_pairs={{0,4},{1,5},{2,6},{3,7},{4,0},{5,1},{6,2},{7,3},{8,12},{9,13},{10,... | collective-permute-start | bytes 688136 | tf_op jit(solution)/shard_map/ppermute | solution.py:54
  103.0 20.0 %collective-permute-start.26 = (bf16[64,1792]{1,0:T(8,128)(2,1)S(1)}, bf16[64,1792]{1,0:T(8,128)(2,1)S(1)}, u32[]{:S(2)}, u32[]{:S(2)}) collective-permute-start(bf16[64,1792]{1,0:T(8,128)(2,1)S(1)} %get-tuple-element.56), channel_id=1, source_target_pairs={{0,4},{1,5},{2,6},{3,7},{4,0},{5,1},{6,2},{7,3},{8,12},{9,13},{10,... | collective-permute-start | bytes 688136 | tf_op jit(solution)/shard_map/ppermute | solution.py:54
  104.3 22.0 %collective-permute-start.31 = (bf16[64,1792]{1,0:T(8,128)(2,1)S(1)}, bf16[64,1792]{1,0:T(8,128)(2,1)S(1)}, u32[]{:S(2)}, u32[]{:S(2)}) collective-permute-start(bf16[64,1792]{1,0:T(8,128)(2,1)S(1)} %constant_dynamic-update-slice_fusion.2.refs_0_), channel_id=1, source_target_pairs={{0,8},{1,9},{2,10},{3,11},{4,12},{5,13},{6,14},{7,15},{8,0},{9,1},... | collective-permute-start | bytes 688136 | tf_op jit(solution)/shard_map/ppermute | solution.py:54
  106.0 8.5 %collective-permute-start.13 = (bf16[32,1792]{1,0:T(8,128)(2,1)S(1)}, bf16[32,1792]{1,0:T(8,128)(2,1)S(1)}, u32[]{:S(2)}, u32[]{:S(2)}) collective-permute-start(bf16[32,1792]{1,0:T(8,128)(2,1)S(1)} %add_convert_fusion.8), channel_id=1, source_target_pairs={{0,16},{1,17},{2,18},{3,19},{4,20},{5,21},{6,22},{7,23},{8,24},{9,... | collective-permute-start | bytes 344072 | tf_op jit(solution)/shard_map/ppermute | solution.py:54
  107.3 19.6 %collective-permute-start.28 = (bf16[64,1792]{1,0:T(8,128)(2,1)S(1)}, bf16[64,1792]{1,0:T(8,128)(2,1)S(1)}, u32[]{:S(2)}, u32[]{:S(2)}) collective-permute-start(bf16[64,1792]{1,0:T(8,128)(2,1)S(1)} %add_convert_fusion.2), channel_id=1, source_target_pairs={{0,8},{1,9},{2,10},{3,11},{4,12},{5,13},{6,14},{7,15},{8,0},{9,1},... | collective-permute-start | bytes 688136 | tf_op jit(solution)/shard_map/ppermute | solution.py:54
  122.2 12.0 %collective-permute-start.32 = (bf16[64,1792]{1,0:T(8,128)(2,1)S(1)}, bf16[64,1792]{1,0:T(8,128)(2,1)S(1)}, u32[]{:S(2)}, u32[]{:S(2)}) collective-permute-start(bf16[64,1792]{1,0:T(8,128)(2,1)S(1)} %constant_dynamic-update-slice_fusion.2.refs_0_), channel_id=1, source_target_pairs={{0,4},{1,5},{2,6},{3,7},{4,0},{5,1},{6,2},{7,3},{8,12},{9,13},{10,... | collective-permute-start | bytes 688136 | tf_op jit(solution)/shard_map/ppermute | solution.py:54
  122.9 9.3 %collective-permute-start.24 = (bf16[64,1792]{1,0:T(8,128)(2,1)S(1)}, bf16[64,1792]{1,0:T(8,128)(2,1)S(1)}, u32[]{:S(2)}, u32[]{:S(2)}) collective-permute-start(bf16[64,1792]{1,0:T(8,128)(2,1)S(1)} %add_convert_fusion.3), channel_id=1, source_target_pairs={{0,8},{1,9},{2,10},{3,11},{4,12},{5,13},{6,14},{7,15},{8,0},{9,1},... | collective-permute-start | bytes 688136 | tf_op jit(solution)/shard_map/ppermute | solution.py:54
  126.4 14.4 %collective-permute-start.33 = (bf16[64,1792]{1,0:T(8,128)(2,1)S(1)}, bf16[64,1792]{1,0:T(8,128)(2,1)S(1)}, u32[]{:S(2)}, u32[]{:S(2)}) collective-permute-start(bf16[64,1792]{1,0:T(8,128)(2,1)S(1)} %collective-permute-done.31.refs_8_.refs_1_), channel_id=1, source_target_pairs={{0,4},{1,5},{2,6},{3,7},{4,0},{5,1},{6,2},{7,3},{8,12},{9,13},{10,... | collective-permute-start | bytes 688136 | tf_op jit(solution)/shard_map/ppermute | solution.py:54
  127.0 20.5 %collective-permute-start.20 = (bf16[64,1792]{1,0:T(8,128)(2,1)S(1)}, bf16[64,1792]{1,0:T(8,128)(2,1)S(1)}, u32[]{:S(2)}, u32[]{:S(2)}) collective-permute-start(bf16[64,1792]{1,0:T(8,128)(2,1)S(1)} %constant_dynamic-update-slice_fusion.refs_0_), channel_id=1, source_target_pairs={{0,4},{1,5},{2,6},{3,7},{4,0},{5,1},{6,2},{7,3},{8,12},{9,13},{10,... | collective-permute-start | bytes 688136 | tf_op jit(solution)/shard_map/ppermute | solution.py:54
  128.5 13.2 %collective-permute-start.19 = (bf16[64,1792]{1,0:T(8,128)(2,1)S(1)}, bf16[64,1792]{1,0:T(8,128)(2,1)S(1)}, u32[]{:S(2)}, u32[]{:S(2)}) collective-permute-start(bf16[64,1792]{1,0:T(8,128)(2,1)S(1)} %constant_dynamic-update-slice_fusion.refs_0_), channel_id=1, source_target_pairs={{0,8},{1,9},{2,10},{3,11},{4,12},{5,13},{6,14},{7,15},{8,0},{9,1},... | collective-permute-start | bytes 688136 | tf_op jit(solution)/shard_map/ppermute | solution.py:54
  132.2 8.6 %collective-permute-start.29 = (bf16[32,1792]{1,0:T(8,128)(2,1)S(1)}, bf16[32,1792]{1,0:T(8,128)(2,1)S(1)}, u32[]{:S(2)}, u32[]{:S(2)}) collective-permute-start(bf16[32,1792]{1,0:T(8,128)(2,1)S(1)} %add_convert_fusion.5), channel_id=1, source_target_pairs={{0,16},{1,17},{2,18},{3,19},{4,20},{5,21},{6,22},{7,23},{8,24},{9,... | collective-permute-start | bytes 344072 | tf_op jit(solution)/shard_map/ppermute | solution.py:54
  134.3 13.2 %collective-permute-start.25 = (bf16[32,1792]{1,0:T(8,128)(2,1)S(1)}, bf16[32,1792]{1,0:T(8,128)(2,1)S(1)}, u32[]{:S(2)}, u32[]{:S(2)}) collective-permute-start(bf16[32,1792]{1,0:T(8,128)(2,1)S(1)} %add_convert_fusion.6), channel_id=1, source_target_pairs={{0,16},{1,17},{2,18},{3,19},{4,20},{5,21},{6,22},{7,23},{8,24},{9,... | collective-permute-start | bytes 344072 | tf_op jit(solution)/shard_map/ppermute | solution.py:54
  147.4 10.4 %collective-permute-start.39 = (bf16[64,1792]{1,0:T(8,128)(2,1)S(1)}, bf16[64,1792]{1,0:T(8,128)(2,1)S(1)}, u32[]{:S(2)}, u32[]{:S(2)}) collective-permute-start(bf16[64,1792]{1,0:T(8,128)(2,1)S(1)} %constant_dynamic-update-slice_fusion.6.refs_4_), channel_id=1, source_target_pairs={{0,8},{1,9},{2,10},{3,11},{4,12},{5,13},{6,14},{7,15},{8,0},{9,1},... | collective-permute-start | bytes 688136 | tf_op jit(solution)/shard_map/ppermute | solution.py:54
  148.6 8.1 %collective-permute-start.34 = (bf16[32,1792]{1,0:T(8,128)(2,1)S(1)}, bf16[32,1792]{1,0:T(8,128)(2,1)S(1)}, u32[]{:S(2)}, u32[]{:S(2)}) collective-permute-start(bf16[32,1792]{1,0:T(8,128)(2,1)S(1)} %get-tuple-element.63), channel_id=1, source_target_pairs={{0,16},{1,17},{2,18},{3,19},{4,20},{5,21},{6,22},{7,23},{8,24},{9,... | collective-permute-start | bytes 344072 | tf_op jit(solution)/shard_map/ppermute | solution.py:54
  157.8 7.5 %collective-permute-start.41 = (bf16[64,1792]{1,0:T(8,128)(2,1)S(1)}, bf16[64,1792]{1,0:T(8,128)(2,1)S(1)}, u32[]{:S(2)}, u32[]{:S(2)}) collective-permute-start(bf16[64,1792]{1,0:T(8,128)(2,1)S(1)} %collective-permute-done.39.refs_5_), channel_id=1, source_target_pairs={{0,4},{1,5},{2,6},{3,7},{4,0},{5,1},{6,2},{7,3},{8,12},{9,13},{10,... | collective-permute-start | bytes 688136 | tf_op jit(solution)/shard_map/ppermute | solution.py:54
  158.9 11.1 %collective-permute-start.36 = (bf16[64,1792]{1,0:T(8,128)(2,1)S(1)}, bf16[64,1792]{1,0:T(8,128)(2,1)S(1)}, u32[]{:S(2)}, u32[]{:S(2)}) collective-permute-start(bf16[64,1792]{1,0:T(8,128)(2,1)S(1)} %constant_dynamic-update-slice_fusion.4.refs_4_), channel_id=1, source_target_pairs={{0,4},{1,5},{2,6},{3,7},{4,0},{5,1},{6,2},{7,3},{8,12},{9,13},{10,... | collective-permute-start | bytes 688136 | tf_op jit(solution)/shard_map/ppermute | solution.py:54
  (15 other events, 127.9 us)

commit v4 on v3

--- a/solution.py
+++ b/solution.py
@@ -1,4 +1,4 @@
-import functools
+import itertools
 
 import jax
 import jax.numpy as jnp
@@ -37,6 +37,21 @@
         kernel,
         in_specs=[pl.BlockSpec(one.shape)] * 2 + [ANYWHERE] * len(wait_for),
         out_shape=jax.ShapeDtypeStruct(one.shape, BF16),
+        compiler_params=pltpu.CompilerParams(vmem_limit_bytes=VMEM_LIMIT),
+    )(one, other, *wait_for)
+
+
+def join_after(one, other, wait_for):
+    rows, columns = one.shape
+
+    def kernel(one_ref, other_ref, *refs):
+        refs[-1][:rows, :] = one_ref[...]
+        refs[-1][rows:, :] = other_ref[...]
+
+    return pl.pallas_call(
+        kernel,
+        in_specs=[pl.BlockSpec(one.shape)] * 2 + [ANYWHERE] * len(wait_for),
+        out_shape=jax.ShapeDtypeStruct((2 * rows, columns), BF16),
         compiler_params=pltpu.CompilerParams(vmem_limit_bytes=VMEM_LIMIT),
     )(one, other, *wait_for)
 
@@ -79,10 +94,11 @@
             terms = [(t, at + rows) for t, at in terms] + [(self.swap(out, bit), 0)]
         return terms
 
-    def gather(self, own, order):
+    def gather(self, own, order, wait_for):
         first, second = order[:2]
         for bit in order[:1:-1]:
-            own = jnp.concatenate([own, self.swap(own, bit)])
+            got = self.swap(own, bit)
+            own = join_after(own, got, wait_for) if wait_for else jnp.concatenate([own, got])
         across = self.swap(own, second)
         return [own, across, self.swap(own, first), self.swap(across, first)]
 
@@ -126,59 +142,26 @@
     return here
 
 
-def project(cube, index, blocks, activations, wait_for):
+def project(cube, blocks, activations):
     tokens, features = activations.shape
     rows, ranks = blocks[0].shape
     shards = len(blocks) // 2
-    half = cube.mp // 2
-    step = tokens // (2 * half)
-
-    def block_of(i, index):
-        return jnp.where(i < half, 1 - index[1], index[1]) * half + lax.rem(i, half)
-
-    def kernel(index_ref, *refs):
-        pieces, act_ref, (send_ref, keep_ref, held) = refs[: 2 * shards], refs[2 * shards], refs[-3:]
-        i = pl.program_id(0)
-
-        @pl.when(i == 0)
-        def _():
-            line, pair = index_ref[0] // 2, lax.rem(index_ref[0], 2)
-            for j in range(2 * shards):
-                side = pair if j < shards else 1 - pair
-                start = (lax.rem(line + j, shards) * 2 + side) * rows
-                held[pl.ds(pl.multiple_of(start, rows), rows), :] = pieces[j][...]
-
-        value = jnp.dot(act_ref[...], held[...], preferred_element_type=F32)
-
-        @pl.when(i < half)
-        def _():
-            send_ref[...] = value
-
-        @pl.when(i >= half)
-        def _():
-            keep_ref[...] = value
-
-    shape = jax.ShapeDtypeStruct((tokens // 2, ranks), F32)
-    return pl.pallas_call(
-        kernel,
-        grid_spec=pltpu.PrefetchScalarGridSpec(
-            num_scalar_prefetch=1,
-            grid=(2 * half,),
-            in_specs=[pl.BlockSpec(b.shape, lambda i, index: (0, 0)) for b in blocks]
-            + [pl.BlockSpec((step, features), lambda i, index: (block_of(i, index), 0))]
-            + [ANYWHERE] * len(wait_for),
-            out_specs=[
-                pl.BlockSpec((step, ranks), lambda i, index: (jnp.minimum(i, half - 1), 0)),
-                pl.BlockSpec((step, ranks), lambda i, index: (jnp.maximum(i - half, 0), 0)),
-            ],
-            scratch_shapes=[pltpu.VMEM((features, ranks), BF16)],
-        ),
-        out_shape=[shape, shape],
-        compiler_params=pltpu.CompilerParams(vmem_limit_bytes=VMEM_LIMIT),
-        cost_estimate=pl.CostEstimate(
-            flops=2 * tokens * features * ranks, bytes_accessed=2 * tokens * features, transcendentals=0
-        ),
-    )(index, *blocks, activations, *wait_for)
+    d, core = lax.axis_index("dp"), lax.axis_index("mp") % 2
+    if shards == 1:
+        one, other = blocks
+        held = jnp.where(d % 2 == 0, jnp.concatenate([one, other]), jnp.concatenate([other, one]))
+    else:
+        held = jnp.zeros((features, ranks), BF16)
+        for j, block in enumerate(blocks):
+            side = d % 2 if j < shards else 1 - d % 2
+            start = ((d // 2 + j) % shards * 2 + side) * rows
+            held = lax.dynamic_update_slice_in_dim(held, block, start, 0)
+
+    def half(which):
+        own = lax.dynamic_slice_in_dim(activations, which * (tokens // 2), tokens // 2, 0)
+        return jnp.dot(own, held, preferred_element_type=F32)
+
+    return half(1 - core), half(core)
 
 
 def sum_columns(cube, send, keep):
@@ -343,32 +326,38 @@
         partial = []
         for h in range(parts):
             blocks = here[h] + [cube.swap(value, 1) for value in here[h]]
-            partial.append(project(cube, index, blocks, activations, []))
+            partial.append(project(cube, blocks, activations))
         sums, quarters, groups, moments, update = {}, {}, [[None] * parts for _ in range(HALVES)], [], []
         projected = [sum_columns(cube, *value) for value in partial]
-        sum_orders = [cube.pair_mid, cube.pair_first] if parts > 1 else [cube.pair_first]
-        gather_orders = [cube.pair_first, cube.pair_first] if parts > 1 else [cube.pair_first]
+        sum_order = {key: cube.pair_first for key in itertools.product(range(parts), range(HALVES))}
+        gather_order = dict(sum_order)
+        if parts > 1:
+            sum_order[0, 0] = sum_order[0, 1] = cube.pair_mid
         for h in range(parts):
             for f in range(HALVES):
                 wait_for = []
                 if h + 1 < parts:
                     wait_for = [partial[h + 1][0]]
                 quarters[h, f] = grad_rows(
-                    cube, index, projected[h], out_grads, sum_orders[h], f * columns, columns, wait_for
+                    cube, index, projected[h], out_grads, sum_order[h, f], f * columns, columns, wait_for
                 )
         for h in range(parts):
             for f in range(HALVES):
                 wait_for = [quarters[h + 1, g][0] for g in range(HALVES)] if h + 1 < parts and f else []
-                sums[h, f] = cube.sum_up(quarters[h, f], sum_orders[h], wait_for)
-        for h in range(parts):
+                sums[h, f] = cube.sum_up(quarters[h, f], sum_order[h, f], wait_for)
+        for h in range(parts):
+            directions = []
             for f in range(HALVES):
                 wait_for = groups[f][h - 1][1:] if h else []
                 direction, *moments = adam(
                     cube, sums[h, f], first_moment, second_moment, h, f * columns, moments, wait_for
                 )
-                groups[f][h] = cube.gather(direction, gather_orders[h])
+                directions.append(direction)
+            for f in range(HALVES):
+                wait_for = directions[f + 1 :] if h == parts - 1 else []
+                groups[f][h] = cube.gather(directions[f], gather_order[h, f], wait_for)
         for f in range(HALVES):
-            update = [make_update(cube, index, groups[f], gather_orders, basis, f * columns, width, update)]
+            update = [make_update(cube, index, groups[f], [gather_order[h, f] for h in range(parts)], basis, f * columns, width, update)]
         return (*update, *moments)
 
     return jax.shard_map(

time: 175 us -> 169 us (0.966)
  Pallas kernels: 38.4 us -> 29.4 us
  starting transfers between devices: 80.1 us -> 72.7 us
  matrix products: 0 us -> 7.01 us
  waiting for transfers between devices: 52.3 us -> 56.7 us
    pallas_call x2 -> x1, Pallas kernels: 9.14 us -> 0.02 us  [join_after(): pl.pallas_call(kernel, in_specs=[pl.BlockSpec(one.shape)] * 2 + [ANYWHERE...]
    dot_general x0 -> x4, matrix products: none -> 7.01 us  [half(): return jnp.dot(own, held, preferred_element_type=F32)]
    ppermute x6, waiting for transfers between devices: 6.55 us -> 12.9 us  [move(): return lax.ppermute(value, AXES, pairs)]
    ppermute x34, starting transfers between devices: 47.1 us -> 42.1 us  [swap(): return lax.ppermute(value, AXES, pairs)]
    ppermute x6, starting transfers between devices: 31.6 us -> 29.1 us  [move(): return lax.ppermute(value, AXES, pairs)]
    ppermute x34, waiting for transfers between devices: 45.7 us -> 43.8 us  [swap(): return lax.ppermute(value, AXES, pairs)]
  transfers between devices with their start and end apart: 42 -> 42, of which waited for: 18 -> 20; matrix products, arithmetic and copies ran while one was open for 0% -> 5% of each run, Pallas kernels for 19% -> 14%
where the time goes in v4:
time: 169 us
  starting transfers between devices  72.7 us (43%)
  waiting for transfers between devices  56.7 us (34%)
  Pallas kernels  29.4 us (17%)
  matrix products  7.01 us (4%)
    ppermute x34, waiting for transfers between devices, swap(): return lax.ppermute(value, AXES, pairs)  43.8 us
    ppermute x34, starting transfers between devices, swap(): return lax.ppermute(value, AXES, pairs)  42.1 us
    ppermute x6, starting transfers between devices, move(): return lax.ppermute(value, AXES, pairs)  29.1 us
    pallas_call x4, Pallas kernels, grad_rows(): pl.pallas_call(kernel, grid_spec=pltpu.PrefetchScalarGridSpec(num_scalar_...  15.6 us
    ppermute x6, waiting for transfers between devices, move(): return lax.ppermute(value, AXES, pairs)  12.9 us
    pallas_call x2, Pallas kernels, make_update(): pl.pallas_call(kernel, grid_spec=pltpu.PrefetchScalarGridSpec(num_scalar_...  9.33 us
    dot_general x4, matrix products, half(): return jnp.dot(own, held, preferred_element_type=F32)  7.01 us
    pallas_call x4, Pallas kernels, adam(): pl.pallas_call(kernel, grid=(1,), in_specs=term_specs + [moment_spec] * 2...  3.55 us
  transfers between devices with their start and end apart: 42, of which 20 were waited for; matrix products, arithmetic and copies ran while one was open for 5% of the time, Pallas kernels for 14%

profile of v4, /device:TPU:0, one launch (start us, length us, event | category | flops | bytes accessed | tf_op | source)
XLA Modules:
  0.0 168.6 jit_solution(5945058609072034336)
XLA Ops:
  3.0 3.0 %collective-permute-start.1 = (bf16[1024,256]{1,0:T(8,128)(2,1)S(1)}, bf16[1024,256]{1,0:T(8,128)(2,1)S(1)}, u32[]{:S(2)}, u32[]{:S(2)}) collective-permute-start(bf16[1024,256]{1,0:T(8,128)(2,1)S(1)} %collective-permute-done.refs_0_), channel_id=1, source_target_pairs={{0,4},{1,5},{2,6},{3,7},{4,0},{5,1},{6,2},{7,3},{8,12},{9,13},{10,... | collective-permute-start | bytes 1572872 | tf_op jit(solution)/shard_map/ppermute | solution.py:69
  7.2 6.0 %collective-permute-done.1 = bf16[1024,256]{1,0:T(8,128)(2,1)S(1)} collective-permute-done((bf16[1024,256]{1,0:T(8,128)(2,1)S(1)}, bf16[1024,256]{1,0:T(8,128)(2,1)S(1)}, u32[]{:S(2)}, u32[]{:S(2)}) %collective-permute-start.1) | collective-permute-done | bytes 524320 | tf_op jit(solution)/shard_map/ppermute | solution.py:69
  13.2 3.1 %fusion.2 = f32[512,256]{1,0:T(8,128)} fusion(bf16[1024,2048]{1,0:T(8,128)(2,1)} %param.5, s32[]{:T(128)S(6)} %select_n.42, bf16[1024,256]{1,0:T(8,128)(2,1)S(1)} %collective-permute-done.1, bf16[1024,256]{1,0:T(8,128)(2,1)S(1)} %collective-permute-done.refs_0_, pred[]{:T(512)S(6)} %eq.10), kind=kOutput, calls=%fused_computation.2 | convolution fusion | flops 541589504 | bytes 3670021 | tf_op jit(solution)/shard_map/dot_general | solution.py:162
  16.3 13.6 %collective-permute-start.2 = (f32[512,256]{1,0:T(8,128)}, f32[512,256]{1,0:T(8,128)}, u32[]{:S(2)}, u32[]{:S(2)}) collective-permute-start(f32[512,256]{1,0:T(8,128)} %fusion.2), channel_id=1, source_target_pairs={{0,1},{1,0},{2,3},{3,2},{4,5},{5,4},{6,7},{7,6},{8,9},{9,8},{10,11... | collective-permute-start | bytes 1572872 | tf_op jit(solution)/shard_map/ppermute | solution.py:177
  31.8 2.4 %fusion.8 = f32[512,256]{1,0:T(8,128)S(1)} fusion(f32[512,256]{1,0:T(8,128)} %collective-permute-done.2, bf16[1024,2048]{1,0:T(8,128)(2,1)} %param.5, s32[]{:T(128)S(6)} %select_n.38, bf16[1024,256]{1,0:T(8,128)(2,1)S(1)} %collective-permute-done.1, bf16[1024,256]{1,0:T(8,128)(2,1)S(1)} %collective-permute-done.refs_0_, pred[]{:T(512)S(6)} %eq.10), kind=kOutput, calls=%fused_computation.8 | convolution fusion | flops 541720576 | bytes 4194309 | tf_op jit(solution)/shard_map/dot_general | solution.py:162
  34.3 11.6 %collective-permute-start.3 = (f32[512,256]{1,0:T(8,128)S(1)}, f32[512,256]{1,0:T(8,128)S(1)}, u32[]{:S(2)}, u32[]{:S(2)}) collective-permute-start(f32[512,256]{1,0:T(8,128)S(1)} %fusion.8), channel_id=1, source_target_pairs={{0,2},{1,3},{2,0},{3,1},{4,6},{5,7},{6,4},{7,5},{8,10},{9,11},{10,... | collective-permute-start | bytes 1572872 | tf_op jit(solution)/shard_map/ppermute | solution.py:177
  46.6 2.0 %collective-permute-start.9 = (f32[512,256]{1,0:T(8,128)S(1)}, f32[512,256]{1,0:T(8,128)S(1)}, u32[]{:S(2)}, u32[]{:S(2)}) collective-permute-start(f32[512,256]{1,0:T(8,128)S(1)} %fusion.refs_0_), channel_id=1, source_target_pairs={{0,1},{1,0},{2,3},{3,2},{4,5},{5,4},{6,7},{7,6},{8,9},{9,8},{10,11... | collective-permute-start | bytes 1572872 | tf_op jit(solution)/shard_map/ppermute | solution.py:177
  48.5 8.4 %collective-permute-done.3 = f32[512,256]{1,0:T(8,128)S(1)} collective-permute-done((f32[512,256]{1,0:T(8,128)S(1)}, f32[512,256]{1,0:T(8,128)S(1)}, u32[]{:S(2)}, u32[]{:S(2)}) %collective-permute-start.3) | collective-permute-done | bytes 524320 | tf_op jit(solution)/shard_map/ppermute | solution.py:177
  58.6 4.0 %shard_map.82 = (bf16[64,1792]{1,0:T(8,128)(2,1)S(1)}, bf16[64,1792]{1,0:T(8,128)(2,1)S(1)}, bf16[64,1792]{1,0:T(8,128)(2,1)S(1)}, bf16[64,1792]{1,0:T(8,128)(2,1)S(1)}) custom-call(s32[2]{0:T(128)S(1)} %pad_add_fusion.index_ref, bf16[512,256]{1,0:T(8,128)(2,1)S(1)} %add_convert_fusion.1.own_ref, bf16[512,256]{1,0:T(8,128)(2,1)S(1)} %collective-permute-done.4.other_ref, ...), custom_call_target="tpu_custom_call" | custom-call | flops 939524096 | bytes 3670016 | tf_op jit(solution)/shard_map/pallas_call | solution.py:213
  65.2 2.0 %collective-permute-start.14 = (bf16[64,1792]{1,0:T(8,128)(2,1)S(1)}, bf16[64,1792]{1,0:T(8,128)(2,1)S(1)}, u32[]{:S(2)}, u32[]{:S(2)}) collective-permute-start(bf16[64,1792]{1,0:T(8,128)(2,1)S(1)} %get-tuple-element.38), channel_id=1, source_target_pairs={{0,8},{1,9},{2,10},{3,11},{4,12},{5,13},{6,14},{7,15},{8,0},{9,1},... | collective-permute-start | bytes 688136 | tf_op jit(solution)/shard_map/ppermute | solution.py:69
  67.2 3.9 %shard_map.78 = (bf16[64,1792]{1,0:T(8,128)(2,1)S(1)}, bf16[64,1792]{1,0:T(8,128)(2,1)S(1)}, bf16[64,1792]{1,0:T(8,128)(2,1)S(1)}, bf16[64,1792]{1,0:T(8,128)(2,1)S(1)}) custom-call(s32[2]{0:T(128)S(1)} %pad_add_fusion.index_ref, bf16[512,256]{1,0:T(8,128)(2,1)S(1)} %add_convert_fusion.1.own_ref, bf16[512,256]{1,0:T(8,128)(2,1)S(1)} %collective-permute-done.4.other_ref, ...), custom_call_target="tpu_custom_call" | custom-call | flops 939524096 | bytes 3670016 | tf_op jit(solution)/shard_map/pallas_call | solution.py:213
  71.2 2.0 %collective-permute-start.8 = (bf16[64,1792]{1,0:T(8,128)(2,1)S(1)}, bf16[64,1792]{1,0:T(8,128)(2,1)S(1)}, u32[]{:S(2)}, u32[]{:S(2)}) collective-permute-start(bf16[64,1792]{1,0:T(8,128)(2,1)S(1)} %get-tuple-element.34), channel_id=1, source_target_pairs={{0,8},{1,9},{2,10},{3,11},{4,12},{5,13},{6,14},{7,15},{8,0},{9,1},... | collective-permute-start | bytes 688136 | tf_op jit(solution)/shard_map/ppermute | solution.py:69
  74.8 2.7 %collective-permute-done.10 = f32[512,256]{1,0:T(8,128)S(1)} collective-permute-done((f32[512,256]{1,0:T(8,128)S(1)}, f32[512,256]{1,0:T(8,128)S(1)}, u32[]{:S(2)}, u32[]{:S(2)}) %collective-permute-start.10) | collective-permute-done | bytes 524320 | tf_op jit(solution)/shard_map/ppermute | solution.py:177
  77.6 1.9 %collective-permute-done.16.refs_2_ = bf16[64,1792]{1,0:T(8,128)(2,1)S(1)} collective-permute-done((bf16[64,1792]{1,0:T(8,128)(2,1)S(1)}, bf16[64,1792]{1,0:T(8,128)(2,1)S(1)}, u32[]{:S(2)}, u32[]{:S(2)}) %collective-permute-start.16) | collective-permute-done | bytes 229408 | tf_op jit(solution)/shard_map/ppermute | solution.py:69
  80.7 3.9 %shard_map.80 = (bf16[64,1792]{1,0:T(8,128)(2,1)S(1)}, bf16[64,1792]{1,0:T(8,128)(2,1)S(1)}, bf16[64,1792]{1,0:T(8,128)(2,1)S(1)}, bf16[64,1792]{1,0:T(8,128)(2,1)S(1)}) custom-call(s32[2]{0:T(128)S(1)} %pad_add_fusion.index_ref, bf16[512,256]{1,0:T(8,128)(2,1)S(1)} %add_convert_fusion.own_ref, bf16[512,256]{1,0:T(8,128)(2,1)S(1)} %collective-permute-done.11.other_ref, ...), custom_call_target="tpu_custom_call" | custom-call | flops 939524096 | bytes 3670016 | tf_op jit(solution)/shard_map/pallas_call | solution.py:213
  86.2 3.8 %shard_map.79 = (bf16[64,1792]{1,0:T(8,128)(2,1)S(1)}, bf16[64,1792]{1,0:T(8,128)(2,1)S(1)}, bf16[64,1792]{1,0:T(8,128)(2,1)S(1)}, bf16[64,1792]{1,0:T(8,128)(2,1)S(1)}) custom-call(s32[2]{0:T(128)S(1)} %pad_add_fusion.index_ref, bf16[512,256]{1,0:T(8,128)(2,1)S(1)} %add_convert_fusion.own_ref, bf16[512,256]{1,0:T(8,128)(2,1)S(1)} %collective-permute-done.11.other_ref, ...), custom_call_target="tpu_custom_call" | custom-call | flops 939524096 | bytes 3670016 | tf_op jit(solution)/shard_map/pallas_call | solution.py:213
  93.1 1.9 %collective-permute-start.30 = (bf16[32,1792]{1,0:T(8,128)(2,1)S(1)}, bf16[32,1792]{1,0:T(8,128)(2,1)S(1)}, u32[]{:S(2)}, u32[]{:S(2)}) collective-permute-start(bf16[32,1792]{1,0:T(8,128)(2,1)S(1)} %get-tuple-element.52), channel_id=1, source_target_pairs={{0,16},{1,17},{2,18},{3,19},{4,20},{5,21},{6,22},{7,23},{8,24},{9,... | collective-permute-start | bytes 344072 | tf_op jit(solution)/shard_map/ppermute | solution.py:69
  95.0 5.6 %collective-permute-done.30 = bf16[32,1792]{1,0:T(8,128)(2,1)S(1)} collective-permute-done((bf16[32,1792]{1,0:T(8,128)(2,1)S(1)}, bf16[32,1792]{1,0:T(8,128)(2,1)S(1)}, u32[]{:S(2)}, u32[]{:S(2)}) %collective-permute-start.30) | collective-permute-done | bytes 114720 | tf_op jit(solution)/shard_map/ppermute | solution.py:69
  105.8 1.9 %collective-permute-start.28 = (bf16[64,1792]{1,0:T(8,128)(2,1)S(1)}, bf16[64,1792]{1,0:T(8,128)(2,1)S(1)}, u32[]{:S(2)}, u32[]{:S(2)}) collective-permute-start(bf16[64,1792]{1,0:T(8,128)(2,1)S(1)} %add_convert_fusion.2), channel_id=1, source_target_pairs={{0,8},{1,9},{2,10},{3,11},{4,12},{5,13},{6,14},{7,15},{8,0},{9,1},... | collective-permute-start | bytes 688136 | tf_op jit(solution)/shard_map/ppermute | solution.py:69
  107.8 5.1 %collective-permute-done.13.refs_3_ = bf16[32,1792]{1,0:T(8,128)(2,1)S(1)} collective-permute-done((bf16[32,1792]{1,0:T(8,128)(2,1)S(1)}, bf16[32,1792]{1,0:T(8,128)(2,1)S(1)}, u32[]{:S(2)}, u32[]{:S(2)}) %collective-permute-start.13) | collective-permute-done | bytes 114720 | tf_op jit(solution)/shard_map/ppermute | solution.py:69
  113.8 3.4 %collective-permute-start.18 = (bf16[32,1792]{1,0:T(8,128)(2,1)S(1)}, bf16[32,1792]{1,0:T(8,128)(2,1)S(1)}, u32[]{:S(2)}, u32[]{:S(2)}) collective-permute-start(bf16[32,1792]{1,0:T(8,128)(2,1)S(1)} %get-tuple-element.43), channel_id=1, source_target_pairs={{0,16},{1,17},{2,18},{3,19},{4,20},{5,21},{6,22},{7,23},{8,24},{9,... | collective-permute-start | bytes 344072 | tf_op jit(solution)/shard_map/ppermute | solution.py:69
  117.2 3.4 %collective-permute-done.18 = bf16[32,1792]{1,0:T(8,128)(2,1)S(1)} collective-permute-done((bf16[32,1792]{1,0:T(8,128)(2,1)S(1)}, bf16[32,1792]{1,0:T(8,128)(2,1)S(1)}, u32[]{:S(2)}, u32[]{:S(2)}) %collective-permute-start.18) | collective-permute-done | bytes 114720 | tf_op jit(solution)/shard_map/ppermute | solution.py:69
  121.4 3.5 %collective-permute-start.24 = (bf16[64,1792]{1,0:T(8,128)(2,1)S(1)}, bf16[64,1792]{1,0:T(8,128)(2,1)S(1)}, u32[]{:S(2)}, u32[]{:S(2)}) collective-permute-start(bf16[64,1792]{1,0:T(8,128)(2,1)S(1)} %add_convert_fusion.3), channel_id=1, source_target_pairs={{0,8},{1,9},{2,10},{3,11},{4,12},{5,13},{6,14},{7,15},{8,0},{9,1},... | collective-permute-start | bytes 688136 | tf_op jit(solution)/shard_map/ppermute | solution.py:69
  127.1 3.5 %collective-permute-done.24.refs_2_ = bf16[64,1792]{1,0:T(8,128)(2,1)S(1)} collective-permute-done((bf16[64,1792]{1,0:T(8,128)(2,1)S(1)}, bf16[64,1792]{1,0:T(8,128)(2,1)S(1)}, u32[]{:S(2)}, u32[]{:S(2)}) %collective-permute-start.24) | collective-permute-done | bytes 229408 | tf_op jit(solution)/shard_map/ppermute | solution.py:69
  132.3 2.0 %collective-permute-done.19.refs_8_.refs_1_ = bf16[64,1792]{1,0:T(8,128)(2,1)S(1)} collective-permute-done((bf16[64,1792]{1,0:T(8,128)(2,1)S(1)}, bf16[64,1792]{1,0:T(8,128)(2,1)S(1)}, u32[]{:S(2)}, u32[]{:S(2)}) %collective-permute-start.19) | collective-permute-done | bytes 229408 | tf_op jit(solution)/shard_map/ppermute | solution.py:69
  135.0 2.0 %collective-permute-start.25 = (bf16[32,1792]{1,0:T(8,128)(2,1)S(1)}, bf16[32,1792]{1,0:T(8,128)(2,1)S(1)}, u32[]{:S(2)}, u32[]{:S(2)}) collective-permute-start(bf16[32,1792]{1,0:T(8,128)(2,1)S(1)} %add_convert_fusion.6), channel_id=1, source_target_pairs={{0,16},{1,17},{2,18},{3,19},{4,20},{5,21},{6,22},{7,23},{8,24},{9,... | collective-permute-start | bytes 344072 | tf_op jit(solution)/shard_map/ppermute | solution.py:69
  137.0 2.8 %collective-permute-done.29.refs_3_ = bf16[32,1792]{1,0:T(8,128)(2,1)S(1)} collective-permute-done((bf16[32,1792]{1,0:T(8,128)(2,1)S(1)}, bf16[32,1792]{1,0:T(8,128)(2,1)S(1)}, u32[]{:S(2)}, u32[]{:S(2)}) %collective-permute-start.29) | collective-permute-done | bytes 114720 | tf_op jit(solution)/shard_map/ppermute | solution.py:69
  146.7 3.7 %collective-permute-done.34 = bf16[32,1792]{1,0:T(8,128)(2,1)S(1)} collective-permute-done((bf16[32,1792]{1,0:T(8,128)(2,1)S(1)}, bf16[32,1792]{1,0:T(8,128)(2,1)S(1)}, u32[]{:S(2)}, u32[]{:S(2)}) %collective-permute-start.34) | collective-permute-done | bytes 114720 | tf_op jit(solution)/shard_map/ppermute | solution.py:69
  150.9 1.8 %collective-permute-done.39.refs_5_ = bf16[64,1792]{1,0:T(8,128)(2,1)S(1)} collective-permute-done((bf16[64,1792]{1,0:T(8,128)(2,1)S(1)}, bf16[64,1792]{1,0:T(8,128)(2,1)S(1)}, u32[]{:S(2)}, u32[]{:S(2)}) %collective-permute-start.39) | collective-permute-done | bytes 229408 | tf_op jit(solution)/shard_map/ppermute | solution.py:69
  156.5 2.5 %collective-permute-done.41.refs_7_ = bf16[64,1792]{1,0:T(8,128)(2,1)S(1)} collective-permute-done((bf16[64,1792]{1,0:T(8,128)(2,1)S(1)}, bf16[64,1792]{1,0:T(8,128)(2,1)S(1)}, u32[]{:S(2)}, u32[]{:S(2)}) %collective-permute-start.41) | collective-permute-done | bytes 229408 | tf_op jit(solution)/shard_map/ppermute | solution.py:69
  159.0 4.7 %shard_map.88.refs_9_ = bf16[1024,3584]{1,0:T(8,128)(2,1)} custom-call(s32[2]{0:T(128)S(1)} %pad_add_fusion.index_ref, bf16[64,1792]{1,0:T(8,128)(2,1)S(1)} %constant_dynamic-update-slice_fusion.2.refs_0_, bf16[64,1792]{1,0:T(8,128)(2,1)S(1)} %collective-permute-done.31.refs_8_.refs_1_, bf16[64,1792]{1,0:T(8,128)(2,1)S(1)} %collective-permute-done.32.refs_9_.refs_2_, ...), custom_call_target="tpu_custom_call" | custom-call | flops 1879048192 | bytes 3670016 | tf_op jit(solution)/shard_map/pallas_call | solution.py:293
  163.9 4.7 %shard_map.89 = bf16[1024,3584]{1,0:T(8,128)(2,1)} custom-call(s32[2]{0:T(128)S(1)} %pad_add_fusion.index_ref, bf16[64,1792]{1,0:T(8,128)(2,1)S(1)} %constant_dynamic-update-slice_fusion.refs_0_, bf16[64,1792]{1,0:T(8,128)(2,1)S(1)} %collective-permute-done.19.refs_8_.refs_1_, ...), custom_call_target="tpu_custom_call", output_to_operand_aliasing={{}: (10, {})} | custom-call | flops 1879048192 | bytes 3670016 | tf_op jit(solution)/shard_map/pallas_call | solution.py:293
  (96 shorter events, 40.9 us)
Async XLA Ops:
  3.0 10.2 %collective-permute-start.1 = (bf16[1024,256]{1,0:T(8,128)(2,1)S(1)}, bf16[1024,256]{1,0:T(8,128)(2,1)S(1)}, u32[]{:S(2)}, u32[]{:S(2)}) collective-permute-start(bf16[1024,256]{1,0:T(8,128)(2,1)S(1)} %collective-permute-done.refs_0_), channel_id=1, source_target_pairs={{0,4},{1,5},{2,6},{3,7},{4,0},{5,1},{6,2},{7,3},{8,12},{9,13},{10,... | collective-permute-start | bytes 1572872 | tf_op jit(solution)/shard_map/ppermute | solution.py:69
  6.5 23.5 %collective-permute-start.5 = (bf16[1024,256]{1,0:T(8,128)(2,1)S(1)}, bf16[1024,256]{1,0:T(8,128)(2,1)S(1)}, u32[]{:S(2)}, u32[]{:S(2)}) collective-permute-start(bf16[1024,256]{1,0:T(8,128)(2,1)S(1)} %shard_map.77), channel_id=1, source_target_pairs={{0,0},{10,1},{16,2},{26,3},{4,4},{14,5},{20,6},{30,7},{2,8},{8,9},... | collective-permute-start | bytes 1572872 | tf_op jit(solution)/shard_map/ppermute | solution.py:141
  16.3 15.5 %collective-permute-start.2 = (f32[512,256]{1,0:T(8,128)}, f32[512,256]{1,0:T(8,128)}, u32[]{:S(2)}, u32[]{:S(2)}) collective-permute-start(f32[512,256]{1,0:T(8,128)} %fusion.2), channel_id=1, source_target_pairs={{0,1},{1,0},{2,3},{3,2},{4,5},{5,4},{6,7},{7,6},{8,9},{9,8},{10,11... | collective-permute-start | bytes 1572872 | tf_op jit(solution)/shard_map/ppermute | solution.py:177
  30.0 15.9 %collective-permute-start.6 = (bf16[1024,256]{1,0:T(8,128)(2,1)S(1)}, bf16[1024,256]{1,0:T(8,128)(2,1)S(1)}, u32[]{:S(2)}, u32[]{:S(2)}) collective-permute-start(bf16[1024,256]{1,0:T(8,128)(2,1)S(1)} %collective-permute-done.5), channel_id=1, source_target_pairs={{0,4},{1,5},{2,6},{3,7},{4,0},{5,1},{6,2},{7,3},{8,12},{9,13},{10,... | collective-permute-start | bytes 1572872 | tf_op jit(solution)/shard_map/ppermute | solution.py:69
  34.3 22.6 %collective-permute-start.3 = (f32[512,256]{1,0:T(8,128)S(1)}, f32[512,256]{1,0:T(8,128)S(1)}, u32[]{:S(2)}, u32[]{:S(2)}) collective-permute-start(f32[512,256]{1,0:T(8,128)S(1)} %fusion.8), channel_id=1, source_target_pairs={{0,2},{1,3},{2,0},{3,1},{4,6},{5,7},{6,4},{7,5},{8,10},{9,11},{10,... | collective-permute-start | bytes 1572872 | tf_op jit(solution)/shard_map/ppermute | solution.py:177
  46.6 16.1 %collective-permute-start.9 = (f32[512,256]{1,0:T(8,128)S(1)}, f32[512,256]{1,0:T(8,128)S(1)}, u32[]{:S(2)}, u32[]{:S(2)}) collective-permute-start(f32[512,256]{1,0:T(8,128)S(1)} %fusion.refs_0_), channel_id=1, source_target_pairs={{0,1},{1,0},{2,3},{3,2},{4,5},{5,4},{6,7},{7,6},{8,9},{9,8},{10,11... | collective-permute-start | bytes 1572872 | tf_op jit(solution)/shard_map/ppermute | solution.py:177
  62.6 10.6 %collective-permute-start.15 = (bf16[64,1792]{1,0:T(8,128)(2,1)S(1)}, bf16[64,1792]{1,0:T(8,128)(2,1)S(1)}, u32[]{:S(2)}, u32[]{:S(2)}) collective-permute-start(bf16[64,1792]{1,0:T(8,128)(2,1)S(1)} %get-tuple-element.40), channel_id=1, source_target_pairs={{0,8},{1,9},{2,10},{3,11},{4,12},{5,13},{6,14},{7,15},{8,0},{9,1},... | collective-permute-start | bytes 688136 | tf_op jit(solution)/shard_map/ppermute | solution.py:69
  63.4 14.0 %collective-permute-start.10 = (f32[512,256]{1,0:T(8,128)S(1)}, f32[512,256]{1,0:T(8,128)S(1)}, u32[]{:S(2)}, u32[]{:S(2)}) collective-permute-start(f32[512,256]{1,0:T(8,128)S(1)} %fusion.11), channel_id=1, source_target_pairs={{0,2},{1,3},{2,0},{3,1},{4,6},{5,7},{6,4},{7,5},{8,10},{9,11},{10,... | collective-permute-start | bytes 1572872 | tf_op jit(solution)/shard_map/ppermute | solution.py:177
  65.2 12.4 %collective-permute-start.14 = (bf16[64,1792]{1,0:T(8,128)(2,1)S(1)}, bf16[64,1792]{1,0:T(8,128)(2,1)S(1)}, u32[]{:S(2)}, u32[]{:S(2)}) collective-permute-start(bf16[64,1792]{1,0:T(8,128)(2,1)S(1)} %get-tuple-element.38), channel_id=1, source_target_pairs={{0,8},{1,9},{2,10},{3,11},{4,12},{5,13},{6,14},{7,15},{8,0},{9,1},... | collective-permute-start | bytes 688136 | tf_op jit(solution)/shard_map/ppermute | solution.py:69
  71.1 30.1 %collective-permute-start.7 = (bf16[64,1792]{1,0:T(8,128)(2,1)S(1)}, bf16[64,1792]{1,0:T(8,128)(2,1)S(1)}, u32[]{:S(2)}, u32[]{:S(2)}) collective-permute-start(bf16[64,1792]{1,0:T(8,128)(2,1)S(1)} %get-tuple-element.32), channel_id=1, source_target_pairs={{0,8},{1,9},{2,10},{3,11},{4,12},{5,13},{6,14},{7,15},{8,0},{9,1},... | collective-permute-start | bytes 688136 | tf_op jit(solution)/shard_map/ppermute | solution.py:69
  71.2 19.4 %collective-permute-start.8 = (bf16[64,1792]{1,0:T(8,128)(2,1)S(1)}, bf16[64,1792]{1,0:T(8,128)(2,1)S(1)}, u32[]{:S(2)}, u32[]{:S(2)}) collective-permute-start(bf16[64,1792]{1,0:T(8,128)(2,1)S(1)} %get-tuple-element.34), channel_id=1, source_target_pairs={{0,8},{1,9},{2,10},{3,11},{4,12},{5,13},{6,14},{7,15},{8,0},{9,1},... | collective-permute-start | bytes 688136 | tf_op jit(solution)/shard_map/ppermute | solution.py:69
  79.6 12.6 %collective-permute-start.17 = (bf16[32,1792]{1,0:T(8,128)(2,1)S(1)}, bf16[32,1792]{1,0:T(8,128)(2,1)S(1)}, u32[]{:S(2)}, u32[]{:S(2)}) collective-permute-start(bf16[32,1792]{1,0:T(8,128)(2,1)S(1)} %add_convert_fusion.7), channel_id=1, source_target_pairs={{0,16},{1,17},{2,18},{3,19},{4,20},{5,21},{6,22},{7,23},{8,24},{9,... | collective-permute-start | bytes 344072 | tf_op jit(solution)/shard_map/ppermute | solution.py:69
  84.6 21.2 %collective-permute-start.23 = (bf16[64,1792]{1,0:T(8,128)(2,1)S(1)}, bf16[64,1792]{1,0:T(8,128)(2,1)S(1)}, u32[]{:S(2)}, u32[]{:S(2)}) collective-permute-start(bf16[64,1792]{1,0:T(8,128)(2,1)S(1)} %get-tuple-element.36.refs_1_), channel_id=1, source_target_pairs={{0,4},{1,5},{2,6},{3,7},{4,0},{5,1},{6,2},{7,3},{8,12},{9,13},{10,... | collective-permute-start | bytes 688136 | tf_op jit(solution)/shard_map/ppermute | solution.py:69
  90.0 14.4 %collective-permute-start.27 = (bf16[64,1792]{1,0:T(8,128)(2,1)S(1)}, bf16[64,1792]{1,0:T(8,128)(2,1)S(1)}, u32[]{:S(2)}, u32[]{:S(2)}) collective-permute-start(bf16[64,1792]{1,0:T(8,128)(2,1)S(1)} %get-tuple-element.35.refs_0_), channel_id=1, source_target_pairs={{0,4},{1,5},{2,6},{3,7},{4,0},{5,1},{6,2},{7,3},{8,12},{9,13},{10,... | collective-permute-start | bytes 688136 | tf_op jit(solution)/shard_map/ppermute | solution.py:69
  90.7 12.1 %collective-permute-start.12 = (bf16[64,1792]{1,0:T(8,128)(2,1)S(1)}, bf16[64,1792]{1,0:T(8,128)(2,1)S(1)}, u32[]{:S(2)}, u32[]{:S(2)}) collective-permute-start(bf16[64,1792]{1,0:T(8,128)(2,1)S(1)} %shard_map.81), channel_id=1, source_target_pairs={{0,4},{1,5},{2,6},{3,7},{4,0},{5,1},{6,2},{7,3},{8,12},{9,13},{10,... | collective-permute-start | bytes 688136 | tf_op jit(solution)/shard_map/ppermute | solution.py:69
  93.1 7.5 %collective-permute-start.30 = (bf16[32,1792]{1,0:T(8,128)(2,1)S(1)}, bf16[32,1792]{1,0:T(8,128)(2,1)S(1)}, u32[]{:S(2)}, u32[]{:S(2)}) collective-permute-start(bf16[32,1792]{1,0:T(8,128)(2,1)S(1)} %get-tuple-element.52), channel_id=1, source_target_pairs={{0,16},{1,17},{2,18},{3,19},{4,20},{5,21},{6,22},{7,23},{8,24},{9,... | collective-permute-start | bytes 344072 | tf_op jit(solution)/shard_map/ppermute | solution.py:69
  100.6 25.2 %collective-permute-start.22 = (bf16[64,1792]{1,0:T(8,128)(2,1)S(1)}, bf16[64,1792]{1,0:T(8,128)(2,1)S(1)}, u32[]{:S(2)}, u32[]{:S(2)}) collective-permute-start(bf16[64,1792]{1,0:T(8,128)(2,1)S(1)} %get-tuple-element.45), channel_id=1, source_target_pairs={{0,4},{1,5},{2,6},{3,7},{4,0},{5,1},{6,2},{7,3},{8,12},{9,13},{10,... | collective-permute-start | bytes 688136 | tf_op jit(solution)/shard_map/ppermute | solution.py:69
  101.2 20.2 %collective-permute-start.26 = (bf16[64,1792]{1,0:T(8,128)(2,1)S(1)}, bf16[64,1792]{1,0:T(8,128)(2,1)S(1)}, u32[]{:S(2)}, u32[]{:S(2)}) collective-permute-start(bf16[64,1792]{1,0:T(8,128)(2,1)S(1)} %get-tuple-element.48), channel_id=1, source_target_pairs={{0,4},{1,5},{2,6},{3,7},{4,0},{5,1},{6,2},{7,3},{8,12},{9,13},{10,... | collective-permute-start | bytes 688136 | tf_op jit(solution)/shard_map/ppermute | solution.py:69
  102.8 22.1 %collective-permute-start.31 = (bf16[64,1792]{1,0:T(8,128)(2,1)S(1)}, bf16[64,1792]{1,0:T(8,128)(2,1)S(1)}, u32[]{:S(2)}, u32[]{:S(2)}) collective-permute-start(bf16[64,1792]{1,0:T(8,128)(2,1)S(1)} %constant_dynamic-update-slice_fusion.2.refs_0_), channel_id=1, source_target_pairs={{0,8},{1,9},{2,10},{3,11},{4,12},{5,13},{6,14},{7,15},{8,0},{9,1},... | collective-permute-start | bytes 688136 | tf_op jit(solution)/shard_map/ppermute | solution.py:69
  104.4 8.5 %collective-permute-start.13 = (bf16[32,1792]{1,0:T(8,128)(2,1)S(1)}, bf16[32,1792]{1,0:T(8,128)(2,1)S(1)}, u32[]{:S(2)}, u32[]{:S(2)}) collective-permute-start(bf16[32,1792]{1,0:T(8,128)(2,1)S(1)} %add_convert_fusion.8), channel_id=1, source_target_pairs={{0,16},{1,17},{2,18},{3,19},{4,20},{5,21},{6,22},{7,23},{8,24},{9,... | collective-permute-start | bytes 344072 | tf_op jit(solution)/shard_map/ppermute | solution.py:69
  105.8 19.9 %collective-permute-start.28 = (bf16[64,1792]{1,0:T(8,128)(2,1)S(1)}, bf16[64,1792]{1,0:T(8,128)(2,1)S(1)}, u32[]{:S(2)}, u32[]{:S(2)}) collective-permute-start(bf16[64,1792]{1,0:T(8,128)(2,1)S(1)} %add_convert_fusion.2), channel_id=1, source_target_pairs={{0,8},{1,9},{2,10},{3,11},{4,12},{5,13},{6,14},{7,15},{8,0},{9,1},... | collective-permute-start | bytes 688136 | tf_op jit(solution)/shard_map/ppermute | solution.py:69
  120.5 14.4 %collective-permute-start.32 = (bf16[64,1792]{1,0:T(8,128)(2,1)S(1)}, bf16[64,1792]{1,0:T(8,128)(2,1)S(1)}, u32[]{:S(2)}, u32[]{:S(2)}) collective-permute-start(bf16[64,1792]{1,0:T(8,128)(2,1)S(1)} %constant_dynamic-update-slice_fusion.2.refs_0_), channel_id=1, source_target_pairs={{0,4},{1,5},{2,6},{3,7},{4,0},{5,1},{6,2},{7,3},{8,12},{9,13},{10,... | collective-permute-start | bytes 688136 | tf_op jit(solution)/shard_map/ppermute | solution.py:69
  121.4 9.3 %collective-permute-start.24 = (bf16[64,1792]{1,0:T(8,128)(2,1)S(1)}, bf16[64,1792]{1,0:T(8,128)(2,1)S(1)}, u32[]{:S(2)}, u32[]{:S(2)}) collective-permute-start(bf16[64,1792]{1,0:T(8,128)(2,1)S(1)} %add_convert_fusion.3), channel_id=1, source_target_pairs={{0,8},{1,9},{2,10},{3,11},{4,12},{5,13},{6,14},{7,15},{8,0},{9,1},... | collective-permute-start | bytes 688136 | tf_op jit(solution)/shard_map/ppermute | solution.py:69
  124.8 15.0 %collective-permute-start.33 = (bf16[64,1792]{1,0:T(8,128)(2,1)S(1)}, bf16[64,1792]{1,0:T(8,128)(2,1)S(1)}, u32[]{:S(2)}, u32[]{:S(2)}) collective-permute-start(bf16[64,1792]{1,0:T(8,128)(2,1)S(1)} %collective-permute-done.31.refs_8_.refs_1_), channel_id=1, source_target_pairs={{0,4},{1,5},{2,6},{3,7},{4,0},{5,1},{6,2},{7,3},{8,12},{9,13},{10,... | collective-permute-start | bytes 688136 | tf_op jit(solution)/shard_map/ppermute | solution.py:69
  125.7 8.6 %collective-permute-start.19 = (bf16[64,1792]{1,0:T(8,128)(2,1)S(1)}, bf16[64,1792]{1,0:T(8,128)(2,1)S(1)}, u32[]{:S(2)}, u32[]{:S(2)}) collective-permute-start(bf16[64,1792]{1,0:T(8,128)(2,1)S(1)} %constant_dynamic-update-slice_fusion.refs_0_), channel_id=1, source_target_pairs={{0,8},{1,9},{2,10},{3,11},{4,12},{5,13},{6,14},{7,15},{8,0},{9,1},... | collective-permute-start | bytes 688136 | tf_op jit(solution)/shard_map/ppermute | solution.py:69
  125.8 16.7 %collective-permute-start.20 = (bf16[64,1792]{1,0:T(8,128)(2,1)S(1)}, bf16[64,1792]{1,0:T(8,128)(2,1)S(1)}, u32[]{:S(2)}, u32[]{:S(2)}) collective-permute-start(bf16[64,1792]{1,0:T(8,128)(2,1)S(1)} %constant_dynamic-update-slice_fusion.refs_0_), channel_id=1, source_target_pairs={{0,4},{1,5},{2,6},{3,7},{4,0},{5,1},{6,2},{7,3},{8,12},{9,13},{10,... | collective-permute-start | bytes 688136 | tf_op jit(solution)/shard_map/ppermute | solution.py:69
  130.6 9.2 %collective-permute-start.29 = (bf16[32,1792]{1,0:T(8,128)(2,1)S(1)}, bf16[32,1792]{1,0:T(8,128)(2,1)S(1)}, u32[]{:S(2)}, u32[]{:S(2)}) collective-permute-start(bf16[32,1792]{1,0:T(8,128)(2,1)S(1)} %add_convert_fusion.5), channel_id=1, source_target_pairs={{0,16},{1,17},{2,18},{3,19},{4,20},{5,21},{6,22},{7,23},{8,24},{9,... | collective-permute-start | bytes 344072 | tf_op jit(solution)/shard_map/ppermute | solution.py:69
  134.3 8.2 %collective-permute-start.21 = (bf16[64,1792]{1,0:T(8,128)(2,1)S(1)}, bf16[64,1792]{1,0:T(8,128)(2,1)S(1)}, u32[]{:S(2)}, u32[]{:S(2)}) collective-permute-start(bf16[64,1792]{1,0:T(8,128)(2,1)S(1)} %collective-permute-done.19.refs_8_.refs_1_), channel_id=1, source_target_pairs={{0,4},{1,5},{2,6},{3,7},{4,0},{5,1},{6,2},{7,3},{8,12},{9,13},{10,... | collective-permute-start | bytes 688136 | tf_op jit(solution)/shard_map/ppermute | solution.py:69
  135.0 7.5 %collective-permute-start.25 = (bf16[32,1792]{1,0:T(8,128)(2,1)S(1)}, bf16[32,1792]{1,0:T(8,128)(2,1)S(1)}, u32[]{:S(2)}, u32[]{:S(2)}) collective-permute-start(bf16[32,1792]{1,0:T(8,128)(2,1)S(1)} %add_convert_fusion.6), channel_id=1, source_target_pairs={{0,16},{1,17},{2,18},{3,19},{4,20},{5,21},{6,22},{7,23},{8,24},{9,... | collective-permute-start | bytes 344072 | tf_op jit(solution)/shard_map/ppermute | solution.py:69
  143.4 6.9 %collective-permute-start.34 = (bf16[32,1792]{1,0:T(8,128)(2,1)S(1)}, bf16[32,1792]{1,0:T(8,128)(2,1)S(1)}, u32[]{:S(2)}, u32[]{:S(2)}) collective-permute-start(bf16[32,1792]{1,0:T(8,128)(2,1)S(1)} %get-tuple-element.55.refs_0_), channel_id=1, source_target_pairs={{0,16},{1,17},{2,18},{3,19},{4,20},{5,21},{6,22},{7,23},{8,24},{9,... | collective-permute-start | bytes 344072 | tf_op jit(solution)/shard_map/ppermute | solution.py:69
  153.9 9.7 %collective-permute-start.36 = (bf16[64,1792]{1,0:T(8,128)(2,1)S(1)}, bf16[64,1792]{1,0:T(8,128)(2,1)S(1)}, u32[]{:S(2)}, u32[]{:S(2)}) collective-permute-start(bf16[64,1792]{1,0:T(8,128)(2,1)S(1)} %constant_dynamic-update-slice_fusion.4.refs_4_), channel_id=1, source_target_pairs={{0,4},{1,5},{2,6},{3,7},{4,0},{5,1},{6,2},{7,3},{8,12},{9,13},{10,... | collective-permute-start | bytes 688136 | tf_op jit(solution)/shard_map/ppermute | solution.py:69
  156.4 7.5 %collective-permute-start.37 = (bf16[64,1792]{1,0:T(8,128)(2,1)S(1)}, bf16[64,1792]{1,0:T(8,128)(2,1)S(1)}, u32[]{:S(2)}, u32[]{:S(2)}) collective-permute-start(bf16[64,1792]{1,0:T(8,128)(2,1)S(1)} %collective-permute-done.35.refs_5_), channel_id=1, source_target_pairs={{0,4},{1,5},{2,6},{3,7},{4,0},{5,1},{6,2},{7,3},{8,12},{9,13},{10,... | collective-permute-start | bytes 688136 | tf_op jit(solution)/shard_map/ppermute | solution.py:69
  (15 other events, 85.4 us)

commit v5 on v4

--- a/solution.py
+++ b/solution.py
@@ -181,7 +181,7 @@
     for j in range(1, half):
         total = total + move(chip, 0, j)
     own = total.astype(BF16)
-    return own, move(own, 1, 0)
+    return own, move(own, 1, 0), chip
 
 
 def grad_rows(cube, index, pieces, out_grads, order, first_column, columns, wait_for):
@@ -337,9 +337,9 @@
             for f in range(HALVES):
                 wait_for = []
                 if h + 1 < parts:
-                    wait_for = [partial[h + 1][0]]
+                    wait_for = [projected[h + 1][2]]
                 quarters[h, f] = grad_rows(
-                    cube, index, projected[h], out_grads, sum_order[h, f], f * columns, columns, wait_for
+                    cube, index, projected[h][:2], out_grads, sum_order[h, f], f * columns, columns, wait_for
                 )
         for h in range(parts):
             for f in range(HALVES):

time: 169 us -> 167 us (0.988)
  waiting for transfers between devices: 56.7 us -> 48.2 us
  starting transfers between devices: 72.7 us -> 79.7 us
    ppermute x34, waiting for transfers between devices: 43.8 us -> 35.4 us  [swap(): return lax.ppermute(value, AXES, pairs)]
    ppermute x34, starting transfers between devices: 42.1 us -> 49.3 us  [swap(): return lax.ppermute(value, AXES, pairs)]
  transfers between devices with their start and end apart: 42 -> 42, of which waited for: 20 -> 18; matrix products, arithmetic and copies ran while one was open for 5% -> 5% of each run, Pallas kernels for 14% -> 12%
where the time goes in v5:
time: 167 us
  starting transfers between devices  79.7 us (48%)
  waiting for transfers between devices  48.2 us (29%)
  Pallas kernels  29.4 us (18%)
  matrix products  7.2 us (4%)
    ppermute x34, starting transfers between devices, swap(): return lax.ppermute(value, AXES, pairs)  49.3 us
    ppermute x34, waiting for transfers between devices, swap(): return lax.ppermute(value, AXES, pairs)  35.4 us
    ppermute x6, starting transfers between devices, move(): return lax.ppermute(value, AXES, pairs)  28.9 us
    pallas_call x4, Pallas kernels, grad_rows(): pl.pallas_call(kernel, grid_spec=pltpu.PrefetchScalarGridSpec(num_scalar_...  15.6 us
    ppermute x6, waiting for transfers between devices, move(): return lax.ppermute(value, AXES, pairs)  12.8 us
    pallas_call x2, Pallas kernels, make_update(): pl.pallas_call(kernel, grid_spec=pltpu.PrefetchScalarGridSpec(num_scalar_...  9.33 us
    dot_general x4, matrix products, half(): return jnp.dot(own, held, preferred_element_type=F32)  7.2 us
    pallas_call x4, Pallas kernels, adam(): pl.pallas_call(kernel, grid=(1,), in_specs=term_specs + [moment_spec] * 2...  3.55 us
  transfers between devices with their start and end apart: 42, of which 18 were waited for; matrix products, arithmetic and copies ran while one was open for 5% of the time, Pallas kernels for 12%

profile of v5, /device:TPU:0, one launch (start us, length us, event | category | flops | bytes accessed | tf_op | source)
XLA Modules:
  0.0 167.3 jit_solution(8360368234321384170)
XLA Ops:
  3.0 3.0 %collective-permute-start.1 = (bf16[1024,256]{1,0:T(8,128)(2,1)S(1)}, bf16[1024,256]{1,0:T(8,128)(2,1)S(1)}, u32[]{:S(2)}, u32[]{:S(2)}) collective-permute-start(bf16[1024,256]{1,0:T(8,128)(2,1)S(1)} %collective-permute-done.refs_0_), channel_id=1, source_target_pairs={{0,4},{1,5},{2,6},{3,7},{4,0},{5,1},{6,2},{7,3},{8,12},{9,13},{10,... | collective-permute-start | bytes 1572872 | tf_op jit(solution)/shard_map/ppermute | solution.py:69
  7.2 6.0 %collective-permute-done.1 = bf16[1024,256]{1,0:T(8,128)(2,1)S(1)} collective-permute-done((bf16[1024,256]{1,0:T(8,128)(2,1)S(1)}, bf16[1024,256]{1,0:T(8,128)(2,1)S(1)}, u32[]{:S(2)}, u32[]{:S(2)}) %collective-permute-start.1) | collective-permute-done | bytes 524320 | tf_op jit(solution)/shard_map/ppermute | solution.py:69
  13.2 3.1 %fusion.2 = f32[512,256]{1,0:T(8,128)} fusion(bf16[1024,2048]{1,0:T(8,128)(2,1)} %param.5, s32[]{:T(128)S(6)} %select_n.42, bf16[1024,256]{1,0:T(8,128)(2,1)S(1)} %collective-permute-done.1, bf16[1024,256]{1,0:T(8,128)(2,1)S(1)} %collective-permute-done.refs_0_, pred[]{:T(512)S(6)} %eq.10), kind=kOutput, calls=%fused_computation.2 | convolution fusion | flops 541589504 | bytes 3670021 | tf_op jit(solution)/shard_map/dot_general | solution.py:162
  16.3 13.6 %collective-permute-start.2 = (f32[512,256]{1,0:T(8,128)}, f32[512,256]{1,0:T(8,128)}, u32[]{:S(2)}, u32[]{:S(2)}) collective-permute-start(f32[512,256]{1,0:T(8,128)} %fusion.2), channel_id=1, source_target_pairs={{0,1},{1,0},{2,3},{3,2},{4,5},{5,4},{6,7},{7,6},{8,9},{9,8},{10,11... | collective-permute-start | bytes 1572872 | tf_op jit(solution)/shard_map/ppermute | solution.py:177
  31.8 2.6 %fusion.8 = f32[512,256]{1,0:T(8,128)S(1)} fusion(f32[512,256]{1,0:T(8,128)} %collective-permute-done.2, bf16[1024,2048]{1,0:T(8,128)(2,1)} %param.5, s32[]{:T(128)S(6)} %select_n.38, bf16[1024,256]{1,0:T(8,128)(2,1)S(1)} %collective-permute-done.1, bf16[1024,256]{1,0:T(8,128)(2,1)S(1)} %collective-permute-done.refs_0_, pred[]{:T(512)S(6)} %eq.10), kind=kOutput, calls=%fused_computation.8 | convolution fusion | flops 541720576 | bytes 4194309 | tf_op jit(solution)/shard_map/dot_general | solution.py:162
  34.5 11.5 %collective-permute-start.3 = (f32[512,256]{1,0:T(8,128)S(1)}, f32[512,256]{1,0:T(8,128)S(1)}, u32[]{:S(2)}, u32[]{:S(2)}) collective-permute-start(f32[512,256]{1,0:T(8,128)S(1)} %fusion.8), channel_id=1, source_target_pairs={{0,2},{1,3},{2,0},{3,1},{4,6},{5,7},{6,4},{7,5},{8,10},{9,11},{10,... | collective-permute-start | bytes 1572872 | tf_op jit(solution)/shard_map/ppermute | solution.py:177
  48.6 8.6 %collective-permute-done.3 = f32[512,256]{1,0:T(8,128)S(1)} collective-permute-done((f32[512,256]{1,0:T(8,128)S(1)}, f32[512,256]{1,0:T(8,128)S(1)}, u32[]{:S(2)}, u32[]{:S(2)}) %collective-permute-start.3) | collective-permute-done | bytes 524320 | tf_op jit(solution)/shard_map/ppermute | solution.py:177
  58.9 4.0 %shard_map.82 = (bf16[64,1792]{1,0:T(8,128)(2,1)S(1)}, bf16[64,1792]{1,0:T(8,128)(2,1)S(1)}, bf16[64,1792]{1,0:T(8,128)(2,1)S(1)}, bf16[64,1792]{1,0:T(8,128)(2,1)S(1)}) custom-call(s32[2]{0:T(128)S(1)} %pad_add_fusion.index_ref, bf16[512,256]{1,0:T(8,128)(2,1)S(1)} %add_convert_fusion.1.own_ref, bf16[512,256]{1,0:T(8,128)(2,1)S(1)} %collective-permute-done.4.other_ref, ...), custom_call_target="tpu_custom_call" | custom-call | flops 939524096 | bytes 3670016 | tf_op jit(solution)/shard_map/pallas_call | solution.py:213
  64.8 1.9 %collective-permute-start.14 = (bf16[64,1792]{1,0:T(8,128)(2,1)S(1)}, bf16[64,1792]{1,0:T(8,128)(2,1)S(1)}, u32[]{:S(2)}, u32[]{:S(2)}) collective-permute-start(bf16[64,1792]{1,0:T(8,128)(2,1)S(1)} %get-tuple-element.38), channel_id=1, source_target_pairs={{0,8},{1,9},{2,10},{3,11},{4,12},{5,13},{6,14},{7,15},{8,0},{9,1},... | collective-permute-start | bytes 688136 | tf_op jit(solution)/shard_map/ppermute | solution.py:69
  66.8 3.9 %shard_map.78 = (bf16[64,1792]{1,0:T(8,128)(2,1)S(1)}, bf16[64,1792]{1,0:T(8,128)(2,1)S(1)}, bf16[64,1792]{1,0:T(8,128)(2,1)S(1)}, bf16[64,1792]{1,0:T(8,128)(2,1)S(1)}) custom-call(s32[2]{0:T(128)S(1)} %pad_add_fusion.index_ref, bf16[512,256]{1,0:T(8,128)(2,1)S(1)} %add_convert_fusion.1.own_ref, bf16[512,256]{1,0:T(8,128)(2,1)S(1)} %collective-permute-done.4.other_ref, ...), custom_call_target="tpu_custom_call" | custom-call | flops 939524096 | bytes 3670016 | tf_op jit(solution)/shard_map/pallas_call | solution.py:213
  70.8 1.9 %collective-permute-start.9 = (bf16[64,1792]{1,0:T(8,128)(2,1)S(1)}, bf16[64,1792]{1,0:T(8,128)(2,1)S(1)}, u32[]{:S(2)}, u32[]{:S(2)}) collective-permute-start(bf16[64,1792]{1,0:T(8,128)(2,1)S(1)} %get-tuple-element.34), channel_id=1, source_target_pairs={{0,8},{1,9},{2,10},{3,11},{4,12},{5,13},{6,14},{7,15},{8,0},{9,1},... | collective-permute-start | bytes 688136 | tf_op jit(solution)/shard_map/ppermute | solution.py:69
  74.0 3.0 %collective-permute-done.10 = f32[512,256]{1,0:T(8,128)S(1)} collective-permute-done((f32[512,256]{1,0:T(8,128)S(1)}, f32[512,256]{1,0:T(8,128)S(1)}, u32[]{:S(2)}, u32[]{:S(2)}) %collective-permute-start.10) | collective-permute-done | bytes 524320 | tf_op jit(solution)/shard_map/ppermute | solution.py:177
  77.2 1.9 %collective-permute-done.16.refs_2_ = bf16[64,1792]{1,0:T(8,128)(2,1)S(1)} collective-permute-done((bf16[64,1792]{1,0:T(8,128)(2,1)S(1)}, bf16[64,1792]{1,0:T(8,128)(2,1)S(1)}, u32[]{:S(2)}, u32[]{:S(2)}) %collective-permute-start.16) | collective-permute-done | bytes 229408 | tf_op jit(solution)/shard_map/ppermute | solution.py:69
  80.3 3.9 %shard_map.80 = (bf16[64,1792]{1,0:T(8,128)(2,1)S(1)}, bf16[64,1792]{1,0:T(8,128)(2,1)S(1)}, bf16[64,1792]{1,0:T(8,128)(2,1)S(1)}, bf16[64,1792]{1,0:T(8,128)(2,1)S(1)}) custom-call(s32[2]{0:T(128)S(1)} %pad_add_fusion.index_ref, bf16[512,256]{1,0:T(8,128)(2,1)S(1)} %add_convert_fusion.own_ref, bf16[512,256]{1,0:T(8,128)(2,1)S(1)} %collective-permute-done.11.other_ref, ...), custom_call_target="tpu_custom_call" | custom-call | flops 939524096 | bytes 3670016 | tf_op jit(solution)/shard_map/pallas_call | solution.py:213
  85.4 3.8 %shard_map.79 = (bf16[64,1792]{1,0:T(8,128)(2,1)S(1)}, bf16[64,1792]{1,0:T(8,128)(2,1)S(1)}, bf16[64,1792]{1,0:T(8,128)(2,1)S(1)}, bf16[64,1792]{1,0:T(8,128)(2,1)S(1)}) custom-call(s32[2]{0:T(128)S(1)} %pad_add_fusion.index_ref, bf16[512,256]{1,0:T(8,128)(2,1)S(1)} %add_convert_fusion.own_ref, bf16[512,256]{1,0:T(8,128)(2,1)S(1)} %collective-permute-done.11.other_ref, ...), custom_call_target="tpu_custom_call" | custom-call | flops 939524096 | bytes 3670016 | tf_op jit(solution)/shard_map/pallas_call | solution.py:213
  92.4 1.8 %collective-permute-start.30 = (bf16[32,1792]{1,0:T(8,128)(2,1)S(1)}, bf16[32,1792]{1,0:T(8,128)(2,1)S(1)}, u32[]{:S(2)}, u32[]{:S(2)}) collective-permute-start(bf16[32,1792]{1,0:T(8,128)(2,1)S(1)} %get-tuple-element.52), channel_id=1, source_target_pairs={{0,16},{1,17},{2,18},{3,19},{4,20},{5,21},{6,22},{7,23},{8,24},{9,... | collective-permute-start | bytes 344072 | tf_op jit(solution)/shard_map/ppermute | solution.py:69
  94.2 5.7 %collective-permute-done.30 = bf16[32,1792]{1,0:T(8,128)(2,1)S(1)} collective-permute-done((bf16[32,1792]{1,0:T(8,128)(2,1)S(1)}, bf16[32,1792]{1,0:T(8,128)(2,1)S(1)}, u32[]{:S(2)}, u32[]{:S(2)}) %collective-permute-start.30) | collective-permute-done | bytes 114720 | tf_op jit(solution)/shard_map/ppermute | solution.py:69
  106.9 5.2 %collective-permute-done.13.refs_3_ = bf16[32,1792]{1,0:T(8,128)(2,1)S(1)} collective-permute-done((bf16[32,1792]{1,0:T(8,128)(2,1)S(1)}, bf16[32,1792]{1,0:T(8,128)(2,1)S(1)}, u32[]{:S(2)}, u32[]{:S(2)}) %collective-permute-start.13) | collective-permute-done | bytes 114720 | tf_op jit(solution)/shard_map/ppermute | solution.py:69
  113.0 3.4 %collective-permute-start.18 = (bf16[32,1792]{1,0:T(8,128)(2,1)S(1)}, bf16[32,1792]{1,0:T(8,128)(2,1)S(1)}, u32[]{:S(2)}, u32[]{:S(2)}) collective-permute-start(bf16[32,1792]{1,0:T(8,128)(2,1)S(1)} %get-tuple-element.43), channel_id=1, source_target_pairs={{0,16},{1,17},{2,18},{3,19},{4,20},{5,21},{6,22},{7,23},{8,24},{9,... | collective-permute-start | bytes 344072 | tf_op jit(solution)/shard_map/ppermute | solution.py:69
  116.4 3.5 %collective-permute-done.18 = bf16[32,1792]{1,0:T(8,128)(2,1)S(1)} collective-permute-done((bf16[32,1792]{1,0:T(8,128)(2,1)S(1)}, bf16[32,1792]{1,0:T(8,128)(2,1)S(1)}, u32[]{:S(2)}, u32[]{:S(2)}) %collective-permute-start.18) | collective-permute-done | bytes 114720 | tf_op jit(solution)/shard_map/ppermute | solution.py:69
  120.7 3.7 %collective-permute-start.24 = (bf16[64,1792]{1,0:T(8,128)(2,1)S(1)}, bf16[64,1792]{1,0:T(8,128)(2,1)S(1)}, u32[]{:S(2)}, u32[]{:S(2)}) collective-permute-start(bf16[64,1792]{1,0:T(8,128)(2,1)S(1)} %add_convert_fusion.3), channel_id=1, source_target_pairs={{0,8},{1,9},{2,10},{3,11},{4,12},{5,13},{6,14},{7,15},{8,0},{9,1},... | collective-permute-start | bytes 688136 | tf_op jit(solution)/shard_map/ppermute | solution.py:69
  126.6 2.6 %collective-permute-done.24.refs_2_ = bf16[64,1792]{1,0:T(8,128)(2,1)S(1)} collective-permute-done((bf16[64,1792]{1,0:T(8,128)(2,1)S(1)}, bf16[64,1792]{1,0:T(8,128)(2,1)S(1)}, u32[]{:S(2)}, u32[]{:S(2)}) %collective-permute-start.24) | collective-permute-done | bytes 229408 | tf_op jit(solution)/shard_map/ppermute | solution.py:69
  129.3 2.4 %collective-permute-start.29 = (bf16[32,1792]{1,0:T(8,128)(2,1)S(1)}, bf16[32,1792]{1,0:T(8,128)(2,1)S(1)}, u32[]{:S(2)}, u32[]{:S(2)}) collective-permute-start(bf16[32,1792]{1,0:T(8,128)(2,1)S(1)} %add_convert_fusion.5), channel_id=1, source_target_pairs={{0,16},{1,17},{2,18},{3,19},{4,20},{5,21},{6,22},{7,23},{8,24},{9,... | collective-permute-start | bytes 344072 | tf_op jit(solution)/shard_map/ppermute | solution.py:69
  131.6 1.9 %collective-permute-done.19.refs_8_.refs_1_ = bf16[64,1792]{1,0:T(8,128)(2,1)S(1)} collective-permute-done((bf16[64,1792]{1,0:T(8,128)(2,1)S(1)}, bf16[64,1792]{1,0:T(8,128)(2,1)S(1)}, u32[]{:S(2)}, u32[]{:S(2)}) %collective-permute-start.19) | collective-permute-done | bytes 229408 | tf_op jit(solution)/shard_map/ppermute | solution.py:69
  133.8 2.6 %collective-permute-start.25 = (bf16[32,1792]{1,0:T(8,128)(2,1)S(1)}, bf16[32,1792]{1,0:T(8,128)(2,1)S(1)}, u32[]{:S(2)}, u32[]{:S(2)}) collective-permute-start(bf16[32,1792]{1,0:T(8,128)(2,1)S(1)} %add_convert_fusion.6), channel_id=1, source_target_pairs={{0,16},{1,17},{2,18},{3,19},{4,20},{5,21},{6,22},{7,23},{8,24},{9,... | collective-permute-start | bytes 344072 | tf_op jit(solution)/shard_map/ppermute | solution.py:69
  138.4 2.1 %collective-permute-done.25.refs_3_ = bf16[32,1792]{1,0:T(8,128)(2,1)S(1)} collective-permute-done((bf16[32,1792]{1,0:T(8,128)(2,1)S(1)}, bf16[32,1792]{1,0:T(8,128)(2,1)S(1)}, u32[]{:S(2)}, u32[]{:S(2)}) %collective-permute-start.25) | collective-permute-done | bytes 114720 | tf_op jit(solution)/shard_map/ppermute | solution.py:69
  141.4 2.9 %collective-permute-start.34 = (bf16[32,1792]{1,0:T(8,128)(2,1)S(1)}, bf16[32,1792]{1,0:T(8,128)(2,1)S(1)}, u32[]{:S(2)}, u32[]{:S(2)}) collective-permute-start(bf16[32,1792]{1,0:T(8,128)(2,1)S(1)} %get-tuple-element.55.refs_0_), channel_id=1, source_target_pairs={{0,16},{1,17},{2,18},{3,19},{4,20},{5,21},{6,22},{7,23},{8,24},{9,... | collective-permute-start | bytes 344072 | tf_op jit(solution)/shard_map/ppermute | solution.py:69
  144.9 2.2 %collective-permute-done.34 = bf16[32,1792]{1,0:T(8,128)(2,1)S(1)} collective-permute-done((bf16[32,1792]{1,0:T(8,128)(2,1)S(1)}, bf16[32,1792]{1,0:T(8,128)(2,1)S(1)}, u32[]{:S(2)}, u32[]{:S(2)}) %collective-permute-start.34) | collective-permute-done | bytes 114720 | tf_op jit(solution)/shard_map/ppermute | solution.py:69
  150.4 2.1 %collective-permute-start.41 = (bf16[64,1792]{1,0:T(8,128)(2,1)S(1)}, bf16[64,1792]{1,0:T(8,128)(2,1)S(1)}, u32[]{:S(2)}, u32[]{:S(2)}) collective-permute-start(bf16[64,1792]{1,0:T(8,128)(2,1)S(1)} %collective-permute-done.39.refs_5_), channel_id=1, source_target_pairs={{0,4},{1,5},{2,6},{3,7},{4,0},{5,1},{6,2},{7,3},{8,12},{9,13},{10,... | collective-permute-start | bytes 688136 | tf_op jit(solution)/shard_map/ppermute | solution.py:69
  155.2 2.5 %collective-permute-done.41.refs_7_ = bf16[64,1792]{1,0:T(8,128)(2,1)S(1)} collective-permute-done((bf16[64,1792]{1,0:T(8,128)(2,1)S(1)}, bf16[64,1792]{1,0:T(8,128)(2,1)S(1)}, u32[]{:S(2)}, u32[]{:S(2)}) %collective-permute-start.41) | collective-permute-done | bytes 229408 | tf_op jit(solution)/shard_map/ppermute | solution.py:69
  157.7 4.7 %shard_map.88.refs_9_ = bf16[1024,3584]{1,0:T(8,128)(2,1)} custom-call(s32[2]{0:T(128)S(1)} %pad_add_fusion.index_ref, bf16[64,1792]{1,0:T(8,128)(2,1)S(1)} %constant_dynamic-update-slice_fusion.2.refs_0_, bf16[64,1792]{1,0:T(8,128)(2,1)S(1)} %collective-permute-done.31.refs_8_.refs_1_, bf16[64,1792]{1,0:T(8,128)(2,1)S(1)} %collective-permute-done.32.refs_9_.refs_2_, ...), custom_call_target="tpu_custom_call" | custom-call | flops 1879048192 | bytes 3670016 | tf_op jit(solution)/shard_map/pallas_call | solution.py:293
  162.6 4.7 %shard_map.89 = bf16[1024,3584]{1,0:T(8,128)(2,1)} custom-call(s32[2]{0:T(128)S(1)} %pad_add_fusion.index_ref, bf16[64,1792]{1,0:T(8,128)(2,1)S(1)} %constant_dynamic-update-slice_fusion.refs_0_, bf16[64,1792]{1,0:T(8,128)(2,1)S(1)} %collective-permute-done.19.refs_8_.refs_1_, ...), custom_call_target="tpu_custom_call", output_to_operand_aliasing={{}: (10, {})} | custom-call | flops 1879048192 | bytes 3670016 | tf_op jit(solution)/shard_map/pallas_call | solution.py:293
  (96 shorter events, 39.6 us)
Async XLA Ops:
  3.0 10.2 %collective-permute-start.1 = (bf16[1024,256]{1,0:T(8,128)(2,1)S(1)}, bf16[1024,256]{1,0:T(8,128)(2,1)S(1)}, u32[]{:S(2)}, u32[]{:S(2)}) collective-permute-start(bf16[1024,256]{1,0:T(8,128)(2,1)S(1)} %collective-permute-done.refs_0_), channel_id=1, source_target_pairs={{0,4},{1,5},{2,6},{3,7},{4,0},{5,1},{6,2},{7,3},{8,12},{9,13},{10,... | collective-permute-start | bytes 1572872 | tf_op jit(solution)/shard_map/ppermute | solution.py:69
  6.5 23.5 %collective-permute-start.5 = (bf16[1024,256]{1,0:T(8,128)(2,1)S(1)}, bf16[1024,256]{1,0:T(8,128)(2,1)S(1)}, u32[]{:S(2)}, u32[]{:S(2)}) collective-permute-start(bf16[1024,256]{1,0:T(8,128)(2,1)S(1)} %shard_map.77), channel_id=1, source_target_pairs={{0,0},{10,1},{16,2},{26,3},{4,4},{14,5},{20,6},{30,7},{2,8},{8,9},... | collective-permute-start | bytes 1572872 | tf_op jit(solution)/shard_map/ppermute | solution.py:141
  16.3 15.5 %collective-permute-start.2 = (f32[512,256]{1,0:T(8,128)}, f32[512,256]{1,0:T(8,128)}, u32[]{:S(2)}, u32[]{:S(2)}) collective-permute-start(f32[512,256]{1,0:T(8,128)} %fusion.2), channel_id=1, source_target_pairs={{0,1},{1,0},{2,3},{3,2},{4,5},{5,4},{6,7},{7,6},{8,9},{9,8},{10,11... | collective-permute-start | bytes 1572872 | tf_op jit(solution)/shard_map/ppermute | solution.py:177
  30.0 16.0 %collective-permute-start.6 = (bf16[1024,256]{1,0:T(8,128)(2,1)S(1)}, bf16[1024,256]{1,0:T(8,128)(2,1)S(1)}, u32[]{:S(2)}, u32[]{:S(2)}) collective-permute-start(bf16[1024,256]{1,0:T(8,128)(2,1)S(1)} %collective-permute-done.5), channel_id=1, source_target_pairs={{0,4},{1,5},{2,6},{3,7},{4,0},{5,1},{6,2},{7,3},{8,12},{9,13},{10,... | collective-permute-start | bytes 1572872 | tf_op jit(solution)/shard_map/ppermute | solution.py:69
  34.5 22.8 %collective-permute-start.3 = (f32[512,256]{1,0:T(8,128)S(1)}, f32[512,256]{1,0:T(8,128)S(1)}, u32[]{:S(2)}, u32[]{:S(2)}) collective-permute-start(f32[512,256]{1,0:T(8,128)S(1)} %fusion.8), channel_id=1, source_target_pairs={{0,2},{1,3},{2,0},{3,1},{4,6},{5,7},{6,4},{7,5},{8,10},{9,11},{10,... | collective-permute-start | bytes 1572872 | tf_op jit(solution)/shard_map/ppermute | solution.py:177
  46.7 10.7 %collective-permute-start.7 = (f32[512,256]{1,0:T(8,128)S(1)}, f32[512,256]{1,0:T(8,128)S(1)}, u32[]{:S(2)}, u32[]{:S(2)}) collective-permute-start(f32[512,256]{1,0:T(8,128)S(1)} %fusion), channel_id=1, source_target_pairs={{0,1},{1,0},{2,3},{3,2},{4,5},{5,4},{6,7},{7,6},{8,9},{9,8},{10,11... | collective-permute-start | bytes 1572872 | tf_op jit(solution)/shard_map/ppermute | solution.py:177
  62.9 9.8 %collective-permute-start.15 = (bf16[64,1792]{1,0:T(8,128)(2,1)S(1)}, bf16[64,1792]{1,0:T(8,128)(2,1)S(1)}, u32[]{:S(2)}, u32[]{:S(2)}) collective-permute-start(bf16[64,1792]{1,0:T(8,128)(2,1)S(1)} %get-tuple-element.40), channel_id=1, source_target_pairs={{0,8},{1,9},{2,10},{3,11},{4,12},{5,13},{6,14},{7,15},{8,0},{9,1},... | collective-permute-start | bytes 688136 | tf_op jit(solution)/shard_map/ppermute | solution.py:69
  63.0 14.0 %collective-permute-start.10 = (f32[512,256]{1,0:T(8,128)S(1)}, f32[512,256]{1,0:T(8,128)S(1)}, u32[]{:S(2)}, u32[]{:S(2)}) collective-permute-start(f32[512,256]{1,0:T(8,128)S(1)} %fusion.11.refs_0_), channel_id=1, source_target_pairs={{0,2},{1,3},{2,0},{3,1},{4,6},{5,7},{6,4},{7,5},{8,10},{9,11},{10,... | collective-permute-start | bytes 1572872 | tf_op jit(solution)/shard_map/ppermute | solution.py:177
  64.8 12.4 %collective-permute-start.14 = (bf16[64,1792]{1,0:T(8,128)(2,1)S(1)}, bf16[64,1792]{1,0:T(8,128)(2,1)S(1)}, u32[]{:S(2)}, u32[]{:S(2)}) collective-permute-start(bf16[64,1792]{1,0:T(8,128)(2,1)S(1)} %get-tuple-element.38), channel_id=1, source_target_pairs={{0,8},{1,9},{2,10},{3,11},{4,12},{5,13},{6,14},{7,15},{8,0},{9,1},... | collective-permute-start | bytes 688136 | tf_op jit(solution)/shard_map/ppermute | solution.py:69
  70.6 30.1 %collective-permute-start.8 = (bf16[64,1792]{1,0:T(8,128)(2,1)S(1)}, bf16[64,1792]{1,0:T(8,128)(2,1)S(1)}, u32[]{:S(2)}, u32[]{:S(2)}) collective-permute-start(bf16[64,1792]{1,0:T(8,128)(2,1)S(1)} %get-tuple-element.32), channel_id=1, source_target_pairs={{0,8},{1,9},{2,10},{3,11},{4,12},{5,13},{6,14},{7,15},{8,0},{9,1},... | collective-permute-start | bytes 688136 | tf_op jit(solution)/shard_map/ppermute | solution.py:69
  70.8 19.4 %collective-permute-start.9 = (bf16[64,1792]{1,0:T(8,128)(2,1)S(1)}, bf16[64,1792]{1,0:T(8,128)(2,1)S(1)}, u32[]{:S(2)}, u32[]{:S(2)}) collective-permute-start(bf16[64,1792]{1,0:T(8,128)(2,1)S(1)} %get-tuple-element.34), channel_id=1, source_target_pairs={{0,8},{1,9},{2,10},{3,11},{4,12},{5,13},{6,14},{7,15},{8,0},{9,1},... | collective-permute-start | bytes 688136 | tf_op jit(solution)/shard_map/ppermute | solution.py:69
  79.1 12.3 %collective-permute-start.17 = (bf16[32,1792]{1,0:T(8,128)(2,1)S(1)}, bf16[32,1792]{1,0:T(8,128)(2,1)S(1)}, u32[]{:S(2)}, u32[]{:S(2)}) collective-permute-start(bf16[32,1792]{1,0:T(8,128)(2,1)S(1)} %add_convert_fusion.7), channel_id=1, source_target_pairs={{0,16},{1,17},{2,18},{3,19},{4,20},{5,21},{6,22},{7,23},{8,24},{9,... | collective-permute-start | bytes 344072 | tf_op jit(solution)/shard_map/ppermute | solution.py:69
  84.1 21.0 %collective-permute-start.23 = (bf16[64,1792]{1,0:T(8,128)(2,1)S(1)}, bf16[64,1792]{1,0:T(8,128)(2,1)S(1)}, u32[]{:S(2)}, u32[]{:S(2)}) collective-permute-start(bf16[64,1792]{1,0:T(8,128)(2,1)S(1)} %get-tuple-element.36.refs_1_), channel_id=1, source_target_pairs={{0,4},{1,5},{2,6},{3,7},{4,0},{5,1},{6,2},{7,3},{8,12},{9,13},{10,... | collective-permute-start | bytes 688136 | tf_op jit(solution)/shard_map/ppermute | solution.py:69
  89.3 14.3 %collective-permute-start.27 = (bf16[64,1792]{1,0:T(8,128)(2,1)S(1)}, bf16[64,1792]{1,0:T(8,128)(2,1)S(1)}, u32[]{:S(2)}, u32[]{:S(2)}) collective-permute-start(bf16[64,1792]{1,0:T(8,128)(2,1)S(1)} %get-tuple-element.35.refs_0_), channel_id=1, source_target_pairs={{0,4},{1,5},{2,6},{3,7},{4,0},{5,1},{6,2},{7,3},{8,12},{9,13},{10,... | collective-permute-start | bytes 688136 | tf_op jit(solution)/shard_map/ppermute | solution.py:69
  90.2 11.9 %collective-permute-start.12 = (bf16[64,1792]{1,0:T(8,128)(2,1)S(1)}, bf16[64,1792]{1,0:T(8,128)(2,1)S(1)}, u32[]{:S(2)}, u32[]{:S(2)}) collective-permute-start(bf16[64,1792]{1,0:T(8,128)(2,1)S(1)} %shard_map.81), channel_id=1, source_target_pairs={{0,4},{1,5},{2,6},{3,7},{4,0},{5,1},{6,2},{7,3},{8,12},{9,13},{10,... | collective-permute-start | bytes 688136 | tf_op jit(solution)/shard_map/ppermute | solution.py:69
  92.4 7.6 %collective-permute-start.30 = (bf16[32,1792]{1,0:T(8,128)(2,1)S(1)}, bf16[32,1792]{1,0:T(8,128)(2,1)S(1)}, u32[]{:S(2)}, u32[]{:S(2)}) collective-permute-start(bf16[32,1792]{1,0:T(8,128)(2,1)S(1)} %get-tuple-element.52), channel_id=1, source_target_pairs={{0,16},{1,17},{2,18},{3,19},{4,20},{5,21},{6,22},{7,23},{8,24},{9,... | collective-permute-start | bytes 344072 | tf_op jit(solution)/shard_map/ppermute | solution.py:69
  99.9 25.4 %collective-permute-start.22 = (bf16[64,1792]{1,0:T(8,128)(2,1)S(1)}, bf16[64,1792]{1,0:T(8,128)(2,1)S(1)}, u32[]{:S(2)}, u32[]{:S(2)}) collective-permute-start(bf16[64,1792]{1,0:T(8,128)(2,1)S(1)} %get-tuple-element.45), channel_id=1, source_target_pairs={{0,4},{1,5},{2,6},{3,7},{4,0},{5,1},{6,2},{7,3},{8,12},{9,13},{10,... | collective-permute-start | bytes 688136 | tf_op jit(solution)/shard_map/ppermute | solution.py:69
  100.8 19.9 %collective-permute-start.26 = (bf16[64,1792]{1,0:T(8,128)(2,1)S(1)}, bf16[64,1792]{1,0:T(8,128)(2,1)S(1)}, u32[]{:S(2)}, u32[]{:S(2)}) collective-permute-start(bf16[64,1792]{1,0:T(8,128)(2,1)S(1)} %get-tuple-element.48), channel_id=1, source_target_pairs={{0,4},{1,5},{2,6},{3,7},{4,0},{5,1},{6,2},{7,3},{8,12},{9,13},{10,... | collective-permute-start | bytes 688136 | tf_op jit(solution)/shard_map/ppermute | solution.py:69
  102.1 22.3 %collective-permute-start.31 = (bf16[64,1792]{1,0:T(8,128)(2,1)S(1)}, bf16[64,1792]{1,0:T(8,128)(2,1)S(1)}, u32[]{:S(2)}, u32[]{:S(2)}) collective-permute-start(bf16[64,1792]{1,0:T(8,128)(2,1)S(1)} %constant_dynamic-update-slice_fusion.2.refs_0_), channel_id=1, source_target_pairs={{0,8},{1,9},{2,10},{3,11},{4,12},{5,13},{6,14},{7,15},{8,0},{9,1},... | collective-permute-start | bytes 688136 | tf_op jit(solution)/shard_map/ppermute | solution.py:69
  103.6 8.5 %collective-permute-start.13 = (bf16[32,1792]{1,0:T(8,128)(2,1)S(1)}, bf16[32,1792]{1,0:T(8,128)(2,1)S(1)}, u32[]{:S(2)}, u32[]{:S(2)}) collective-permute-start(bf16[32,1792]{1,0:T(8,128)(2,1)S(1)} %add_convert_fusion.8), channel_id=1, source_target_pairs={{0,16},{1,17},{2,18},{3,19},{4,20},{5,21},{6,22},{7,23},{8,24},{9,... | collective-permute-start | bytes 344072 | tf_op jit(solution)/shard_map/ppermute | solution.py:69
  105.2 20.0 %collective-permute-start.28 = (bf16[64,1792]{1,0:T(8,128)(2,1)S(1)}, bf16[64,1792]{1,0:T(8,128)(2,1)S(1)}, u32[]{:S(2)}, u32[]{:S(2)}) collective-permute-start(bf16[64,1792]{1,0:T(8,128)(2,1)S(1)} %add_convert_fusion.2), channel_id=1, source_target_pairs={{0,8},{1,9},{2,10},{3,11},{4,12},{5,13},{6,14},{7,15},{8,0},{9,1},... | collective-permute-start | bytes 688136 | tf_op jit(solution)/shard_map/ppermute | solution.py:69
  119.8 14.0 %collective-permute-start.32 = (bf16[64,1792]{1,0:T(8,128)(2,1)S(1)}, bf16[64,1792]{1,0:T(8,128)(2,1)S(1)}, u32[]{:S(2)}, u32[]{:S(2)}) collective-permute-start(bf16[64,1792]{1,0:T(8,128)(2,1)S(1)} %constant_dynamic-update-slice_fusion.2.refs_0_), channel_id=1, source_target_pairs={{0,4},{1,5},{2,6},{3,7},{4,0},{5,1},{6,2},{7,3},{8,12},{9,13},{10,... | collective-permute-start | bytes 688136 | tf_op jit(solution)/shard_map/ppermute | solution.py:69
  120.7 8.5 %collective-permute-start.24 = (bf16[64,1792]{1,0:T(8,128)(2,1)S(1)}, bf16[64,1792]{1,0:T(8,128)(2,1)S(1)}, u32[]{:S(2)}, u32[]{:S(2)}) collective-permute-start(bf16[64,1792]{1,0:T(8,128)(2,1)S(1)} %add_convert_fusion.3), channel_id=1, source_target_pairs={{0,8},{1,9},{2,10},{3,11},{4,12},{5,13},{6,14},{7,15},{8,0},{9,1},... | collective-permute-start | bytes 688136 | tf_op jit(solution)/shard_map/ppermute | solution.py:69
  124.4 12.0 %collective-permute-start.33 = (bf16[64,1792]{1,0:T(8,128)(2,1)S(1)}, bf16[64,1792]{1,0:T(8,128)(2,1)S(1)}, u32[]{:S(2)}, u32[]{:S(2)}) collective-permute-start(bf16[64,1792]{1,0:T(8,128)(2,1)S(1)} %collective-permute-done.31.refs_8_.refs_1_), channel_id=1, source_target_pairs={{0,4},{1,5},{2,6},{3,7},{4,0},{5,1},{6,2},{7,3},{8,12},{9,13},{10,... | collective-permute-start | bytes 688136 | tf_op jit(solution)/shard_map/ppermute | solution.py:69
  125.2 8.4 %collective-permute-start.19 = (bf16[64,1792]{1,0:T(8,128)(2,1)S(1)}, bf16[64,1792]{1,0:T(8,128)(2,1)S(1)}, u32[]{:S(2)}, u32[]{:S(2)}) collective-permute-start(bf16[64,1792]{1,0:T(8,128)(2,1)S(1)} %constant_dynamic-update-slice_fusion.refs_0_), channel_id=1, source_target_pairs={{0,8},{1,9},{2,10},{3,11},{4,12},{5,13},{6,14},{7,15},{8,0},{9,1},... | collective-permute-start | bytes 688136 | tf_op jit(solution)/shard_map/ppermute | solution.py:69
  125.3 15.2 %collective-permute-start.20 = (bf16[64,1792]{1,0:T(8,128)(2,1)S(1)}, bf16[64,1792]{1,0:T(8,128)(2,1)S(1)}, u32[]{:S(2)}, u32[]{:S(2)}) collective-permute-start(bf16[64,1792]{1,0:T(8,128)(2,1)S(1)} %constant_dynamic-update-slice_fusion.refs_0_), channel_id=1, source_target_pairs={{0,4},{1,5},{2,6},{3,7},{4,0},{5,1},{6,2},{7,3},{8,12},{9,13},{10,... | collective-permute-start | bytes 688136 | tf_op jit(solution)/shard_map/ppermute | solution.py:69
  129.3 7.1 %collective-permute-start.29 = (bf16[32,1792]{1,0:T(8,128)(2,1)S(1)}, bf16[32,1792]{1,0:T(8,128)(2,1)S(1)}, u32[]{:S(2)}, u32[]{:S(2)}) collective-permute-start(bf16[32,1792]{1,0:T(8,128)(2,1)S(1)} %add_convert_fusion.5), channel_id=1, source_target_pairs={{0,16},{1,17},{2,18},{3,19},{4,20},{5,21},{6,22},{7,23},{8,24},{9,... | collective-permute-start | bytes 344072 | tf_op jit(solution)/shard_map/ppermute | solution.py:69
  133.5 7.0 %collective-permute-start.21 = (bf16[64,1792]{1,0:T(8,128)(2,1)S(1)}, bf16[64,1792]{1,0:T(8,128)(2,1)S(1)}, u32[]{:S(2)}, u32[]{:S(2)}) collective-permute-start(bf16[64,1792]{1,0:T(8,128)(2,1)S(1)} %collective-permute-done.19.refs_8_.refs_1_), channel_id=1, source_target_pairs={{0,4},{1,5},{2,6},{3,7},{4,0},{5,1},{6,2},{7,3},{8,12},{9,13},{10,... | collective-permute-start | bytes 688136 | tf_op jit(solution)/shard_map/ppermute | solution.py:69
  137.3 7.0 %collective-permute-start.38 = (bf16[32,1792]{1,0:T(8,128)(2,1)S(1)}, bf16[32,1792]{1,0:T(8,128)(2,1)S(1)}, u32[]{:S(2)}, u32[]{:S(2)}) collective-permute-start(bf16[32,1792]{1,0:T(8,128)(2,1)S(1)} %get-tuple-element.56.one_ref), channel_id=1, source_target_pairs={{0,16},{1,17},{2,18},{3,19},{4,20},{5,21},{6,22},{7,23},{8,24},{9,... | collective-permute-start | bytes 344072 | tf_op jit(solution)/shard_map/ppermute | solution.py:69
  150.4 7.3 %collective-permute-start.41 = (bf16[64,1792]{1,0:T(8,128)(2,1)S(1)}, bf16[64,1792]{1,0:T(8,128)(2,1)S(1)}, u32[]{:S(2)}, u32[]{:S(2)}) collective-permute-start(bf16[64,1792]{1,0:T(8,128)(2,1)S(1)} %collective-permute-done.39.refs_5_), channel_id=1, source_target_pairs={{0,4},{1,5},{2,6},{3,7},{4,0},{5,1},{6,2},{7,3},{8,12},{9,13},{10,... | collective-permute-start | bytes 688136 | tf_op jit(solution)/shard_map/ppermute | solution.py:69
  152.5 9.8 %collective-permute-start.36 = (bf16[64,1792]{1,0:T(8,128)(2,1)S(1)}, bf16[64,1792]{1,0:T(8,128)(2,1)S(1)}, u32[]{:S(2)}, u32[]{:S(2)}) collective-permute-start(bf16[64,1792]{1,0:T(8,128)(2,1)S(1)} %constant_dynamic-update-slice_fusion.4.refs_4_), channel_id=1, source_target_pairs={{0,4},{1,5},{2,6},{3,7},{4,0},{5,1},{6,2},{7,3},{8,12},{9,13},{10,... | collective-permute-start | bytes 688136 | tf_op jit(solution)/shard_map/ppermute | solution.py:69
  153.3 9.3 %collective-permute-start.37 = (bf16[64,1792]{1,0:T(8,128)(2,1)S(1)}, bf16[64,1792]{1,0:T(8,128)(2,1)S(1)}, u32[]{:S(2)}, u32[]{:S(2)}) collective-permute-start(bf16[64,1792]{1,0:T(8,128)(2,1)S(1)} %collective-permute-done.35.refs_5_), channel_id=1, source_target_pairs={{0,4},{1,5},{2,6},{3,7},{4,0},{5,1},{6,2},{7,3},{8,12},{9,13},{10,... | collective-permute-start | bytes 688136 | tf_op jit(solution)/shard_map/ppermute | solution.py:69
  (15 other events, 84.2 us)
